TPU v7x, 32 devices: a whole 2x2x4 slice. The times are simulated.
32 devices in a mesh: gx: 8 (over z, y), gy: 4 (over x, core).
Axes of the slice: x: 2, y: 2, z: 4, core: 2. Of those that a mesh axis runs over, the one named last changes fastest.
Arguments:
- tracers: float32 [4, 8, 512, 1024], P(None, None, 'gy', 'gx'), may hold values from -6 to 6
- velocity: float32 [2, 8, 512, 1024], P(None, None, 'gy', 'gx'), may hold values from -0.35 to 0.35
- mixing: float32 [8, 512, 1024], P(None, 'gy', 'gx'), may hold values from 0.01 to 0.075
- land_mask: int32 [512, 1024], P('gy', 'gx'), may hold values 0 or 1
- remap_weights: bfloat16 [512, 4, 1024, 128], P('gy', None, 'gx'), may hold values from 0 to 0.015625
- remap_dest: int32 [512, 8, 4], P('gy', 'gx'), may hold values from 0 to 511, as said below
Outputs:
- final_tracers: float32 [4, 8, 512, 1024], P(None, None, 'gy', 'gx')
- atmo_fields: float32 [512, 5, 128], P(('gx', 'gy'))
Inputs may be any that keep to these rules, and one draw needn't show every extreme that they name: `remap_dest`: block b belongs to owner b // 16; owner o is the device with gx index o // 4 and gy index o % 4 (the order of the output's split over (gx, gy)). Among the 512 entries of one tile (one index of gy and of gx) no owner is named more than 32 times; 4 owners are named exactly 32 times by every tile.
All inputs are finite; a program needn't handle non-finite values. No bound on the sum of `land_mask` on one device may be relied on, other than what follows from the above.
Results may differ from a plain program's by a relative error of at most 0.0003.
Values sent between devices are 32-bit elements; how exact they have to be, the bound alone decides.
No kernel may reach another device: no remote copies, remote signals or barrier semaphores. Data moves between devices by JAX's collectives and lax.ppermute only.
A program may use at most 128 MiB of HBM per device.

v0:
```python
import functools

import jax
import jax.numpy as jnp
from jax import lax
from jax.experimental import pallas as pl
from jax.experimental.pallas import tpu as pltpu
from jax.sharding import PartitionSpec as P

STEPS = 4
ABD = 16
NTR = 4
FIELDS = 8
OFF = 16
GROUP = 48
AXES = ("gx", "gy")


def lane_ids(rows):
    return lax.broadcasted_iota(jnp.int32, (rows, 128), 1)


def sub_ids(rows):
    return lax.broadcasted_iota(jnp.int32, (rows, 128), 0)


def lat_pack_kernel(has_ocean, *refs):
    if has_ocean:
        tl, vl, ml, ol, th, vh, mh, oh, south_ref, north_ref = refs
    else:
        tl, vl, ml, th, vh, mh, south_ref, north_ref = refs
        ol = oh = None
    top = sub_ids(8) < 4

    def fields(t, v, m, o):
        out = [t[i, 0] for i in range(NTR)] + [v[0, 0], v[1, 0], m[0]]
        out.append(m[0] if o is None else o[...].astype(jnp.float32))
        return out

    low, high = fields(tl, vl, ml, ol), fields(th, vh, mh, oh)
    for p in range(FIELDS // 2):
        a, b = low[2 * p], low[2 * p + 1]
        south_ref[0, 8 * p : 8 * p + 8] = jnp.where(top, a, pltpu.roll(b, 4, 0))
        a, b = high[2 * p], high[2 * p + 1]
        north_ref[0, 8 * p : 8 * p + 8] = jnp.where(top, pltpu.roll(a, 4, 0), b)


def lat_pack(tracers, velocity, mixing, ocean, first, levels):
    rows = tracers.shape[2]
    last = rows // 8 - 1
    has_ocean = ocean is not None

    def specs(block):
        out = [
            pl.BlockSpec((NTR, 1, 8, 128), lambda l: (0, l + first, block, 0)),
            pl.BlockSpec((2, 1, 8, 128), lambda l: (0, l + first, block, 0)),
            pl.BlockSpec((1, 8, 128), lambda l: (l + first, block, 0)),
        ]
        if has_ocean:
            out.append(pl.BlockSpec((8, 128), lambda l: (block, 0)))
        return out

    arrays = [tracers, velocity, mixing] + ([ocean] if has_ocean else [])
    strip = jax.ShapeDtypeStruct((levels, 32, 128), jnp.float32)
    return pl.pallas_call(
        functools.partial(lat_pack_kernel, has_ocean),
        grid=(levels,),
        in_specs=specs(0) + specs(last),
        out_specs=[pl.BlockSpec((1, 32, 128), lambda l: (l, 0, 0))] * 2,
        out_shape=[strip, strip],
        name="lat_pack",
    )(*arrays, *arrays)


def lat_halo_blocks(from_south, from_north, f):
    p, odd = f // 2, f % 2
    s = from_south[0, 8 * p : 8 * p + 8]
    n = from_north[0, 8 * p : 8 * p + 8]
    if odd:
        return s, pltpu.roll(n, 4, 0)
    return pltpu.roll(s, 4, 0), n


def interior(t, v, m, o, f):
    if f < NTR:
        return t[f, 0]
    if f < NTR + 2:
        return v[f - NTR, 0]
    if f == NTR + 2:
        return m[0]
    return o[...].astype(jnp.float32)


def lon_pack_kernel(has_ocean, *refs):
    if has_ocean:
        t, v, m, o, fs, fn, west_ref, east_ref = refs
    else:
        t, v, m, fs, fn, west_ref, east_ref = refs
        o = None
    rows = t.shape[2]
    lane = lane_ids(GROUP)
    groups = (rows + 16) // GROUP
    west = jnp.zeros((GROUP, 128), jnp.float32)
    east = jnp.zeros((GROUP, 128), jnp.float32)
    for f in range(FIELDS if has_ocean else FIELDS - 1):
        s, n = lat_halo_blocks(fs, fn, f)
        whole = jnp.concatenate([s, interior(t, v, m, o, f), n], axis=0)
        for g in range(groups):
            at = 32 * g + 4 * f
            moved = pltpu.roll(whole[GROUP * g : GROUP * g + GROUP], (at - 124) % 128, 1)
            east = jnp.where((lane >= at) & (lane < at + 4), moved, east)
            west = jnp.where((lane >= at + 4) & (lane < at + 8), moved, west)
    west_ref[0] = west
    east_ref[0] = east


def lon_pack(tracers, velocity, mixing, ocean, from_south, from_north, first, levels):
    rows = tracers.shape[2]
    has_ocean = ocean is not None
    strip = jax.ShapeDtypeStruct((levels, GROUP, 128), jnp.float32)
    specs = tile_specs(rows, lambda l: l + first, has_ocean)
    arrays = [tracers, velocity, mixing] + ([ocean] if has_ocean else [])
    return pl.pallas_call(
        functools.partial(lon_pack_kernel, has_ocean),
        grid=(levels,),
        in_specs=specs + [pl.BlockSpec((1, 32, 128), lambda l: (l, 0, 0))] * 2,
        out_specs=[pl.BlockSpec((1, GROUP, 128), lambda l: (l, 0, 0))] * 2,
        out_shape=[strip, strip],
        name="lon_pack",
    )(*arrays, from_south, from_north)


def tile_specs(rows, level, has_ocean):
    out = [
        pl.BlockSpec((NTR, 1, rows, 128), lambda l: (0, level(l), 0, 0)),
        pl.BlockSpec((2, 1, rows, 128), lambda l: (0, level(l), 0, 0)),
        pl.BlockSpec((1, rows, 128), lambda l: (level(l), 0, 0)),
    ]
    if has_ocean:
        out.append(pl.BlockSpec((rows, 128), lambda l: (0, 0)))
    return out


def unpack_field(ext, f, t, v, m, o, fs, fn, even, odd):
    rows = t.shape[2]
    s, n = lat_halo_blocks(fs, fn, f)
    ext[0, OFF - 8 : OFF] = s
    ext[0, OFF : OFF + rows] = interior(t, v, m, o, f)
    ext[0, OFF + rows : OFF + rows + 8] = n
    strip = odd if f % 2 else even
    for g in range((rows + 16) // GROUP):
        base = OFF - 8 + GROUP * g
        ext[1, base : base + GROUP] = pltpu.roll(strip, (124 - (32 * g + 4 * f)) % 128, 1)


def strips(fw, fe):
    near = lane_ids(GROUP) % 8 < 4
    w, e = fw[0], fe[0]
    return jnp.where(near, w, e), jnp.where(near, e, w)


def to_right(a, b):
    end = lane_ids(a.shape[0]) == 127
    ra, rb = pltpu.roll(a, 127, 1), pltpu.roll(b, 127, 1)
    return jnp.where(end, rb, ra), jnp.where(end, ra, rb)


def to_left(a, b):
    start = lane_ids(a.shape[0]) == 0
    ra, rb = pltpu.roll(a, 1, 1), pltpu.roll(b, 1, 1)
    return jnp.where(start, rb, ra), jnp.where(start, ra, rb)


CHUNK = 24


def chunks(rows):
    return range(OFF - 8, OFF + rows + 8, CHUNK)


def coefficients(rows, u, v, k, oc, coef, north_a, north_b):
    for r in chunks(rows):
        here, above = slice(r, r + CHUNK), slice(r + 1, r + CHUNK + 1)
        for h in range(2):
            vel = 0.5 * (v[h, here] + v[h, above])
            mix = 0.5 * (k[h, here] + k[h, above])
            face = oc[h, here] * oc[h, above]
            north_a[h, here] = face * (jnp.maximum(vel, 0.0) + mix)
            north_b[h, here] = face * (jnp.minimum(vel, 0.0) - mix)
    for r in chunks(rows):
        here, below = slice(r, r + CHUNK), slice(r - 1, r + CHUNK - 1)
        us, ks, os = ((x[0, here], x[1, here]) for x in (u, k, oc))
        ur, kr, orr = to_right(*us), to_right(*ks), to_right(*os)
        east_a, east_b = [], []
        for h in range(2):
            vel = 0.5 * (us[h] + ur[h])
            mix = 0.5 * (ks[h] + kr[h])
            face = os[h] * orr[h]
            east_a.append(face * (jnp.maximum(vel, 0.0) + mix))
            east_b.append(face * (jnp.minimum(vel, 0.0) - mix))
        west_a, west_b = to_left(*east_a), to_left(*east_b)
        for h in range(2):
            coef[0, h, here] = (
                1.0 - (east_a[h] - west_b[h]) - (north_a[h, here] - north_b[h, below])
            )
            coef[1, h, here] = -east_b[h]
            coef[2, h, here] = west_a[h]
            coef[3, h, here] = -north_b[h, here]
            coef[4, h, here] = north_a[h, below]


def advance(rows, coef, q):
    for step in range(STEPS):
        src, dst = step % 2, (step + 1) % 2
        for r in chunks(rows):
            here = slice(r, r + CHUNK)
            c = [[coef[i, h, here] for h in range(2)] for i in range(5)]
            for i in range(NTR):
                mid = [q[src, i, h, here] for h in range(2)]
                right, left = to_right(*mid), to_left(*mid)
                for h in range(2):
                    up = q[src, i, h, r + 1 : r + CHUNK + 1]
                    down = q[src, i, h, r - 1 : r + CHUNK - 1]
                    q[dst, i, h, here] = (
                        c[0][h] * mid[h]
                        + c[1][h] * right[h]
                        + c[2][h] * left[h]
                        + c[3][h] * up
                        + c[4][h] * down
                    )


def field_scratch(rows):
    ext = (2, rows + 32, 128)
    return [
        pltpu.VMEM((4,) + ext, jnp.float32),
        pltpu.VMEM((2,) + ext, jnp.float32),
        pltpu.VMEM((5,) + ext, jnp.float32),
        pltpu.VMEM((2, NTR) + ext, jnp.float32),
    ]


def run_level(rows, t, v, m, o, fs, fn, fw, fe, vel, north, coef, q):
    even, odd = strips(fw, fe)
    for i in range(NTR):
        unpack_field(q.at[0, i], i, t, v, m, o, fs, fn, even, odd)
    for i in range(3):
        unpack_field(vel.at[i], NTR + i, t, v, m, o, fs, fn, even, odd)
    coefficients(
        rows, vel.at[0], vel.at[1], vel.at[2], vel.at[3], coef, north.at[0], north.at[1]
    )
    advance(rows, coef, q)


def surface_kernel(
    order, accs, slot, t, v, m, o, fs, fn, fw, fe, w, out_q, out_send, out_keep,
    vel, north, coef, q, surf, *sums,
):
    rows = t.shape[2]
    even, odd = strips(fw, fe)
    unpack_field(vel.at[3], FIELDS - 1, t, v, m, o, fs, fn, even, odd)
    run_level(rows, t, v, m, o, fs, fn, fw, fe, vel, north, coef, q)
    ocean = o[...].astype(jnp.float32)
    for i in range(NTR):
        done = q[0, i, 0, OFF : OFF + rows]
        out_q[i] = done
        surf[pl.ds(i, rows, stride=8), :] = done * ocean
    surf[pl.ds(NTR, rows, stride=8), :] = ocean
    for i in range(NTR + 1, 8):
        surf[pl.ds(i, rows, stride=8), :] = jnp.zeros((rows, 128), jnp.float32)
    for d in sums:
        d[...] = jnp.zeros_like(d)
    first = sub_ids(16) < 8
    kb = w.shape[1]

    def body(i, carry):
        s = surf[pl.ds(pl.multiple_of(16 * i, 16), 16), :]
        lhs = jnp.concatenate(
            [jnp.where(first, s, 0.0), jnp.where(first, 0.0, s)], axis=1
        ).astype(jnp.bfloat16)
        for k in range(0, kb, 2):
            rhs = jnp.concatenate(
                [
                    jnp.concatenate([w[2 * i + r, k], w[2 * i + r, k + 1]], axis=1)
                    for r in range(2)
                ],
                axis=0,
            )
            part = jnp.dot(lhs, rhs, preferred_element_type=jnp.float32)
            for r in range(2):
                for kk in range(2):
                    d = sums[(k + kk) % accs]
                    at = pl.ds(
                        pl.multiple_of(8 * slot[(2 * i + r) * kb + k + kk], 8), 8
                    )
                    d[at, :] += part[8 * r : 8 * r + 8, 128 * kk : 128 * kk + 128]
        return carry

    lax.fori_loop(0, rows // 2, body, 0, unroll=2)
    chunk = ABD * (NTR + 1)
    half = len(order) // 2
    for place, owner in enumerate(order):
        ref, base = (out_keep, place) if place < half else (out_send, place - half)
        for f in range(NTR + 1):
            total = sums[0][pl.ds(owner * ABD * 8 + f, ABD, stride=8), :]
            for d in sums[1:]:
                total = total + d[pl.ds(owner * ABD * 8 + f, ABD, stride=8), :]
            at = base * chunk + f * ABD
            ref[at : at + ABD, :] = total


def surface(order, slot, tracers, velocity, mixing, ocean, halo, weights):
    rows = tracers.shape[2]
    owners = len(order)
    accs = 4 if owners <= 32 else 1
    strip = [pl.BlockSpec((1, 32, 128), lambda l, s: (0, 0, 0))] * 2
    strip += [pl.BlockSpec((1, GROUP, 128), lambda l, s: (0, 0, 0))] * 2
    tiles = [
        pl.BlockSpec((NTR, 1, rows, 128), lambda l, s: (0, 0, 0, 0)),
        pl.BlockSpec((2, 1, rows, 128), lambda l, s: (0, 0, 0, 0)),
        pl.BlockSpec((1, rows, 128), lambda l, s: (0, 0, 0)),
        pl.BlockSpec((rows, 128), lambda l, s: (0, 0)),
    ]
    half = owners // 2 * ABD * (NTR + 1)
    return pl.pallas_call(
        functools.partial(surface_kernel, order, accs),
        grid_spec=pltpu.PrefetchScalarGridSpec(
            num_scalar_prefetch=1,
            grid=(1,),
            in_specs=tiles + strip + [pl.BlockSpec(memory_space=pltpu.VMEM)],
            out_specs=[
                pl.BlockSpec((NTR, rows, 128), lambda l, s: (0, 0, 0)),
                pl.BlockSpec(memory_space=pltpu.VMEM),
                pl.BlockSpec(memory_space=pltpu.VMEM),
            ],
            scratch_shapes=field_scratch(rows)
            + [pltpu.VMEM((rows * 8, 128), jnp.float32)]
            + [pltpu.VMEM((owners * ABD * 8, 128), jnp.float32)] * accs,
        ),
        out_shape=[
            jax.ShapeDtypeStruct((NTR, rows, 128), jnp.float32),
            jax.ShapeDtypeStruct((half, 128), jnp.float32),
            jax.ShapeDtypeStruct((half, 128), jnp.float32),
        ],
        compiler_params=pltpu.CompilerParams(vmem_limit_bytes=48 << 20),
        name="surface",
    )(slot, tracers, velocity, mixing, ocean, *halo, weights)


def deep_kernel(t, v, m, o, fs, fn, fw, fe, ofs, ofn, ofw, ofe, done, out, vel, north, coef, q):
    rows = t.shape[2]
    level = pl.program_id(0)

    @pl.when(level == 0)
    def _():
        out[:, 0] = done[...]
        even, odd = strips(ofw, ofe)
        unpack_field(vel.at[3], FIELDS - 1, t, v, m, o, ofs, ofn, even, odd)

    @pl.when(level > 0)
    def _():
        run_level(rows, t, v, m, o, fs, fn, fw, fe, vel, north, coef, q)
        for i in range(NTR):
            out[i, 0] = q[0, i, 0, OFF : OFF + rows]


def deep(tracers, velocity, mixing, ocean, halo, ocean_halo, done):
    rows, levels = tracers.shape[2], tracers.shape[1]
    specs = tile_specs(rows, lambda l: jnp.maximum(l, 1), True)
    strip = [pl.BlockSpec((1, 32, 128), lambda l: (jnp.maximum(l - 1, 0), 0, 0))] * 2
    strip += [pl.BlockSpec((1, GROUP, 128), lambda l: (jnp.maximum(l - 1, 0), 0, 0))] * 2
    fixed = [pl.BlockSpec((1, 32, 128), lambda l: (0, 0, 0))] * 2
    fixed += [pl.BlockSpec((1, GROUP, 128), lambda l: (0, 0, 0))] * 2
    return pl.pallas_call(
        deep_kernel,
        grid=(levels,),
        in_specs=specs + strip + fixed
        + [pl.BlockSpec((NTR, rows, 128), lambda l: (0, 0, 0))],
        out_specs=pl.BlockSpec((NTR, 1, rows, 128), lambda l: (0, l, 0, 0)),
        out_shape=jax.ShapeDtypeStruct(tracers.shape, jnp.float32),
        scratch_shapes=field_scratch(rows),
        compiler_params=pltpu.CompilerParams(vmem_limit_bytes=24 << 20),
        name="deep",
    )(tracers, velocity, mixing, ocean, *halo, *ocean_halo, done)


def exchange_lat(to_south, to_north):
    n = lax.axis_size("gy")
    from_south = lax.ppermute(to_north, "gy", [(i, i + 1) for i in range(n - 1)])
    from_north = lax.ppermute(to_south, "gy", [(i + 1, i) for i in range(n - 1)])
    return from_south, from_north


def exchange_lon(to_west, to_east):
    n = lax.axis_size("gx")
    from_west = lax.ppermute(to_east, "gx", [(i, (i + 1) % n) for i in range(n)])
    from_east = lax.ppermute(to_west, "gx", [((i + 1) % n, i) for i in range(n)])
    return from_west, from_east


def partner(a, mask, n):
    return lax.ppermute(a, AXES, [(i, i ^ mask) for i in range(n)])


def rounds_of(owners):
    bits = owners.bit_length() - 1
    out, at = [(0, 1)], 1
    while at < bits:
        width = min(2, bits - at)
        out.append((at, width))
        at += width
    return out


def order_of(owners):
    def key(owner):
        return tuple((owner >> at) & ((1 << width) - 1) for at, width in rounds_of(owners))
    return sorted(range(owners), key=key)


def per_device(tracers, velocity, mixing, land_mask, remap_weights, remap_dest):
    owners = lax.axis_size("gx") * lax.axis_size("gy")
    levels = tracers.shape[1]
    me = lax.axis_index("gx") * lax.axis_size("gy") + lax.axis_index("gy")
    dest = remap_dest.reshape(-1)
    slot = jnp.bitwise_xor(dest // ABD, me) * ABD + dest % ABD

    lat0 = exchange_lat(*lat_pack(tracers, velocity, mixing, land_mask, 0, 1))
    lon0 = exchange_lon(*lon_pack(tracers, velocity, mixing, land_mask, *lat0, 0, 1))
    halo0 = lat0 + lon0
    lat1 = exchange_lat(*lat_pack(tracers, velocity, mixing, None, 1, levels - 1))
    lon1 = exchange_lon(*lon_pack(tracers, velocity, mixing, None, *lat1, 1, levels - 1))
    halo1 = lat1 + lon1

    order = order_of(owners)
    done, send, keep = surface(
        order, slot, tracers, velocity, mixing, land_mask, halo0, remap_weights
    )
    values = deep(tracers, velocity, mixing, land_mask, halo1, halo0, done)

    total = keep + partner(send, 1, owners)
    for at, width in rounds_of(owners)[1:]:
        parts = total.reshape((1 << width, -1, 128))
        got = [partner(parts[i], i << at, owners) for i in range(1, 1 << width)]
        total = parts[0]
        for g in got:
            total = total + g
    atmo = total.reshape(NTR + 1, ABD, 128).transpose(1, 0, 2)
    return values, atmo


def solution(mesh):
    placed = (
        P(None, None, "gy", "gx"),
        P(None, None, "gy", "gx"),
        P(None, "gy", "gx"),
        P("gy", "gx"),
        P("gy", None, "gx", None),
        P("gy", "gx", None),
    )
    return jax.shard_map(
        per_device,
        mesh=mesh,
        in_specs=placed,
        out_specs=(P(None, None, "gy", "gx"), P(("gx", "gy"), None, None)),
        check_vma=False,
    )
```

profile of v0, /device:TPU:1, one launch (start us, length us, event | category | flops | bytes accessed | tf_op | source)
XLA Modules:
  0.0 94.8 jit_solution(2502576347176649600)
XLA Ops:
  0.6 1.4 %lat_pack.3 = (f32[1,32,128]{2,1,0:T(8,128)}, f32[1,32,128]{2,1,0:T(8,128)}) custom-call(f32[4,8,128,128]{3,2,1,0:T(8,128)} %t.3, f32[2,8,128,128]{3,2,1,0:T(8,128)} %v.3, f32[8,128,128]{2,1,0:T(8,128)} %m.3, s32[128,128]{1,0:T(8,128)} %o.3, f32[4,8,128,128]{3,2,1,0:T(8,128)} %t.3, f32[2,8,128,128]{3,2,1,0:T(8,128)} %v.3, f32[8,128,128]{2,1,0:T(8,128)} %m.3, ...), custom_call_target="tpu_custom_call" | custom-call | tf_op jit(solution)/shard_map/lat_pack/pallas_call | solution.py:65
  2.1 4.8 %collective-permute-start.4 = (f32[1,32,128]{2,1,0:T(8,128)}, f32[1,32,128]{2,1,0:T(8,128)S(1)}, u32[]{:S(2)}, u32[]{:S(2)}) collective-permute-start(f32[1,32,128]{2,1,0:T(8,128)} %get-tuple-element.17), channel_id=1, source_target_pairs={{0,1},{1,2},{2,3},{4,5},{5,6},{6,7},{8,9},{9,10},{10,11},{12,13},{... | collective-permute-start | bytes 49160 | tf_op jit(solution)/shard_map/ppermute | solution.py:389
  6.9 1.9 %collective-permute-start.5 = (f32[1,32,128]{2,1,0:T(8,128)}, f32[1,32,128]{2,1,0:T(8,128)S(1)}, u32[]{:S(2)}, u32[]{:S(2)}) collective-permute-start(f32[1,32,128]{2,1,0:T(8,128)} %get-tuple-element.18), channel_id=1, source_target_pairs={{1,0},{2,1},{3,2},{5,4},{6,5},{7,6},{9,8},{10,9},{11,10},{13,12},{... | collective-permute-start | bytes 49160 | tf_op jit(solution)/shard_map/ppermute | solution.py:390
  9.1 3.1 %collective-permute-done.5.refs_5_.fn.ofn = f32[1,32,128]{2,1,0:T(8,128)S(1)} collective-permute-done((f32[1,32,128]{2,1,0:T(8,128)}, f32[1,32,128]{2,1,0:T(8,128)S(1)}, u32[]{:S(2)}, u32[]{:S(2)}) %collective-permute-start.5) | collective-permute-done | bytes 16416 | tf_op jit(solution)/shard_map/ppermute | solution.py:390
  12.7 1.9 %lon_pack.3 = (f32[1,48,128]{2,1,0:T(8,128)}, f32[1,48,128]{2,1,0:T(8,128)}) custom-call(f32[4,8,128,128]{3,2,1,0:T(8,128)} %t.3, f32[2,8,128,128]{3,2,1,0:T(8,128)} %v.3, f32[8,128,128]{2,1,0:T(8,128)} %m.3, s32[128,128]{1,0:T(8,128)} %o.3, f32[1,32,128]{2,1,0:T(8,128)} %copy-done.13, f32[1,32,128]{2,1,0:T(8,128)} %copy-done.16), custom_call_target="tpu_custom_call" | custom-call | tf_op jit(solution)/shard_map/lon_pack/pallas_call | solution.py:123
  14.6 1.2 %collective-permute-start.6 = (f32[1,48,128]{2,1,0:T(8,128)}, f32[1,48,128]{2,1,0:T(8,128)S(1)}, u32[]{:S(2)}, u32[]{:S(2)}) collective-permute-start(f32[1,48,128]{2,1,0:T(8,128)} %get-tuple-element.19), channel_id=1, source_target_pairs={{0,4},{4,8},{8,12},{12,16},{16,20},{20,24},{24,28},{28,0},{1,5},{5... | collective-permute-start | bytes 73736 | tf_op jit(solution)/shard_map/ppermute | solution.py:396
  15.8 3.0 %collective-permute-start.7 = (f32[1,48,128]{2,1,0:T(8,128)}, f32[1,48,128]{2,1,0:T(8,128)S(1)}, u32[]{:S(2)}, u32[]{:S(2)}) collective-permute-start(f32[1,48,128]{2,1,0:T(8,128)} %get-tuple-element.20), channel_id=1, source_target_pairs={{4,0},{8,4},{12,8},{16,12},{20,16},{24,20},{28,24},{0,28},{5,1},{9... | collective-permute-start | bytes 73736 | tf_op jit(solution)/shard_map/ppermute | solution.py:397
  18.9 1.4 %collective-permute-done.6.fw.ofw = f32[1,48,128]{2,1,0:T(8,128)S(1)} collective-permute-done((f32[1,48,128]{2,1,0:T(8,128)}, f32[1,48,128]{2,1,0:T(8,128)S(1)}, u32[]{:S(2)}, u32[]{:S(2)}) %collective-permute-start.6) | collective-permute-done | bytes 24608 | tf_op jit(solution)/shard_map/ppermute | solution.py:396
  20.3 1.0 %copy-done.4 = f32[8,128,128]{2,1,0:T(8,128)S(1)} copy-done((f32[8,128,128]{2,1,0:T(8,128)S(1)}, f32[8,128,128]{2,1,0:T(8,128)}, u32[]{:S(2)}) %copy-start.4) | copy-done | bytes 524312
  22.8 15.8 %surface.1 = (f32[4,128,128]{2,1,0:T(8,128)S(1)}, f32[1280,128]{1,0:T(8,128)S(1)}, f32[1280,128]{1,0:T(8,128)S(1)}) custom-call(s32[512]{0:T(512)S(1)} %fusion.6.slot, f32[4,8,128,128]{3,2,1,0:T(8,128)S(1)} %copy-done, f32[2,8,128,128]{3,2,1,0:T(8,128)S(1)} %copy-done.2, f32[8,128,128]{2,1,0:T(8,128)S(1)} %copy-done.4, s32[128,128]{1,0:T(8,128)S(1)} %copy-done.6, ...), custom_call_target="tpu_custom_call" | custom-call | tf_op jit(solution)/shard_map/surface/pallas_call | solution.py:325
  38.7 2.1 %collective-permute-done.8 = f32[1280,128]{1,0:T(8,128)S(1)} collective-permute-done((f32[1280,128]{1,0:T(8,128)S(1)}, f32[1280,128]{1,0:T(8,128)S(1)}, u32[]{:S(2)}, u32[]{:S(2)}) %collective-permute-start.8) | collective-permute-done | bytes 655392 | tf_op jit(solution)/shard_map/ppermute | solution.py:402
  42.7 0.9 collective-permute-start.11
  44.5 4.2 %lat_pack.2 = (f32[7,32,128]{2,1,0:T(8,128)}, f32[7,32,128]{2,1,0:T(8,128)}) custom-call(f32[4,8,128,128]{3,2,1,0:T(8,128)} %t.3, f32[2,8,128,128]{3,2,1,0:T(8,128)} %v.3, f32[8,128,128]{2,1,0:T(8,128)} %m.3, f32[4,8,128,128]{3,2,1,0:T(8,128)} %t.3, f32[2,8,128,128]{3,2,1,0:T(8,128)} %v.3, f32[8,128,128]{2,1,0:T(8,128)} %m.3), custom_call_target="tpu_custom_call" | custom-call | tf_op jit(solution)/shard_map/lat_pack/pallas_call | solution.py:65
  48.7 3.8 %collective-permute-start = (f32[7,32,128]{2,1,0:T(8,128)}, f32[7,32,128]{2,1,0:T(8,128)S(1)}, u32[]{:S(2)}, u32[]{:S(2)}) collective-permute-start(f32[7,32,128]{2,1,0:T(8,128)} %get-tuple-element.13), channel_id=1, source_target_pairs={{0,1},{1,2},{2,3},{4,5},{5,6},{6,7},{8,9},{9,10},{10,11},{12,13},{... | collective-permute-start | bytes 344072 | tf_op jit(solution)/shard_map/ppermute | solution.py:389
  52.6 2.2 %collective-permute-start.1 = (f32[7,32,128]{2,1,0:T(8,128)}, f32[7,32,128]{2,1,0:T(8,128)S(1)}, u32[]{:S(2)}, u32[]{:S(2)}) collective-permute-start(f32[7,32,128]{2,1,0:T(8,128)} %get-tuple-element.14), channel_id=1, source_target_pairs={{1,0},{2,1},{3,2},{5,4},{6,5},{7,6},{9,8},{10,9},{11,10},{13,12},{... | collective-permute-start | bytes 344072 | tf_op jit(solution)/shard_map/ppermute | solution.py:390
  54.8 4.4 %collective-permute-done.1.refs_4_.fn = f32[7,32,128]{2,1,0:T(8,128)S(1)} collective-permute-done((f32[7,32,128]{2,1,0:T(8,128)}, f32[7,32,128]{2,1,0:T(8,128)S(1)}, u32[]{:S(2)}, u32[]{:S(2)}) %collective-permute-start.1) | collective-permute-done | bytes 114720 | tf_op jit(solution)/shard_map/ppermute | solution.py:390
  59.8 5.6 %lon_pack.2 = (f32[7,48,128]{2,1,0:T(8,128)}, f32[7,48,128]{2,1,0:T(8,128)}) custom-call(f32[4,8,128,128]{3,2,1,0:T(8,128)} %t.3, f32[2,8,128,128]{3,2,1,0:T(8,128)} %v.3, f32[8,128,128]{2,1,0:T(8,128)} %m.3, f32[7,32,128]{2,1,0:T(8,128)} %copy-done.7, f32[7,32,128]{2,1,0:T(8,128)} %copy-done.9), custom_call_target="tpu_custom_call" | custom-call | tf_op jit(solution)/shard_map/lon_pack/pallas_call | solution.py:123
  65.4 1.0 %collective-permute-start.2 = (f32[7,48,128]{2,1,0:T(8,128)}, f32[7,48,128]{2,1,0:T(8,128)S(1)}, u32[]{:S(2)}, u32[]{:S(2)}) collective-permute-start(f32[7,48,128]{2,1,0:T(8,128)} %get-tuple-element.15), channel_id=1, source_target_pairs={{0,4},{4,8},{8,12},{12,16},{16,20},{20,24},{24,28},{28,0},{1,5},{5... | collective-permute-start | bytes 516104 | tf_op jit(solution)/shard_map/ppermute | solution.py:396
  66.3 3.5 %collective-permute-start.3 = (f32[7,48,128]{2,1,0:T(8,128)}, f32[7,48,128]{2,1,0:T(8,128)S(1)}, u32[]{:S(2)}, u32[]{:S(2)}) collective-permute-start(f32[7,48,128]{2,1,0:T(8,128)} %get-tuple-element.16), channel_id=1, source_target_pairs={{4,0},{8,4},{12,8},{16,12},{20,16},{24,20},{28,24},{0,28},{5,1},{9... | collective-permute-start | bytes 516104 | tf_op jit(solution)/shard_map/ppermute | solution.py:397
  69.9 1.2 %fusion.1 = f32[320,128]{1,0:T(8,128)S(1)} fusion(f32[320,128]{1,0:T(8,128)} %collective-permute-done.11, f32[320,128]{1,0:T(8,128)} %collective-permute-done.10, f32[320,128]{1,0:T(8,128)} %collective-permute-done.9, f32[1280,128]{1,0:T(8,128)} %copy-done.19), kind=kLoop, calls=%fused_computation.2 | loop fusion | flops 122880 | bytes 819200 | tf_op jit(solution)/shard_map/add | solution.py:447
  72.1 1.7 %collective-permute-start.13 = (f32[80,128]{1,0:T(8,128)S(1)}, f32[80,128]{1,0:T(8,128)S(1)}, u32[]{:S(2)}, u32[]{:S(2)}) collective-permute-start(f32[80,128]{1,0:T(8,128)S(1)} %get-tuple-element.29), channel_id=1, source_target_pairs={{0,16},{1,17},{2,18},{3,19},{4,20},{5,21},{6,22},{7,23},{8,24},{9,... | collective-permute-start | bytes 122888 | tf_op jit(solution)/shard_map/ppermute | solution.py:402
  74.5 1.0 %copy-done.5 = f32[8,128,128]{2,1,0:T(8,128)S(1)} copy-done((f32[8,128,128]{2,1,0:T(8,128)S(1)}, f32[8,128,128]{2,1,0:T(8,128)}, u32[]{:S(2)}) %copy-start.5) | copy-done | bytes 524312
  77.3 0.9 %copy-done.12 = f32[4,128,128]{2,1,0:T(8,128)S(1)} copy-done((f32[4,128,128]{2,1,0:T(8,128)S(1)}, f32[4,128,128]{2,1,0:T(8,128)}, u32[]{:S(2)}) %copy-start.12) | copy-done | bytes 262168
  78.3 15.8 %deep.1 = f32[4,8,128,128]{3,2,1,0:T(8,128)} custom-call(f32[4,8,128,128]{3,2,1,0:T(8,128)S(1)} %copy-done.1, f32[2,8,128,128]{3,2,1,0:T(8,128)S(1)} %copy-done.3, f32[8,128,128]{2,1,0:T(8,128)S(1)} %copy-done.5, s32[128,128]{1,0:T(8,128)S(1)} %copy-done.6, f32[7,32,128]{2,1,0:T(8,128)S(1)} %copy-done.8, f32[7,32,128]{2,1,0:T(8,128)S(1)} %copy-done.10, ...), custom_call_target="tpu_custom_call" | custom-call | tf_op jit(solution)/shard_map/deep/pallas_call | solution.py:374
  (62 shorter events, 10.0 us)
Async XLA Ops:
  0.6 8.2 %copy-start.20 = (s32[128,1,4]{0,2,1:T(4,128)S(1)}, s32[128,1,4]{0,2,1:T(4,128)}, u32[]{:S(2)}) copy-start(s32[128,1,4]{0,2,1:T(4,128)} %param.11) | copy-start | bytes 6148
  2.1 18.2 %copy-start = (f32[4,8,128,128]{3,2,1,0:T(8,128)S(1)}, f32[4,8,128,128]{3,2,1,0:T(8,128)}, u32[]{:S(2)}) copy-start(f32[4,8,128,128]{3,2,1,0:T(8,128)} %t.3) | copy-start | bytes 6291460
  2.1 18.2 %copy-start.2 = (f32[2,8,128,128]{3,2,1,0:T(8,128)S(1)}, f32[2,8,128,128]{3,2,1,0:T(8,128)}, u32[]{:S(2)}) copy-start(f32[2,8,128,128]{3,2,1,0:T(8,128)} %v.3) | copy-start | bytes 3145732
  2.1 18.2 %copy-start.6 = (s32[128,128]{1,0:T(8,128)S(1)}, s32[128,128]{1,0:T(8,128)}, u32[]{:S(2)}) copy-start(s32[128,128]{1,0:T(8,128)} %o.3) | copy-start | bytes 196612
  2.1 7.0 %collective-permute-start.4 = (f32[1,32,128]{2,1,0:T(8,128)}, f32[1,32,128]{2,1,0:T(8,128)S(1)}, u32[]{:S(2)}, u32[]{:S(2)}) collective-permute-start(f32[1,32,128]{2,1,0:T(8,128)} %get-tuple-element.17), channel_id=1, source_target_pairs={{0,1},{1,2},{2,3},{4,5},{5,6},{6,7},{8,9},{9,10},{10,11},{12,13},{... | collective-permute-start | bytes 49160 | tf_op jit(solution)/shard_map/ppermute | solution.py:389
  6.9 5.3 %collective-permute-start.5 = (f32[1,32,128]{2,1,0:T(8,128)}, f32[1,32,128]{2,1,0:T(8,128)S(1)}, u32[]{:S(2)}, u32[]{:S(2)}) collective-permute-start(f32[1,32,128]{2,1,0:T(8,128)} %get-tuple-element.18), channel_id=1, source_target_pairs={{1,0},{2,1},{3,2},{5,4},{6,5},{7,6},{9,8},{10,9},{11,10},{13,12},{... | collective-permute-start | bytes 49160 | tf_op jit(solution)/shard_map/ppermute | solution.py:390
  14.6 5.7 %collective-permute-start.6 = (f32[1,48,128]{2,1,0:T(8,128)}, f32[1,48,128]{2,1,0:T(8,128)S(1)}, u32[]{:S(2)}, u32[]{:S(2)}) collective-permute-start(f32[1,48,128]{2,1,0:T(8,128)} %get-tuple-element.19), channel_id=1, source_target_pairs={{0,4},{4,8},{8,12},{12,16},{16,20},{20,24},{24,28},{28,0},{1,5},{5... | collective-permute-start | bytes 73736 | tf_op jit(solution)/shard_map/ppermute | solution.py:396
  15.8 4.5 %collective-permute-start.7 = (f32[1,48,128]{2,1,0:T(8,128)}, f32[1,48,128]{2,1,0:T(8,128)S(1)}, u32[]{:S(2)}, u32[]{:S(2)}) collective-permute-start(f32[1,48,128]{2,1,0:T(8,128)} %get-tuple-element.20), channel_id=1, source_target_pairs={{4,0},{8,4},{12,8},{16,12},{20,16},{24,20},{28,24},{0,28},{5,1},{9... | collective-permute-start | bytes 73736 | tf_op jit(solution)/shard_map/ppermute | solution.py:397
  38.7 2.2 %collective-permute-start.8 = (f32[1280,128]{1,0:T(8,128)S(1)}, f32[1280,128]{1,0:T(8,128)S(1)}, u32[]{:S(2)}, u32[]{:S(2)}) collective-permute-start(f32[1280,128]{1,0:T(8,128)S(1)} %get-tuple-element.23), channel_id=1, source_target_pairs={{0,1},{1,0},{2,3},{3,2},{4,5},{5,4},{6,7},{7,6},{8,9},{9,8},{10,11... | collective-permute-start | bytes 1966088 | tf_op jit(solution)/shard_map/ppermute | solution.py:402
  41.9 28.0 %collective-permute-start.9 = (f32[320,128]{1,0:T(8,128)}, f32[320,128]{1,0:T(8,128)}, u32[]{:S(2)}, u32[]{:S(2)}) collective-permute-start(f32[320,128]{1,0:T(8,128)} %get-tuple-element.24), channel_id=1, source_target_pairs={{0,2},{1,3},{2,0},{3,1},{4,6},{5,7},{6,4},{7,5},{8,10},{9,11},{10,... | collective-permute-start | bytes 491528 | tf_op jit(solution)/shard_map/ppermute | solution.py:402
  42.7 27.2 %collective-permute-start.11 = (f32[320,128]{1,0:T(8,128)}, f32[320,128]{1,0:T(8,128)}, u32[]{:S(2)}, u32[]{:S(2)}) collective-permute-start(f32[320,128]{1,0:T(8,128)} %get-tuple-element.25), channel_id=1, source_target_pairs={{0,6},{1,7},{2,4},{3,5},{4,2},{5,3},{6,0},{7,1},{8,14},{9,15},{10,... | collective-permute-start | bytes 491528 | tf_op jit(solution)/shard_map/ppermute | solution.py:402
  43.6 26.2 %collective-permute-start.10 = (f32[320,128]{1,0:T(8,128)}, f32[320,128]{1,0:T(8,128)}, u32[]{:S(2)}, u32[]{:S(2)}) collective-permute-start(f32[320,128]{1,0:T(8,128)} %get-tuple-element.26), channel_id=1, source_target_pairs={{0,4},{1,5},{2,6},{3,7},{4,0},{5,1},{6,2},{7,3},{8,12},{9,13},{10,... | collective-permute-start | bytes 491528 | tf_op jit(solution)/shard_map/ppermute | solution.py:402
  48.7 6.0 %collective-permute-start = (f32[7,32,128]{2,1,0:T(8,128)}, f32[7,32,128]{2,1,0:T(8,128)S(1)}, u32[]{:S(2)}, u32[]{:S(2)}) collective-permute-start(f32[7,32,128]{2,1,0:T(8,128)} %get-tuple-element.13), channel_id=1, source_target_pairs={{0,1},{1,2},{2,3},{4,5},{5,6},{6,7},{8,9},{9,10},{10,11},{12,13},{... | collective-permute-start | bytes 344072 | tf_op jit(solution)/shard_map/ppermute | solution.py:389
  52.5 22.0 %copy-start.1 = (f32[4,8,128,128]{3,2,1,0:T(8,128)S(1)}, f32[4,8,128,128]{3,2,1,0:T(8,128)}, u32[]{:S(2)}) copy-start(f32[4,8,128,128]{3,2,1,0:T(8,128)} %t.3) | copy-start | bytes 6291460
  52.5 21.9 %copy-start.3 = (f32[2,8,128,128]{3,2,1,0:T(8,128)S(1)}, f32[2,8,128,128]{3,2,1,0:T(8,128)}, u32[]{:S(2)}) copy-start(f32[2,8,128,128]{3,2,1,0:T(8,128)} %v.3) | copy-start | bytes 3145732
  52.5 21.9 %copy-start.15 = (f32[1,32,128]{2,1,0:T(8,128)S(1)}, f32[1,32,128]{2,1,0:T(8,128)}, u32[]{:S(2)}) copy-start(f32[1,32,128]{2,1,0:T(8,128)} %copy-done.13) | copy-start | bytes 49156
  52.5 21.9 %copy-start.18 = (f32[1,32,128]{2,1,0:T(8,128)S(1)}, f32[1,32,128]{2,1,0:T(8,128)}, u32[]{:S(2)}) copy-start(f32[1,32,128]{2,1,0:T(8,128)} %copy-done.16) | copy-start | bytes 49156
  52.6 6.6 %collective-permute-start.1 = (f32[7,32,128]{2,1,0:T(8,128)}, f32[7,32,128]{2,1,0:T(8,128)S(1)}, u32[]{:S(2)}, u32[]{:S(2)}) collective-permute-start(f32[7,32,128]{2,1,0:T(8,128)} %get-tuple-element.14), channel_id=1, source_target_pairs={{1,0},{2,1},{3,2},{5,4},{6,5},{7,6},{9,8},{10,9},{11,10},{13,12},{... | collective-permute-start | bytes 344072 | tf_op jit(solution)/shard_map/ppermute | solution.py:390
  54.8 4.4 %copy-start.7 = (f32[7,32,128]{2,1,0:T(8,128)}, f32[7,32,128]{2,1,0:T(8,128)S(1)}, u32[]{:S(2)}) copy-start(f32[7,32,128]{2,1,0:T(8,128)S(1)} %collective-permute-done.refs_3_.fs) | copy-start | bytes 344068
  65.4 8.4 %collective-permute-start.2 = (f32[7,48,128]{2,1,0:T(8,128)}, f32[7,48,128]{2,1,0:T(8,128)S(1)}, u32[]{:S(2)}, u32[]{:S(2)}) collective-permute-start(f32[7,48,128]{2,1,0:T(8,128)} %get-tuple-element.15), channel_id=1, source_target_pairs={{0,4},{4,8},{8,12},{12,16},{16,20},{20,24},{24,28},{28,0},{1,5},{5... | collective-permute-start | bytes 516104 | tf_op jit(solution)/shard_map/ppermute | solution.py:396
  66.3 8.2 %collective-permute-start.3 = (f32[7,48,128]{2,1,0:T(8,128)}, f32[7,48,128]{2,1,0:T(8,128)S(1)}, u32[]{:S(2)}, u32[]{:S(2)}) collective-permute-start(f32[7,48,128]{2,1,0:T(8,128)} %get-tuple-element.16), channel_id=1, source_target_pairs={{4,0},{8,4},{12,8},{16,12},{20,16},{24,20},{28,24},{0,28},{5,1},{9... | collective-permute-start | bytes 516104 | tf_op jit(solution)/shard_map/ppermute | solution.py:397
  71.1 23.1 %collective-permute-start.12 = (f32[80,128]{1,0:T(8,128)S(1)}, f32[80,128]{1,0:T(8,128)S(1)}, u32[]{:S(2)}, u32[]{:S(2)}) collective-permute-start(f32[80,128]{1,0:T(8,128)S(1)} %get-tuple-element.27), channel_id=1, source_target_pairs={{0,8},{1,9},{2,10},{3,11},{4,12},{5,13},{6,14},{7,15},{8,0},{9,1},... | collective-permute-start | bytes 122888 | tf_op jit(solution)/shard_map/ppermute | solution.py:402
  71.1 23.0 %collective-permute-start.14 = (f32[80,128]{1,0:T(8,128)S(1)}, f32[80,128]{1,0:T(8,128)S(1)}, u32[]{:S(2)}, u32[]{:S(2)}) collective-permute-start(f32[80,128]{1,0:T(8,128)S(1)} %get-tuple-element.28), channel_id=1, source_target_pairs={{0,24},{1,25},{2,26},{3,27},{4,28},{5,29},{6,30},{7,31},{8,16},{9,... | collective-permute-start | bytes 122888 | tf_op jit(solution)/shard_map/ppermute | solution.py:402
  72.1 22.1 %collective-permute-start.13 = (f32[80,128]{1,0:T(8,128)S(1)}, f32[80,128]{1,0:T(8,128)S(1)}, u32[]{:S(2)}, u32[]{:S(2)}) collective-permute-start(f32[80,128]{1,0:T(8,128)S(1)} %get-tuple-element.29), channel_id=1, source_target_pairs={{0,16},{1,17},{2,18},{3,19},{4,20},{5,21},{6,22},{7,23},{8,24},{9,... | collective-permute-start | bytes 122888 | tf_op jit(solution)/shard_map/ppermute | solution.py:402
  (12 other events, 13.9 us)
where the time goes:
time: 95.8 us; the launch traced here: 94.8 us
  Pallas kernels  44.7 us (47%)
  starting transfers between devices  26.9 us (28%)
  waiting for transfers between devices  11.7 us (12%)
  local copies, waits for them, and re-layouts  8.78 us (9%)
  other arithmetic  1.9 us (2%)
    pallas_call x1, Pallas kernels, deep(): pl.pallas_call(deep_kernel, grid=(levels,), in_specs=specs + strip + fixe...  15.8 us
    pallas_call x1, Pallas kernels, surface(): pl.pallas_call(functools.partial(surface_kernel, order, accs), grid_spec=...  15.8 us
    ppermute x2, starting transfers between devices, exchange_lat(): lax.ppermute(to_north, 'gy', [(i, i + 1) for i in range(n - 1)])  8.57 us
    unnamed x43, local copies, waits for them, and re-layouts  7.83 us
    ppermute x2, waiting for transfers between devices, exchange_lat(): lax.ppermute(to_south, 'gy', [(i + 1, i) for i in range(n - 1)])  7.45 us
    pallas_call x2, Pallas kernels, lon_pack(): pl.pallas_call(functools.partial(lon_pack_kernel, has_ocean), grid=(level...  7.42 us
    ppermute x2, starting transfers between devices, exchange_lon(): lax.ppermute(to_west, 'gx', [((i + 1) % n, i) for i in range(n)])  6.57 us
    pallas_call x2, Pallas kernels, lat_pack(): pl.pallas_call(functools.partial(lat_pack_kernel, has_ocean), grid=(level...  5.6 us
  transfers between devices with their start and end apart: 15, of which 5 were waited for; matrix products, arithmetic and copies ran while one was open for 2% of the time, Pallas kernels for 27%

commit v1 on v0

v1 whole, which is shorter than its diff:
```python
import functools

import jax
import jax.numpy as jnp
from jax import lax
from jax.experimental import pallas as pl
from jax.experimental.pallas import tpu as pltpu
from jax.sharding import PartitionSpec as P

STEPS = 4
ABD = 16
NTR = 4
FIELDS = 8
OFF = 16
FETCHES = 1
GROUP = 48
AXES = ("gx", "gy")


WHOLE = pl.BlockSpec(memory_space=pltpu.VMEM)


def took(us):
    return pl.CostEstimate(flops=0, bytes_accessed=int(us * 3.5e6), transcendentals=0)


def lane_ids(rows):
    return lax.broadcasted_iota(jnp.int32, (rows, 128), 1)


def sub_ids(rows):
    return lax.broadcasted_iota(jnp.int32, (rows, 128), 0)


def lat_pack_kernel(tl, vl, ml, ol, th, vh, mh, oh, south_ref, north_ref):
    top = sub_ids(8) < 4
    for level in range(tl.shape[1]):

        def fields(t, v, m, o):
            out = [t[i, level] for i in range(NTR)] + [v[0, level], v[1, level], m[level]]
            out.append(o[...].astype(jnp.float32) if level == 0 else m[level])
            return out

        low, high = fields(tl, vl, ml, ol), fields(th, vh, mh, oh)
        for p in range(FIELDS // 2):
            a, b = low[2 * p], low[2 * p + 1]
            south_ref[level, 8 * p : 8 * p + 8] = jnp.where(top, a, pltpu.roll(b, 4, 0))
            a, b = high[2 * p], high[2 * p + 1]
            north_ref[level, 8 * p : 8 * p + 8] = jnp.where(top, pltpu.roll(a, 4, 0), b)


def lat_pack(tracers, velocity, mixing, ocean):
    levels, rows = tracers.shape[1:3]
    last = rows // 8 - 1

    def specs(block):
        return [
            pl.BlockSpec((NTR, levels, 8, 128), lambda l: (0, 0, block, 0)),
            pl.BlockSpec((2, levels, 8, 128), lambda l: (0, 0, block, 0)),
            pl.BlockSpec((levels, 8, 128), lambda l: (0, block, 0)),
            pl.BlockSpec((8, 128), lambda l: (block, 0)),
        ]

    arrays = [tracers, velocity, mixing, ocean]
    strip = jax.ShapeDtypeStruct((levels, 32, 128), jnp.float32)
    return pl.pallas_call(
        lat_pack_kernel,
        grid=(1,),
        in_specs=specs(0) + specs(last),
        out_specs=[WHOLE] * 2,
        out_shape=[strip, strip],
        cost_estimate=took(2),
        name="lat_pack",
    )(*arrays, *arrays)


def lat_halo_blocks(from_south, from_north, f, level):
    p, odd = f // 2, f % 2
    s = from_south[level, 8 * p : 8 * p + 8]
    n = from_north[level, 8 * p : 8 * p + 8]
    if odd:
        return s, pltpu.roll(n, 4, 0)
    return pltpu.roll(s, 4, 0), n


def interior(t, v, m, o, f, level):
    if f < NTR:
        return t[f, level]
    if f < NTR + 2:
        return v[f - NTR, level]
    if f == NTR + 2:
        return m[level]
    return o[...].astype(jnp.float32)


def fetch(part, parts, w, out, sem):
    rows = w.shape[0] // parts
    return pltpu.make_async_copy(w.at[pl.ds(part * rows, rows)], out, sem)


def fetched(w, parts):
    return pltpu.VMEM((w.shape[0] // parts,) + w.shape[1:], w.dtype)


def lon_pack_kernel(first, fetching, t, v, m, o, fs, fn, *refs):
    if fetching is None:
        lon_pack_body(first, t, v, m, o, fs, fn, *refs)
        return
    w, west_ref, east_ref, out, sem = refs
    copy = fetch(*fetching, w, out, sem)
    copy.start()
    lon_pack_body(first, t, v, m, o, fs, fn, west_ref, east_ref)
    copy.wait()


def lon_pack_body(first, t, v, m, o, fs, fn, west_ref, east_ref):
    rows = t.shape[2]
    lane = lane_ids(GROUP)
    groups = (rows + 16) // GROUP
    for l in range(west_ref.shape[0]):
        level = first + l
        west = jnp.zeros((GROUP, 128), jnp.float32)
        east = jnp.zeros((GROUP, 128), jnp.float32)
        for f in range(FIELDS if level == 0 else FIELDS - 1):
            s, n = lat_halo_blocks(fs, fn, f, level)
            whole = jnp.concatenate([s, interior(t, v, m, o, f, level), n], axis=0)
            for g in range(groups):
                at = 32 * g + 4 * f
                moved = pltpu.roll(whole[GROUP * g : GROUP * g + GROUP], (at - 124) % 128, 1)
                east = jnp.where((lane >= at) & (lane < at + 4), moved, east)
                west = jnp.where((lane >= at + 4) & (lane < at + 8), moved, west)
        west_ref[l] = west
        east_ref[l] = east


def lon_pack(tracers, velocity, mixing, ocean, from_south, from_north, first, levels,
             fetching=None, weights=None):
    strip = jax.ShapeDtypeStruct((levels, GROUP, 128), jnp.float32)
    more = [] if fetching is None else [pl.BlockSpec(memory_space=pltpu.HBM)]
    out = [] if fetching is None else [fetched(weights, fetching[1])]
    return pl.pallas_call(
        functools.partial(lon_pack_kernel, first, fetching),
        in_specs=[WHOLE] * 6 + more,
        out_specs=[WHOLE] * (2 + len(out)),
        out_shape=[strip, strip] + out,
        scratch_shapes=[pltpu.SemaphoreType.DMA] * len(out),
        compiler_params=pltpu.CompilerParams(vmem_limit_bytes=4 << 20),
        cost_estimate=took(0.6 * levels),
        name="lon_pack",
    )(tracers, velocity, mixing, ocean, from_south, from_north, *([weights] if more else []))


def unpack_field(ext, f, level, t, v, m, o, fs, fn, even, odd):
    rows = t.shape[2]
    s, n = lat_halo_blocks(fs, fn, f, level)
    ext[0, OFF - 8 : OFF] = s
    ext[0, OFF : OFF + rows] = interior(t, v, m, o, f, level)
    ext[0, OFF + rows : OFF + rows + 8] = n
    strip = odd if f % 2 else even
    for g in range((rows + 16) // GROUP):
        base = OFF - 8 + GROUP * g
        ext[1, base : base + GROUP] = pltpu.roll(strip, (124 - (32 * g + 4 * f)) % 128, 1)


def strips(fw, fe, l):
    near = lane_ids(GROUP) % 8 < 4
    w, e = fw[l], fe[l]
    return jnp.where(near, w, e), jnp.where(near, e, w)


def to_right(a, b):
    end = lane_ids(a.shape[0]) == 127
    ra, rb = pltpu.roll(a, 127, 1), pltpu.roll(b, 127, 1)
    return jnp.where(end, rb, ra), jnp.where(end, ra, rb)


def to_left(a, b):
    start = lane_ids(a.shape[0]) == 0
    ra, rb = pltpu.roll(a, 1, 1), pltpu.roll(b, 1, 1)
    return jnp.where(start, rb, ra), jnp.where(start, ra, rb)


CHUNK = 24


def chunks(rows):
    return range(OFF - 8, OFF + rows + 8, CHUNK)


def faces(a, b, mix, face):
    vel = a + b
    low = jnp.maximum(vel, 0.0) + mix
    return face * low, face * (low - vel)


def coefficients(rows, u, v, k, oc, coef, north):
    for r in chunks(rows):
        here, above = slice(r, r + CHUNK), slice(r + 1, r + CHUNK + 1)
        for h in range(2):
            face = 0.5 * (oc[h, here] * oc[h, above])
            na, nb = faces(v[h, here], v[h, above], k[h, here] + k[h, above], face)
            north[h, here] = na
            coef[3, h, here] = nb
    for r in chunks(rows):
        here, below = slice(r, r + CHUNK), slice(r - 1, r + CHUNK - 1)
        us, ks, os = ((x[0, here], x[1, here]) for x in (u, k, oc))
        ur, kr, orr = to_right(*us), to_right(*ks), to_right(*os)
        ea, eb = [], []
        for h in range(2):
            a, b = faces(us[h], ur[h], ks[h] + kr[h], 0.5 * (os[h] * orr[h]))
            ea.append(a)
            eb.append(b)
        wa, wb = to_left(*ea), to_left(*eb)
        for h in range(2):
            south = north[h, below]
            coef[0, h, here] = (1.0 - (ea[h] + wb[h])) - (north[h, here] + coef[3, h, below])
            coef[1, h, here] = eb[h]
            coef[2, h, here] = wa[h]
            coef[4, h, here] = south


def advance(rows, coef, q):
    for step in range(STEPS):
        src, dst = step % 2, (step + 1) % 2
        for r in chunks(rows):
            here = slice(r, r + CHUNK)
            c = [[coef[i, h, here] for h in range(2)] for i in range(5)]
            for i in range(NTR):
                mid = [q[src, i, h, here] for h in range(2)]
                right, left = to_right(*mid), to_left(*mid)
                for h in range(2):
                    up = q[src, i, h, r + 1 : r + CHUNK + 1]
                    down = q[src, i, h, r - 1 : r + CHUNK - 1]
                    q[dst, i, h, here] = (
                        c[0][h] * mid[h]
                        + c[1][h] * right[h]
                        + c[2][h] * left[h]
                        + c[3][h] * up
                        + c[4][h] * down
                    )


def field_scratch(rows):
    ext = (2, rows + 32, 128)
    return [
        pltpu.VMEM((4,) + ext, jnp.float32),
        pltpu.VMEM(ext, jnp.float32),
        pltpu.VMEM((5,) + ext, jnp.float32),
        pltpu.VMEM((2, NTR) + ext, jnp.float32),
    ]


def run_level(rows, level, l, t, v, m, o, fs, fn, fw, fe, vel, north, coef, q):
    even, odd = strips(fw, fe, l)
    for i in range(NTR):
        unpack_field(q.at[0, i], i, level, t, v, m, o, fs, fn, even, odd)
    for i in range(3):
        unpack_field(vel.at[i], NTR + i, level, t, v, m, o, fs, fn, even, odd)
    coefficients(rows, vel.at[0], vel.at[1], vel.at[2], vel.at[3], coef, north)
    advance(rows, coef, q)


def unpack_ocean(t, v, m, o, fs, fn, fw, fe, vel):
    even, odd = strips(fw, fe, 0)
    unpack_field(vel.at[3], FIELDS - 1, 0, t, v, m, o, fs, fn, even, odd)


def surface_kernel(
    order, accs, slot, t, v, m, o, fs, fn, fw, fe, *refs):
    surface_body(order, accs, slot, t, v, m, o, fs, fn, fw, fe, refs[:FETCHES], *refs[FETCHES:])


def surface_body(
    order, accs, slot, t, v, m, o, fs, fn, fw, fe, ws, out_q, out_send, out_keep,
    vel, north, coef, q, surf, *sums,
):
    rows = t.shape[2]
    unpack_ocean(t, v, m, o, fs, fn, fw, fe, vel)
    run_level(rows, 0, 0, t, v, m, o, fs, fn, fw, fe, vel, north, coef, q)
    ocean = o[...].astype(jnp.float32)
    for i in range(NTR):
        done = q[0, i, 0, OFF : OFF + rows]
        out_q[i] = done
        surf[pl.ds(i, rows, stride=8), :] = done * ocean
    surf[pl.ds(NTR, rows, stride=8), :] = ocean
    for i in range(NTR + 1, 8):
        surf[pl.ds(i, rows, stride=8), :] = jnp.zeros((rows, 128), jnp.float32)
    for d in sums:
        d[...] = jnp.zeros_like(d)
    first = sub_ids(16) < 8
    kb = ws[0].shape[1]
    per = rows // FETCHES // 2

    def body(w, base, i, carry):
        j = i + base
        s = surf[pl.ds(pl.multiple_of(16 * j, 16), 16), :]
        lhs = jnp.concatenate(
            [jnp.where(first, s, 0.0), jnp.where(first, 0.0, s)], axis=1
        ).astype(jnp.bfloat16)
        for k in range(0, kb, 2):
            rhs = jnp.concatenate(
                [
                    jnp.concatenate([w[2 * i + r, k], w[2 * i + r, k + 1]], axis=1)
                    for r in range(2)
                ],
                axis=0,
            )
            part = jnp.dot(lhs, rhs, preferred_element_type=jnp.float32)
            for r in range(2):
                for kk in range(2):
                    d = sums[(k + kk) % accs]
                    at = pl.ds(
                        pl.multiple_of(8 * slot[(2 * j + r) * kb + k + kk], 8), 8
                    )
                    d[at, :] += part[8 * r : 8 * r + 8, 128 * kk : 128 * kk + 128]
        return carry

    for n, w in enumerate(ws):
        lax.fori_loop(0, per, functools.partial(body, w, n * per), 0, unroll=16)
    chunk = ABD * (NTR + 1)
    half = len(order) // 2
    for place, owner in enumerate(order):
        ref, base = (out_keep, place) if place < half else (out_send, place - half)
        for f in range(NTR + 1):
            total = sums[0][pl.ds(owner * ABD * 8 + f, ABD, stride=8), :]
            for d in sums[1:]:
                total = total + d[pl.ds(owner * ABD * 8 + f, ABD, stride=8), :]
            at = base * chunk + f * ABD
            ref[at : at + ABD, :] = total


def surface(order, slot, tracers, velocity, mixing, ocean, halo, weights):
    rows = tracers.shape[2]
    owners = len(order)
    accs = 4 if owners <= 32 else 1
    half = owners // 2 * ABD * (NTR + 1)
    return pl.pallas_call(
        functools.partial(surface_kernel, order, accs),
        in_specs=[pl.BlockSpec(memory_space=pltpu.SMEM)] + [WHOLE] * (8 + FETCHES),
        out_specs=[WHOLE] * 3,
        scratch_shapes=field_scratch(rows)
        + [pltpu.VMEM((rows * 8, 128), jnp.float32)]
        + [pltpu.VMEM((owners * ABD * 8, 128), jnp.float32)] * accs,
        out_shape=[
            jax.ShapeDtypeStruct((NTR, rows, 128), jnp.float32),
            jax.ShapeDtypeStruct((half, 128), jnp.float32),
            jax.ShapeDtypeStruct((half, 128), jnp.float32),
        ],
        compiler_params=pltpu.CompilerParams(vmem_limit_bytes=22 << 20),
        cost_estimate=took(7),
        name="surface",
    )(slot, tracers, velocity, mixing, ocean, *halo, *weights)


def deep_kernel(first, t, v, m, o, fs, fn, fw, fe, ofw, ofe, base, out, vel, north, coef, q):
    rows = t.shape[2]
    level = pl.program_id(0) + first

    @pl.when(pl.program_id(0) == 0)
    def _():
        unpack_ocean(t, v, m, o, fs, fn, ofw, ofe, vel)

    if first == 0:
        @pl.when(level == 0)
        def _():
            out[:, 0] = base[...]

    @pl.when(level > 0)
    def _():
        run_level(rows, level, level - 1, t, v, m, o, fs, fn, fw, fe, vel, north, coef, q)
        for i in range(NTR):
            out[i, 0] = q[0, i, 0, OFF : OFF + rows]


def deep(tracers, velocity, mixing, ocean, halo, ocean_halo, base, first, levels):
    rows = tracers.shape[2]
    return pl.pallas_call(
        functools.partial(deep_kernel, first),
        grid=(levels,),
        in_specs=[WHOLE] * 10 + [pl.BlockSpec(memory_space=pl.ANY) if first else WHOLE],
        out_specs=pl.BlockSpec((NTR, 1, rows, 128), lambda l: (0, l + first, 0, 0)),
        out_shape=jax.ShapeDtypeStruct(tracers.shape, jnp.float32),
        scratch_shapes=field_scratch(rows),
        input_output_aliases={10: 0} if first else {},
        compiler_params=pltpu.CompilerParams(vmem_limit_bytes=16 << 20),
        cost_estimate=took(1.8 * levels),
        name="deep",
    )(tracers, velocity, mixing, ocean, *halo, *ocean_halo, base)


def exchange_lat(to_south, to_north):
    n = lax.axis_size("gy")
    from_south = lax.ppermute(to_north, "gy", [(i, i + 1) for i in range(n - 1)])
    from_north = lax.ppermute(to_south, "gy", [(i + 1, i) for i in range(n - 1)])
    return from_south, from_north


def exchange_lon(to_west, to_east):
    n = lax.axis_size("gx")
    from_west = lax.ppermute(to_east, "gx", [(i, (i + 1) % n) for i in range(n)])
    from_east = lax.ppermute(to_west, "gx", [((i + 1) % n, i) for i in range(n)])
    return from_west, from_east


def partner(a, mask, n):
    return lax.ppermute(a, AXES, [(i, i ^ mask) for i in range(n)])


def rounds_of(owners):
    bits = owners.bit_length() - 1
    out, at = [(0, 1)], 1
    while at < bits:
        width = min(2, bits - at)
        out.append((at, width))
        at += width
    return out


def order_of(owners):
    def key(owner):
        return tuple((owner >> at) & ((1 << width) - 1) for at, width in rounds_of(owners))
    return sorted(range(owners), key=key)


def per_device(tracers, velocity, mixing, land_mask, remap_weights, remap_dest):
    remap_weights = pltpu.with_memory_space_constraint(remap_weights, pltpu.HBM)
    owners = lax.axis_size("gx") * lax.axis_size("gy")
    levels = tracers.shape[1]
    me = lax.axis_index("gx") * lax.axis_size("gy") + lax.axis_index("gy")
    dest = remap_dest.reshape(-1)
    slot = jnp.bitwise_xor(dest // ABD, me) * ABD + dest % ABD

    tile = (tracers, velocity, mixing, land_mask)
    lat = exchange_lat(*lat_pack(*tile))
    to_west, to_east = lon_pack(*tile, *lat, 0, 1)
    lon0 = exchange_lon(to_west, to_east)
    lat, to_west = lax.optimization_barrier((lat, to_west))
    packed = lon_pack(*tile, *lat, 1, levels - 1, (0, FETCHES), remap_weights)
    lon0, packed = lax.optimization_barrier((lon0, packed))
    lon1 = exchange_lon(*packed[:2])

    order = order_of(owners)
    done, send, keep = surface(order, slot, *tile, lat + lon0,
        [pltpu.with_memory_space_constraint(w, pltpu.VMEM) for w in packed[2:]],
    )
    got = partner(send, 1, owners)
    total = keep + got
    lat, total = lax.optimization_barrier((lat, total))
    values = done
    rounds = rounds_of(owners)[1:]
    cut = [0] + [levels * (i + 1) // len(rounds) for i in range(len(rounds))]
    cut[1:-1] = [c + 1 for c in cut[1:-1]]
    for i, (at, width) in enumerate(rounds):
        parts = total.reshape((1 << width, -1, 128))
        got = [partner(parts[j], j << at, owners) for j in range(1, 1 << width)]
        values = deep(*tile, lat + lon1, lon0, values, cut[i], cut[i + 1] - cut[i])
        got, values = lax.optimization_barrier((got, values))
        total = parts[0]
        for g in got:
            total = total + g
    atmo = total.reshape(NTR + 1, ABD, 128).transpose(1, 0, 2)
    return values, atmo


def solution(mesh):
    placed = (
        P(None, None, "gy", "gx"),
        P(None, None, "gy", "gx"),
        P(None, "gy", "gx"),
        P("gy", "gx"),
        P("gy", None, "gx", None),
        P("gy", "gx", None),
    )
    return jax.shard_map(
        per_device,
        mesh=mesh,
        in_specs=placed,
        out_specs=(P(None, None, "gy", "gx"), P(("gx", "gy"), None, None)),
        check_vma=False,
    )
```

time: 95.8 us -> 69.4 us (0.72)
  the two profiles are of different devices: /device:TPU:1 before, /device:TPU:0 now
where the time goes in v1:
time: 69.4 us; the launch traced here: 69.1 us
  Pallas kernels  31.8 us (46%)
  starting transfers between devices  24.4 us (35%)
  waiting for transfers between devices  10.1 us (15%)
  local copies, waits for them, and re-layouts  1.32 us (2%)
  between operations  0.82 us (1%)
  other arithmetic  0.75 us (1%)
    pallas_call x2, Pallas kernels, deep(): pl.pallas_call(functools.partial(deep_kernel, first), grid=(levels,), in_...  16.3 us
    ppermute x7, starting transfers between devices, partner(): return lax.ppermute(a, AXES, [(i, i ^ mask) for i in range(n)])  11.2 us
    ppermute x2, starting transfers between devices, exchange_lon(): lax.ppermute(to_west, 'gx', [((i + 1) % n, i) for i in range(n)])  7.92 us
    pallas_call x2, Pallas kernels, lon_pack(): pl.pallas_call(functools.partial(lon_pack_kernel, first, fetching), in_sp...  6.86 us
    pallas_call x1, Pallas kernels, surface(): pl.pallas_call(functools.partial(surface_kernel, order, accs), in_specs=[...  6.72 us
    ppermute x1, waiting for transfers between devices, exchange_lat(): lax.ppermute(to_south, 'gy', [(i + 1, i) for i in range(n - 1)])  4 us
    ppermute x2, waiting for transfers between devices, exchange_lon(): lax.ppermute(to_east, 'gx', [(i, (i + 1) % n) for i in range(n)])  3.52 us
    ppermute x2, waiting for transfers between devices, exchange_lon(): lax.ppermute(to_west, 'gx', [((i + 1) % n, i) for i in range(n)])  2.52 us
  transfers between devices with their start and end apart: 13, of which 3 were waited for; matrix products, arithmetic and copies ran while one was open for 0% of the time, Pallas kernels for 33%

profile of v1, /device:TPU:0, one launch (start us, length us, event | category | flops | bytes accessed | tf_op | source)
XLA Modules:
  0.0 69.1 jit_solution(11958454767874132828)
XLA Ops:
  0.7 2.0 %lat_pack.1 = (f32[8,32,128]{2,1,0:T(8,128)}, f32[8,32,128]{2,1,0:T(8,128)}) custom-call(f32[4,8,128,128]{3,2,1,0:T(8,128)} %t.9, f32[2,8,128,128]{3,2,1,0:T(8,128)} %v.9, f32[8,128,128]{2,1,0:T(8,128)} %m.9, s32[128,128]{1,0:T(8,128)} %o.9, f32[4,8,128,128]{3,2,1,0:T(8,128)} %t.9, f32[2,8,128,128]{3,2,1,0:T(8,128)} %v.9, f32[8,128,128]{2,1,0:T(8,128)} %m.9, ...), custom_call_target="tpu_custom_call" | custom-call | bytes 7000000 | tf_op jit(solution)/shard_map/lat_pack/pallas_call | solution.py:66
  2.6 2.4 %collective-permute-start = (f32[8,32,128]{2,1,0:T(8,128)}, f32[8,32,128]{2,1,0:T(8,128)S(1)}, u32[]{:S(2)}, u32[]{:S(2)}) collective-permute-start(f32[8,32,128]{2,1,0:T(8,128)} %get-tuple-element.30), channel_id=1, source_target_pairs={{0,1},{1,2},{2,3},{4,5},{5,6},{6,7},{8,9},{9,10},{10,11},{12,13},{... | collective-permute-start | bytes 393224 | tf_op jit(solution)/shard_map/ppermute | solution.py:393
  5.0 1.3 %collective-permute-start.1 = (f32[8,32,128]{2,1,0:T(8,128)}, f32[8,32,128]{2,1,0:T(8,128)S(1)}, u32[]{:S(2)}, u32[]{:S(2)}) collective-permute-start(f32[8,32,128]{2,1,0:T(8,128)} %get-tuple-element.31), channel_id=1, source_target_pairs={{1,0},{2,1},{3,2},{5,4},{6,5},{7,6},{9,8},{10,9},{11,10},{13,12},{... | collective-permute-start | bytes 393224 | tf_op jit(solution)/shard_map/ppermute | solution.py:394
  6.3 0.1 copy.9
  6.4 0.1 reshape.28
  6.5 4.0 %collective-permute-done.1.fn = f32[8,32,128]{2,1,0:T(8,128)S(1)} collective-permute-done((f32[8,32,128]{2,1,0:T(8,128)}, f32[8,32,128]{2,1,0:T(8,128)S(1)}, u32[]{:S(2)}, u32[]{:S(2)}) %collective-permute-start.1) | collective-permute-done | bytes 131104 | tf_op jit(solution)/shard_map/ppermute | solution.py:394
  10.6 1.0 %copy-done.2 = f32[8,128,128]{2,1,0:T(8,128)S(1)} copy-done((f32[8,128,128]{2,1,0:T(8,128)S(1)}, f32[8,128,128]{2,1,0:T(8,128)}, u32[]{:S(2)}) %copy-start.2) | copy-done | bytes 524312
  11.6 0.2 lon_pack.2
  11.8 1.6 %collective-permute-start.2 = (f32[1,48,128]{2,1,0:T(8,128)S(1)}, f32[1,48,128]{2,1,0:T(8,128)S(1)}, u32[]{:S(2)}, u32[]{:S(2)}) collective-permute-start(f32[1,48,128]{2,1,0:T(8,128)S(1)} %get-tuple-element.35), channel_id=1, source_target_pairs={{0,4},{4,8},{8,12},{12,16},{16,20},{20,24},{24,28},{28,0},{1,5},{5... | collective-permute-start | bytes 73736 | tf_op jit(solution)/shard_map/ppermute | solution.py:400
  13.4 3.2 %collective-permute-start.3 = (f32[1,48,128]{2,1,0:T(8,128)S(1)}, f32[1,48,128]{2,1,0:T(8,128)S(1)}, u32[]{:S(2)}, u32[]{:S(2)}) collective-permute-start(f32[1,48,128]{2,1,0:T(8,128)S(1)} %get-tuple-element.32), channel_id=1, source_target_pairs={{4,0},{8,4},{12,8},{16,12},{20,16},{24,20},{28,24},{0,28},{5,1},{9... | collective-permute-start | bytes 73736 | tf_op jit(solution)/shard_map/ppermute | solution.py:401
  16.6 6.6 %lon_pack.3 = (f32[7,48,128]{2,1,0:T(8,128)S(1)}, f32[7,48,128]{2,1,0:T(8,128)S(1)}, bf16[128,4,128,128]{3,2,1,0:T(8,128)(2,1)S(1)}) custom-call(f32[4,8,128,128]{3,2,1,0:T(8,128)S(1)} %copy-done, f32[2,8,128,128]{3,2,1,0:T(8,128)S(1)} %copy-done.1, f32[8,128,128]{2,1,0:T(8,128)S(1)} %copy-done.3, s32[128,128]{1,0:T(8,128)S(1)} %copy-done.4, ...), custom_call_target="tpu_custom_call" | custom-call | bytes 14700000 | tf_op jit(solution)/shard_map/lon_pack/pallas_call | solution.py:141
  23.3 6.7 %surface.1 = (f32[4,128,128]{2,1,0:T(8,128)S(1)}, f32[1280,128]{1,0:T(8,128)S(1)}, f32[1280,128]{1,0:T(8,128)S(1)}) custom-call(s32[512]{0:T(512)S(1)} %fusion.4.slot, f32[4,8,128,128]{3,2,1,0:T(8,128)S(1)} %copy-done, f32[2,8,128,128]{3,2,1,0:T(8,128)S(1)} %copy-done.1, f32[8,128,128]{2,1,0:T(8,128)S(1)} %copy-done.3, s32[128,128]{1,0:T(8,128)S(1)} %copy-done.4, ...), custom_call_target="tpu_custom_call" | custom-call | bytes 24500000 | tf_op jit(solution)/shard_map/surface/pallas_call | solution.py:337
  30.0 3.2 %collective-permute-start.4 = (f32[1280,128]{1,0:T(8,128)S(1)}, f32[1280,128]{1,0:T(8,128)S(1)}, u32[]{:S(2)}, u32[]{:S(2)}) collective-permute-start(f32[1280,128]{1,0:T(8,128)S(1)} %get-tuple-element.43), channel_id=1, source_target_pairs={{0,1},{1,0},{2,3},{3,2},{4,5},{5,4},{6,7},{7,6},{8,9},{9,8},{10,11... | collective-permute-start | bytes 1966088 | tf_op jit(solution)/shard_map/ppermute | solution.py:406
  33.2 4.7 %collective-permute-start.9 = (f32[7,48,128]{2,1,0:T(8,128)S(1)}, f32[7,48,128]{2,1,0:T(8,128)S(1)}, u32[]{:S(2)}, u32[]{:S(2)}) collective-permute-start(f32[7,48,128]{2,1,0:T(8,128)S(1)} %get-tuple-element.48), channel_id=1, source_target_pairs={{4,0},{8,4},{12,8},{16,12},{20,16},{24,20},{28,24},{0,28},{5,1},{9... | collective-permute-start | bytes 516104 | tf_op jit(solution)/shard_map/ppermute | solution.py:401
  38.1 0.1 collective-permute-start.7
  38.2 1.8 %collective-permute-start.6 = (f32[320,128]{1,0:T(8,128)S(1)}, f32[320,128]{1,0:T(8,128)S(1)}, u32[]{:S(2)}, u32[]{:S(2)}) collective-permute-start(f32[320,128]{1,0:T(8,128)S(1)} %get-tuple-element.59), channel_id=1, source_target_pairs={{0,4},{1,5},{2,6},{3,7},{4,0},{5,1},{6,2},{7,3},{8,12},{9,13},{10,... | collective-permute-start | bytes 491528 | tf_op jit(solution)/shard_map/ppermute | solution.py:406
  39.9 1.7 %collective-permute-start.5 = (f32[320,128]{1,0:T(8,128)S(1)}, f32[320,128]{1,0:T(8,128)S(1)}, u32[]{:S(2)}, u32[]{:S(2)}) collective-permute-start(f32[320,128]{1,0:T(8,128)S(1)} %get-tuple-element.60), channel_id=1, source_target_pairs={{0,2},{1,3},{2,0},{3,1},{4,6},{5,7},{6,4},{7,5},{8,10},{9,11},{10,... | collective-permute-start | bytes 491528 | tf_op jit(solution)/shard_map/ppermute | solution.py:406
  41.6 3.5 %collective-permute-done.8.fw = f32[7,48,128]{2,1,0:T(8,128)S(1)} collective-permute-done((f32[7,48,128]{2,1,0:T(8,128)S(1)}, f32[7,48,128]{2,1,0:T(8,128)S(1)}, u32[]{:S(2)}, u32[]{:S(2)}) %collective-permute-start.8) | collective-permute-done | bytes 172064 | tf_op jit(solution)/shard_map/ppermute | solution.py:400
  45.2 2.5 %collective-permute-done.9.fe = f32[7,48,128]{2,1,0:T(8,128)S(1)} collective-permute-done((f32[7,48,128]{2,1,0:T(8,128)S(1)}, f32[7,48,128]{2,1,0:T(8,128)S(1)}, u32[]{:S(2)}, u32[]{:S(2)}) %collective-permute-start.9) | collective-permute-done | bytes 172064 | tf_op jit(solution)/shard_map/ppermute | solution.py:401
  47.7 9.2 %deep.2.base = f32[4,8,128,128]{3,2,1,0:T(8,128)} custom-call(f32[4,8,128,128]{3,2,1,0:T(8,128)S(1)} %copy-done, f32[2,8,128,128]{3,2,1,0:T(8,128)S(1)} %copy-done.1, f32[8,128,128]{2,1,0:T(8,128)S(1)} %copy-done.3, s32[128,128]{1,0:T(8,128)S(1)} %copy-done.4, f32[8,32,128]{2,1,0:T(8,128)S(1)} %collective-permute-done.fs, ...), custom_call_target="tpu_custom_call" | custom-call | bytes 31500000 | tf_op jit(solution)/shard_map/deep/pallas_call | solution.py:377
  56.9 1.8 %collective-permute-start.12 = (f32[80,128]{1,0:T(8,128)S(1)}, f32[80,128]{1,0:T(8,128)S(1)}, u32[]{:S(2)}, u32[]{:S(2)}) collective-permute-start(f32[80,128]{1,0:T(8,128)S(1)} %get-tuple-element.61), channel_id=1, source_target_pairs={{0,24},{1,25},{2,26},{3,27},{4,28},{5,29},{6,30},{7,31},{8,16},{9,... | collective-permute-start | bytes 122888 | tf_op jit(solution)/shard_map/ppermute | solution.py:406
  58.7 2.7 %collective-permute-start.10 = (f32[80,128]{1,0:T(8,128)S(1)}, f32[80,128]{1,0:T(8,128)S(1)}, u32[]{:S(2)}, u32[]{:S(2)}) collective-permute-start(f32[80,128]{1,0:T(8,128)S(1)} %get-tuple-element.63), channel_id=1, source_target_pairs={{0,8},{1,9},{2,10},{3,11},{4,12},{5,13},{6,14},{7,15},{8,0},{9,1},... | collective-permute-start | bytes 122888 | tf_op jit(solution)/shard_map/ppermute | solution.py:406
  61.4 7.1 %deep.3 = f32[4,8,128,128]{3,2,1,0:T(8,128)} custom-call(f32[4,8,128,128]{3,2,1,0:T(8,128)S(1)} %copy-done, f32[2,8,128,128]{3,2,1,0:T(8,128)S(1)} %copy-done.1, f32[8,128,128]{2,1,0:T(8,128)S(1)} %copy-done.3, s32[128,128]{1,0:T(8,128)S(1)} %copy-done.4, f32[8,32,128]{2,1,0:T(8,128)S(1)} %collective-permute-done.fs, ...), custom_call_target="tpu_custom_call", output_to_operand_aliasing={{}: (10, {})} | custom-call | bytes 18900000 | tf_op jit(solution)/shard_map/deep/pallas_call | solution.py:377
  68.5 0.6 fusion.1
  (28 shorter events, 0.2 us)
Async XLA Ops:
  0.6 9.9 %copy-start.4 = (s32[128,128]{1,0:T(8,128)S(1)}, s32[128,128]{1,0:T(8,128)}, u32[]{:S(2)}) copy-start(s32[128,128]{1,0:T(8,128)} %o.9) | copy-start | bytes 196612
  0.6 9.9 %copy-start.1 = (f32[2,8,128,128]{3,2,1,0:T(8,128)S(1)}, f32[2,8,128,128]{3,2,1,0:T(8,128)}, u32[]{:S(2)}) copy-start(f32[2,8,128,128]{3,2,1,0:T(8,128)} %v.9) | copy-start | bytes 3145732
  0.7 9.9 %copy-start = (f32[4,8,128,128]{3,2,1,0:T(8,128)S(1)}, f32[4,8,128,128]{3,2,1,0:T(8,128)}, u32[]{:S(2)}) copy-start(f32[4,8,128,128]{3,2,1,0:T(8,128)} %t.9) | copy-start | bytes 6291460
  0.7 5.6 %copy-start.5 = (s32[128,1,4]{0,2,1:T(4,128)S(1)}, s32[128,1,4]{0,2,1:T(4,128)}, u32[]{:S(2)}) copy-start(s32[128,1,4]{0,2,1:T(4,128)} %param.11) | copy-start | bytes 6148
  2.6 3.9 %collective-permute-start = (f32[8,32,128]{2,1,0:T(8,128)}, f32[8,32,128]{2,1,0:T(8,128)S(1)}, u32[]{:S(2)}, u32[]{:S(2)}) collective-permute-start(f32[8,32,128]{2,1,0:T(8,128)} %get-tuple-element.30), channel_id=1, source_target_pairs={{0,1},{1,2},{2,3},{4,5},{5,6},{6,7},{8,9},{9,10},{10,11},{12,13},{... | collective-permute-start | bytes 393224 | tf_op jit(solution)/shard_map/ppermute | solution.py:393
  5.0 5.6 %collective-permute-start.1 = (f32[8,32,128]{2,1,0:T(8,128)}, f32[8,32,128]{2,1,0:T(8,128)S(1)}, u32[]{:S(2)}, u32[]{:S(2)}) collective-permute-start(f32[8,32,128]{2,1,0:T(8,128)} %get-tuple-element.31), channel_id=1, source_target_pairs={{1,0},{2,1},{3,2},{5,4},{6,5},{7,6},{9,8},{10,9},{11,10},{13,12},{... | collective-permute-start | bytes 393224 | tf_op jit(solution)/shard_map/ppermute | solution.py:394
  10.5 1.0 %copy-start.2 = (f32[8,128,128]{2,1,0:T(8,128)S(1)}, f32[8,128,128]{2,1,0:T(8,128)}, u32[]{:S(2)}) copy-start(f32[8,128,128]{2,1,0:T(8,128)} %m.9) | copy-start | bytes 1572868
  11.6 5.0 %copy-start.3 = (f32[8,128,128]{2,1,0:T(8,128)S(1)}, f32[8,128,128]{2,1,0:T(8,128)}, u32[]{:S(2)}) copy-start(f32[8,128,128]{2,1,0:T(8,128)} %m.9) | copy-start | bytes 1572868
  11.8 11.5 %collective-permute-start.2 = (f32[1,48,128]{2,1,0:T(8,128)S(1)}, f32[1,48,128]{2,1,0:T(8,128)S(1)}, u32[]{:S(2)}, u32[]{:S(2)}) collective-permute-start(f32[1,48,128]{2,1,0:T(8,128)S(1)} %get-tuple-element.35), channel_id=1, source_target_pairs={{0,4},{4,8},{8,12},{12,16},{16,20},{20,24},{24,28},{28,0},{1,5},{5... | collective-permute-start | bytes 73736 | tf_op jit(solution)/shard_map/ppermute | solution.py:400
  13.4 9.9 %collective-permute-start.3 = (f32[1,48,128]{2,1,0:T(8,128)S(1)}, f32[1,48,128]{2,1,0:T(8,128)S(1)}, u32[]{:S(2)}, u32[]{:S(2)}) collective-permute-start(f32[1,48,128]{2,1,0:T(8,128)S(1)} %get-tuple-element.32), channel_id=1, source_target_pairs={{4,0},{8,4},{12,8},{16,12},{20,16},{24,20},{28,24},{0,28},{5,1},{9... | collective-permute-start | bytes 73736 | tf_op jit(solution)/shard_map/ppermute | solution.py:401
  30.0 8.0 %collective-permute-start.4 = (f32[1280,128]{1,0:T(8,128)S(1)}, f32[1280,128]{1,0:T(8,128)S(1)}, u32[]{:S(2)}, u32[]{:S(2)}) collective-permute-start(f32[1280,128]{1,0:T(8,128)S(1)} %get-tuple-element.43), channel_id=1, source_target_pairs={{0,1},{1,0},{2,3},{3,2},{4,5},{5,4},{6,7},{7,6},{8,9},{9,8},{10,11... | collective-permute-start | bytes 1966088 | tf_op jit(solution)/shard_map/ppermute | solution.py:406
  33.2 11.9 %collective-permute-start.8 = (f32[7,48,128]{2,1,0:T(8,128)S(1)}, f32[7,48,128]{2,1,0:T(8,128)S(1)}, u32[]{:S(2)}, u32[]{:S(2)}) collective-permute-start(f32[7,48,128]{2,1,0:T(8,128)S(1)} %get-tuple-element.47), channel_id=1, source_target_pairs={{0,4},{4,8},{8,12},{12,16},{16,20},{20,24},{24,28},{28,0},{1,5},{5... | collective-permute-start | bytes 516104 | tf_op jit(solution)/shard_map/ppermute | solution.py:400
  33.2 14.4 %collective-permute-start.9 = (f32[7,48,128]{2,1,0:T(8,128)S(1)}, f32[7,48,128]{2,1,0:T(8,128)S(1)}, u32[]{:S(2)}, u32[]{:S(2)}) collective-permute-start(f32[7,48,128]{2,1,0:T(8,128)S(1)} %get-tuple-element.48), channel_id=1, source_target_pairs={{4,0},{8,4},{12,8},{16,12},{20,16},{24,20},{28,24},{0,28},{5,1},{9... | collective-permute-start | bytes 516104 | tf_op jit(solution)/shard_map/ppermute | solution.py:401
  38.1 18.8 %collective-permute-start.7 = (f32[320,128]{1,0:T(8,128)S(1)}, f32[320,128]{1,0:T(8,128)S(1)}, u32[]{:S(2)}, u32[]{:S(2)}) collective-permute-start(f32[320,128]{1,0:T(8,128)S(1)} %get-tuple-element.58), channel_id=1, source_target_pairs={{0,6},{1,7},{2,4},{3,5},{4,2},{5,3},{6,0},{7,1},{8,14},{9,15},{10,... | collective-permute-start | bytes 491528 | tf_op jit(solution)/shard_map/ppermute | solution.py:406
  38.2 18.7 %collective-permute-start.6 = (f32[320,128]{1,0:T(8,128)S(1)}, f32[320,128]{1,0:T(8,128)S(1)}, u32[]{:S(2)}, u32[]{:S(2)}) collective-permute-start(f32[320,128]{1,0:T(8,128)S(1)} %get-tuple-element.59), channel_id=1, source_target_pairs={{0,4},{1,5},{2,6},{3,7},{4,0},{5,1},{6,2},{7,3},{8,12},{9,13},{10,... | collective-permute-start | bytes 491528 | tf_op jit(solution)/shard_map/ppermute | solution.py:406
  39.9 17.0 %collective-permute-start.5 = (f32[320,128]{1,0:T(8,128)S(1)}, f32[320,128]{1,0:T(8,128)S(1)}, u32[]{:S(2)}, u32[]{:S(2)}) collective-permute-start(f32[320,128]{1,0:T(8,128)S(1)} %get-tuple-element.60), channel_id=1, source_target_pairs={{0,2},{1,3},{2,0},{3,1},{4,6},{5,7},{6,4},{7,5},{8,10},{9,11},{10,... | collective-permute-start | bytes 491528 | tf_op jit(solution)/shard_map/ppermute | solution.py:406
  56.9 11.6 %collective-permute-start.12 = (f32[80,128]{1,0:T(8,128)S(1)}, f32[80,128]{1,0:T(8,128)S(1)}, u32[]{:S(2)}, u32[]{:S(2)}) collective-permute-start(f32[80,128]{1,0:T(8,128)S(1)} %get-tuple-element.61), channel_id=1, source_target_pairs={{0,24},{1,25},{2,26},{3,27},{4,28},{5,29},{6,30},{7,31},{8,16},{9,... | collective-permute-start | bytes 122888 | tf_op jit(solution)/shard_map/ppermute | solution.py:406
  58.7 9.8 %collective-permute-start.11 = (f32[80,128]{1,0:T(8,128)S(1)}, f32[80,128]{1,0:T(8,128)S(1)}, u32[]{:S(2)}, u32[]{:S(2)}) collective-permute-start(f32[80,128]{1,0:T(8,128)S(1)} %get-tuple-element.62), channel_id=1, source_target_pairs={{0,16},{1,17},{2,18},{3,19},{4,20},{5,21},{6,22},{7,23},{8,24},{9,... | collective-permute-start | bytes 122888 | tf_op jit(solution)/shard_map/ppermute | solution.py:406
  58.7 9.8 %collective-permute-start.10 = (f32[80,128]{1,0:T(8,128)S(1)}, f32[80,128]{1,0:T(8,128)S(1)}, u32[]{:S(2)}, u32[]{:S(2)}) collective-permute-start(f32[80,128]{1,0:T(8,128)S(1)} %get-tuple-element.63), channel_id=1, source_target_pairs={{0,8},{1,9},{2,10},{3,11},{4,12},{5,13},{6,14},{7,15},{8,0},{9,1},... | collective-permute-start | bytes 122888 | tf_op jit(solution)/shard_map/ppermute | solution.py:406

commit v2 on v1

--- a/solution.py
+++ b/solution.py
@@ -12,7 +12,6 @@
 NTR = 4
 FIELDS = 8
 OFF = 16
-FETCHES = 1
 GROUP = 48
 AXES = ("gx", "gy")
 
@@ -22,6 +21,10 @@
 
 def took(us):
     return pl.CostEstimate(flops=0, bytes_accessed=int(us * 3.5e6), transcendentals=0)
+
+
+def in_hbm(a):
+    return pltpu.with_memory_space_constraint(a, pltpu.HBM)
 
 
 def lane_ids(rows):
@@ -61,7 +64,7 @@
             pl.BlockSpec((8, 128), lambda l: (block, 0)),
         ]
 
-    arrays = [tracers, velocity, mixing, ocean]
+    arrays = [in_hbm(a) for a in (tracers, velocity, mixing, ocean)]
     strip = jax.ShapeDtypeStruct((levels, 32, 128), jnp.float32)
     return pl.pallas_call(
         lat_pack_kernel,
@@ -69,6 +72,7 @@
         in_specs=specs(0) + specs(last),
         out_specs=[WHOLE] * 2,
         out_shape=[strip, strip],
+        compiler_params=pltpu.CompilerParams(vmem_limit_bytes=4 << 20),
         cost_estimate=took(2),
         name="lat_pack",
     )(*arrays, *arrays)
@@ -93,61 +97,61 @@
     return o[...].astype(jnp.float32)
 
 
-def fetch(part, parts, w, out, sem):
-    rows = w.shape[0] // parts
-    return pltpu.make_async_copy(w.at[pl.ds(part * rows, rows)], out, sem)
-
-
-def fetched(w, parts):
-    return pltpu.VMEM((w.shape[0] // parts,) + w.shape[1:], w.dtype)
-
-
-def lon_pack_kernel(first, fetching, t, v, m, o, fs, fn, *refs):
-    if fetching is None:
-        lon_pack_body(first, t, v, m, o, fs, fn, *refs)
-        return
-    w, west_ref, east_ref, out, sem = refs
-    copy = fetch(*fetching, w, out, sem)
+def fetch_kernel(after, w, out, sem):
+    copy = pltpu.make_async_copy(w, out, sem)
     copy.start()
-    lon_pack_body(first, t, v, m, o, fs, fn, west_ref, east_ref)
     copy.wait()
 
 
-def lon_pack_body(first, t, v, m, o, fs, fn, west_ref, east_ref):
+def fetch(weights, after):
+    return pl.pallas_call(
+        fetch_kernel,
+        in_specs=[pl.BlockSpec(memory_space=pl.ANY), pl.BlockSpec(memory_space=pltpu.HBM)],
+        out_specs=WHOLE,
+        out_shape=pltpu.VMEM(weights.shape, weights.dtype),
+        scratch_shapes=[pltpu.SemaphoreType.DMA],
+        compiler_params=pltpu.CompilerParams(vmem_limit_bytes=2 << 20),
+        cost_estimate=took(5),
+        name="fetch",
+    )(after, pltpu.with_memory_space_constraint(weights, pltpu.HBM))
+
+
+def lon_pack_kernel(t, v, m, o_hbm, fs, fn, west_ref, east_ref, o, sem):
+    copy = pltpu.make_async_copy(o_hbm, o, sem)
+    copy.start()
     rows = t.shape[2]
     lane = lane_ids(GROUP)
     groups = (rows + 16) // GROUP
-    for l in range(west_ref.shape[0]):
-        level = first + l
-        west = jnp.zeros((GROUP, 128), jnp.float32)
-        east = jnp.zeros((GROUP, 128), jnp.float32)
+    levels = t.shape[1]
+    for level in [*range(1, levels), 0]:
+        if level == 0:
+            copy.wait()
+        west = east = jnp.zeros((GROUP, 128), jnp.float32)
         for f in range(FIELDS if level == 0 else FIELDS - 1):
             s, n = lat_halo_blocks(fs, fn, f, level)
             whole = jnp.concatenate([s, interior(t, v, m, o, f, level), n], axis=0)
             for g in range(groups):
                 at = 32 * g + 4 * f
-                moved = pltpu.roll(whole[GROUP * g : GROUP * g + GROUP], (at - 124) % 128, 1)
+                part = whole[GROUP * g : GROUP * g + GROUP]
+                moved = pltpu.roll(part, (at - 124) % 128, 1)
                 east = jnp.where((lane >= at) & (lane < at + 4), moved, east)
                 west = jnp.where((lane >= at + 4) & (lane < at + 8), moved, west)
-        west_ref[l] = west
-        east_ref[l] = east
-
-
-def lon_pack(tracers, velocity, mixing, ocean, from_south, from_north, first, levels,
-             fetching=None, weights=None):
-    strip = jax.ShapeDtypeStruct((levels, GROUP, 128), jnp.float32)
-    more = [] if fetching is None else [pl.BlockSpec(memory_space=pltpu.HBM)]
-    out = [] if fetching is None else [fetched(weights, fetching[1])]
+        west_ref[level] = west
+        east_ref[level] = east
+
+
+def lon_pack(tracers, velocity, mixing, ocean, from_south, from_north):
+    strip = jax.ShapeDtypeStruct((tracers.shape[1], GROUP, 128), jnp.float32)
     return pl.pallas_call(
-        functools.partial(lon_pack_kernel, first, fetching),
-        in_specs=[WHOLE] * 6 + more,
-        out_specs=[WHOLE] * (2 + len(out)),
-        out_shape=[strip, strip] + out,
-        scratch_shapes=[pltpu.SemaphoreType.DMA] * len(out),
+        lon_pack_kernel,
+        in_specs=[WHOLE] * 3 + [pl.BlockSpec(memory_space=pltpu.HBM)] + [WHOLE] * 2,
+        out_specs=[WHOLE] * 2,
+        out_shape=[strip, strip],
+        scratch_shapes=[pltpu.VMEM(ocean.shape, ocean.dtype), pltpu.SemaphoreType.DMA],
         compiler_params=pltpu.CompilerParams(vmem_limit_bytes=4 << 20),
-        cost_estimate=took(0.6 * levels),
+        cost_estimate=took(1.2),
         name="lon_pack",
-    )(tracers, velocity, mixing, ocean, from_south, from_north, *([weights] if more else []))
+    )(tracers, velocity, mixing, in_hbm(ocean), from_south, from_north)
 
 
 def unpack_field(ext, f, level, t, v, m, o, fs, fn, even, odd):
@@ -250,8 +254,8 @@
     ]
 
 
-def run_level(rows, level, l, t, v, m, o, fs, fn, fw, fe, vel, north, coef, q):
-    even, odd = strips(fw, fe, l)
+def run_level(rows, level, t, v, m, o, fs, fn, fw, fe, vel, north, coef, q):
+    even, odd = strips(fw, fe, level)
     for i in range(NTR):
         unpack_field(q.at[0, i], i, level, t, v, m, o, fs, fn, even, odd)
     for i in range(3):
@@ -266,17 +270,12 @@
 
 
 def surface_kernel(
-    order, accs, slot, t, v, m, o, fs, fn, fw, fe, *refs):
-    surface_body(order, accs, slot, t, v, m, o, fs, fn, fw, fe, refs[:FETCHES], *refs[FETCHES:])
-
-
-def surface_body(
-    order, accs, slot, t, v, m, o, fs, fn, fw, fe, ws, out_q, out_send, out_keep,
+    order, accs, slot, t, v, m, o, fs, fn, fw, fe, w, out_q, out_send, out_keep,
     vel, north, coef, q, surf, *sums,
 ):
     rows = t.shape[2]
     unpack_ocean(t, v, m, o, fs, fn, fw, fe, vel)
-    run_level(rows, 0, 0, t, v, m, o, fs, fn, fw, fe, vel, north, coef, q)
+    run_level(rows, 0, t, v, m, o, fs, fn, fw, fe, vel, north, coef, q)
     ocean = o[...].astype(jnp.float32)
     for i in range(NTR):
         done = q[0, i, 0, OFF : OFF + rows]
@@ -288,12 +287,10 @@
     for d in sums:
         d[...] = jnp.zeros_like(d)
     first = sub_ids(16) < 8
-    kb = ws[0].shape[1]
-    per = rows // FETCHES // 2
-
-    def body(w, base, i, carry):
-        j = i + base
-        s = surf[pl.ds(pl.multiple_of(16 * j, 16), 16), :]
+    kb = w.shape[1]
+
+    def body(i, carry):
+        s = surf[pl.ds(pl.multiple_of(16 * i, 16), 16), :]
         lhs = jnp.concatenate(
             [jnp.where(first, s, 0.0), jnp.where(first, 0.0, s)], axis=1
         ).astype(jnp.bfloat16)
@@ -310,13 +307,12 @@
                 for kk in range(2):
                     d = sums[(k + kk) % accs]
                     at = pl.ds(
-                        pl.multiple_of(8 * slot[(2 * j + r) * kb + k + kk], 8), 8
+                        pl.multiple_of(8 * slot[k + kk, 2 * i + r], 8), 8
                     )
                     d[at, :] += part[8 * r : 8 * r + 8, 128 * kk : 128 * kk + 128]
         return carry
 
-    for n, w in enumerate(ws):
-        lax.fori_loop(0, per, functools.partial(body, w, n * per), 0, unroll=16)
+    lax.fori_loop(0, rows // 2, body, 0, unroll=16)
     chunk = ABD * (NTR + 1)
     half = len(order) // 2
     for place, owner in enumerate(order):
@@ -336,7 +332,7 @@
     half = owners // 2 * ABD * (NTR + 1)
     return pl.pallas_call(
         functools.partial(surface_kernel, order, accs),
-        in_specs=[pl.BlockSpec(memory_space=pltpu.SMEM)] + [WHOLE] * (8 + FETCHES),
+        in_specs=[pl.BlockSpec(memory_space=pltpu.SMEM)] + [WHOLE] * 9,
         out_specs=[WHOLE] * 3,
         scratch_shapes=field_scratch(rows)
         + [pltpu.VMEM((rows * 8, 128), jnp.float32)]
@@ -349,16 +345,16 @@
         compiler_params=pltpu.CompilerParams(vmem_limit_bytes=22 << 20),
         cost_estimate=took(7),
         name="surface",
-    )(slot, tracers, velocity, mixing, ocean, *halo, *weights)
-
-
-def deep_kernel(first, t, v, m, o, fs, fn, fw, fe, ofw, ofe, base, out, vel, north, coef, q):
+    )(slot, tracers, velocity, mixing, ocean, *halo, weights)
+
+
+def deep_kernel(first, t, v, m, o, fs, fn, fw, fe, base, out, vel, north, coef, q):
     rows = t.shape[2]
     level = pl.program_id(0) + first
 
     @pl.when(pl.program_id(0) == 0)
     def _():
-        unpack_ocean(t, v, m, o, fs, fn, ofw, ofe, vel)
+        unpack_ocean(t, v, m, o, fs, fn, fw, fe, vel)
 
     if first == 0:
         @pl.when(level == 0)
@@ -367,25 +363,25 @@
 
     @pl.when(level > 0)
     def _():
-        run_level(rows, level, level - 1, t, v, m, o, fs, fn, fw, fe, vel, north, coef, q)
+        run_level(rows, level, t, v, m, o, fs, fn, fw, fe, vel, north, coef, q)
         for i in range(NTR):
             out[i, 0] = q[0, i, 0, OFF : OFF + rows]
 
 
-def deep(tracers, velocity, mixing, ocean, halo, ocean_halo, base, first, levels):
+def deep(tracers, velocity, mixing, ocean, halo, base, first, levels):
     rows = tracers.shape[2]
     return pl.pallas_call(
         functools.partial(deep_kernel, first),
         grid=(levels,),
-        in_specs=[WHOLE] * 10 + [pl.BlockSpec(memory_space=pl.ANY) if first else WHOLE],
+        in_specs=[WHOLE] * 8 + [pl.BlockSpec(memory_space=pl.ANY) if first else WHOLE],
         out_specs=pl.BlockSpec((NTR, 1, rows, 128), lambda l: (0, l + first, 0, 0)),
         out_shape=jax.ShapeDtypeStruct(tracers.shape, jnp.float32),
         scratch_shapes=field_scratch(rows),
-        input_output_aliases={10: 0} if first else {},
+        input_output_aliases={8: 0} if first else {},
         compiler_params=pltpu.CompilerParams(vmem_limit_bytes=16 << 20),
         cost_estimate=took(1.8 * levels),
         name="deep",
-    )(tracers, velocity, mixing, ocean, *halo, *ocean_halo, base)
+    )(tracers, velocity, mixing, ocean, *halo, base)
 
 
 def exchange_lat(to_south, to_north):
@@ -423,29 +419,25 @@
 
 
 def per_device(tracers, velocity, mixing, land_mask, remap_weights, remap_dest):
-    remap_weights = pltpu.with_memory_space_constraint(remap_weights, pltpu.HBM)
     owners = lax.axis_size("gx") * lax.axis_size("gy")
     levels = tracers.shape[1]
     me = lax.axis_index("gx") * lax.axis_size("gy") + lax.axis_index("gy")
-    dest = remap_dest.reshape(-1)
+    dest = remap_dest[:, 0].T
     slot = jnp.bitwise_xor(dest // ABD, me) * ABD + dest % ABD
 
     tile = (tracers, velocity, mixing, land_mask)
     lat = exchange_lat(*lat_pack(*tile))
-    to_west, to_east = lon_pack(*tile, *lat, 0, 1)
-    lon0 = exchange_lon(to_west, to_east)
-    lat, to_west = lax.optimization_barrier((lat, to_west))
-    packed = lon_pack(*tile, *lat, 1, levels - 1, (0, FETCHES), remap_weights)
-    lon0, packed = lax.optimization_barrier((lon0, packed))
-    lon1 = exchange_lon(*packed[:2])
+    lat, slot = lax.optimization_barrier((lat, slot))
+    to_west, to_east = lon_pack(*tile, *lat)
+    lon = exchange_lon(to_west, to_east)
+    weights = fetch(remap_weights, to_west)
+    lon, weights = lax.optimization_barrier((lon, weights))
 
     order = order_of(owners)
-    done, send, keep = surface(order, slot, *tile, lat + lon0,
-        [pltpu.with_memory_space_constraint(w, pltpu.VMEM) for w in packed[2:]],
-    )
-    got = partner(send, 1, owners)
-    total = keep + got
-    lat, total = lax.optimization_barrier((lat, total))
+    weights = pltpu.with_memory_space_constraint(weights, pltpu.VMEM)
+    done, send, keep = surface(order, slot, *tile, lat + lon, weights)
+    total = keep + partner(send, 1, owners)
+    lon, total = lax.optimization_barrier((lon, total))
     values = done
     rounds = rounds_of(owners)[1:]
     cut = [0] + [levels * (i + 1) // len(rounds) for i in range(len(rounds))]
@@ -453,7 +445,7 @@
     for i, (at, width) in enumerate(rounds):
         parts = total.reshape((1 << width, -1, 128))
         got = [partner(parts[j], j << at, owners) for j in range(1, 1 << width)]
-        values = deep(*tile, lat + lon1, lon0, values, cut[i], cut[i + 1] - cut[i])
+        values = deep(*tile, lat + lon, values, cut[i], cut[i + 1] - cut[i])
         got, values = lax.optimization_barrier((got, values))
         total = parts[0]
         for g in got:

time: 69.4 us -> 61 us (0.88)
  starting transfers between devices: 24.4 us -> 18.1 us
  waiting for transfers between devices: 10.1 us -> 7.39 us
  Pallas kernels: 31.8 us -> 32.7 us
    ppermute x2 -> x1, starting transfers between devices: 7.92 us -> 3.2 us  [exchange_lon(): lax.ppermute(to_west, 'gx', [((i + 1) % n, i) for i in range(n)])]
    ppermute x2 -> x1, waiting for transfers between devices: 3.52 us -> 0.01 us  [exchange_lon(): lax.ppermute(to_east, 'gx', [(i, (i + 1) % n) for i in range(n)])]
    ppermute x7, waiting for transfers between devices: 0.02 us -> 1.74 us  [partner(): return lax.ppermute(a, AXES, [(i, i ^ mask) for i in range(n)])]
    ppermute x7, starting transfers between devices: 11.2 us -> 9.64 us  [partner(): return lax.ppermute(a, AXES, [(i, i ^ mask) for i in range(n)])]
    pallas_call x2, Pallas kernels: 6.86 us -> 7.77 us  [the longest x1 5.78 us: fetch(): pl.pallas_call(fetch_kernel, in_specs=[pl.BlockSpec(memory_space=pl.ANY),...]
    ppermute x2 -> x1, waiting for transfers between devices: 2.52 us -> 1.65 us  [exchange_lon(): lax.ppermute(to_west, 'gx', [((i + 1) % n, i) for i in range(n)])]
    ppermute x2 -> x1, starting transfers between devices: 1.57 us -> 1.57 us  [exchange_lon(): lax.ppermute(to_east, 'gx', [(i, (i + 1) % n) for i in range(n)])]
  transfers between devices with their start and end apart: 13 -> 11, of which waited for: 3 -> 3; matrix products, arithmetic and copies ran while one was open for 0% -> 0% of each run, Pallas kernels for 33% -> 36%
where the time goes in v2:
time: 61 us; the launch traced here: 60.8 us
  Pallas kernels  32.7 us (54%)
  starting transfers between devices  18.1 us (30%)
  waiting for transfers between devices  7.39 us (12%)
  local copies, waits for them, and re-layouts  1.11 us (2%)
  between operations  0.78 us (1%)
  other arithmetic  0.75 us (1%)
    pallas_call x2, Pallas kernels, deep(): pl.pallas_call(functools.partial(deep_kernel, first), grid=(levels,), in_...  16.3 us
    ppermute x7, starting transfers between devices, partner(): return lax.ppermute(a, AXES, [(i, i ^ mask) for i in range(n)])  9.64 us
    pallas_call x1, Pallas kernels, surface(): pl.pallas_call(functools.partial(surface_kernel, order, accs), in_specs=[...  6.7 us
    pallas_call x1, Pallas kernels, fetch(): pl.pallas_call(fetch_kernel, in_specs=[pl.BlockSpec(memory_space=pl.ANY),...  5.78 us
    ppermute x1, waiting for transfers between devices, exchange_lat(): lax.ppermute(to_south, 'gy', [(i + 1, i) for i in range(n - 1)])  4 us
    ppermute x1, starting transfers between devices, exchange_lon(): lax.ppermute(to_west, 'gx', [((i + 1) % n, i) for i in range(n)])  3.2 us
    ppermute x1, starting transfers between devices, exchange_lat(): lax.ppermute(to_north, 'gy', [(i, i + 1) for i in range(n - 1)])  2.35 us
    pallas_call x1, Pallas kernels, lon_pack(): pl.pallas_call(lon_pack_kernel, in_specs=[WHOLE] * 3 + [pl.BlockSpec(memo...  1.99 us
  transfers between devices with their start and end apart: 11, of which 3 were waited for; matrix products, arithmetic and copies ran while one was open for 0% of the time, Pallas kernels for 36%

profile of v2, /device:TPU:0, one launch (start us, length us, event | category | flops | bytes accessed | tf_op | source)
XLA Modules:
  0.0 60.8 jit_solution(17086524000654725027)
XLA Ops:
  0.7 1.9 %lat_pack.1 = (f32[8,32,128]{2,1,0:T(8,128)S(1)}, f32[8,32,128]{2,1,0:T(8,128)}) custom-call(f32[4,8,128,128]{3,2,1,0:T(8,128)} %t.7, f32[2,8,128,128]{3,2,1,0:T(8,128)} %v.7, f32[8,128,128]{2,1,0:T(8,128)} %m.7, s32[128,128]{1,0:T(8,128)} %o.5, f32[4,8,128,128]{3,2,1,0:T(8,128)} %t.7, f32[2,8,128,128]{3,2,1,0:T(8,128)} %v.7, f32[8,128,128]{2,1,0:T(8,128)} %m.7, ...), custom_call_target="tpu_custom_call" | custom-call | bytes 7000000 | tf_op jit(solution)/shard_map/lat_pack/pallas_call | solution.py:69
  2.6 2.4 %collective-permute-start = (f32[8,32,128]{2,1,0:T(8,128)}, f32[8,32,128]{2,1,0:T(8,128)S(1)}, u32[]{:S(2)}, u32[]{:S(2)}) collective-permute-start(f32[8,32,128]{2,1,0:T(8,128)} %get-tuple-element.26), channel_id=1, source_target_pairs={{0,1},{1,2},{2,3},{4,5},{5,6},{6,7},{8,9},{9,10},{10,11},{12,13},{... | collective-permute-start | bytes 393224 | tf_op jit(solution)/shard_map/ppermute | solution.py:389
  4.9 1.3 %collective-permute-start.1 = (f32[8,32,128]{2,1,0:T(8,128)S(1)}, f32[8,32,128]{2,1,0:T(8,128)S(1)}, u32[]{:S(2)}, u32[]{:S(2)}) collective-permute-start(f32[8,32,128]{2,1,0:T(8,128)S(1)} %get-tuple-element.27), channel_id=1, source_target_pairs={{1,0},{2,1},{3,2},{5,4},{6,5},{7,6},{9,8},{10,9},{11,10},{13,12},{... | collective-permute-start | bytes 393224 | tf_op jit(solution)/shard_map/ppermute | solution.py:390
  6.3 0.0 collective-permute-done.fs
  6.3 4.0 %collective-permute-done.1.fn = f32[8,32,128]{2,1,0:T(8,128)S(1)} collective-permute-done((f32[8,32,128]{2,1,0:T(8,128)S(1)}, f32[8,32,128]{2,1,0:T(8,128)S(1)}, u32[]{:S(2)}, u32[]{:S(2)}) %collective-permute-start.1) | collective-permute-done | bytes 131104 | tf_op jit(solution)/shard_map/ppermute | solution.py:390
  10.3 1.0 %copy-done.2 = f32[8,128,128]{2,1,0:T(8,128)S(1)} copy-done((f32[8,128,128]{2,1,0:T(8,128)S(1)}, f32[8,128,128]{2,1,0:T(8,128)}, u32[]{:S(2)}) %copy-start.2) | copy-done | bytes 524312
  11.3 2.0 %lon_pack.1 = (f32[8,48,128]{2,1,0:T(8,128)S(1)}, f32[8,48,128]{2,1,0:T(8,128)S(1)}) custom-call(f32[4,8,128,128]{3,2,1,0:T(8,128)S(1)} %copy-done, f32[2,8,128,128]{3,2,1,0:T(8,128)S(1)} %copy-done.1, f32[8,128,128]{2,1,0:T(8,128)S(1)} %copy-done.2, s32[128,128]{1,0:T(8,128)} %o.5, f32[8,32,128]{2,1,0:T(8,128)S(1)} %collective-permute-done.fs, ...), custom_call_target="tpu_custom_call" | custom-call | bytes 4200000 | tf_op jit(solution)/shard_map/lon_pack/pallas_call | solution.py:145
  13.3 1.6 %collective-permute-start.2 = (f32[8,48,128]{2,1,0:T(8,128)S(1)}, f32[8,48,128]{2,1,0:T(8,128)S(1)}, u32[]{:S(2)}, u32[]{:S(2)}) collective-permute-start(f32[8,48,128]{2,1,0:T(8,128)S(1)} %get-tuple-element.30), channel_id=1, source_target_pairs={{0,4},{4,8},{8,12},{12,16},{16,20},{20,24},{24,28},{28,0},{1,5},{5... | collective-permute-start | bytes 589832 | tf_op jit(solution)/shard_map/ppermute | solution.py:396
  14.9 3.2 %collective-permute-start.3 = (f32[8,48,128]{2,1,0:T(8,128)S(1)}, f32[8,48,128]{2,1,0:T(8,128)S(1)}, u32[]{:S(2)}, u32[]{:S(2)}) collective-permute-start(f32[8,48,128]{2,1,0:T(8,128)S(1)} %get-tuple-element.31.after), channel_id=1, source_target_pairs={{4,0},{8,4},{12,8},{16,12},{20,16},{24,20},{28,24},{0,28},{5,1},{9... | collective-permute-start | bytes 589832 | tf_op jit(solution)/shard_map/ppermute | solution.py:397
  18.1 5.8 %fetch.1.w = bf16[128,4,128,128]{3,2,1,0:T(8,128)(2,1)S(1)} custom-call(f32[8,48,128]{2,1,0:T(8,128)S(1)} %get-tuple-element.31.after, bf16[128,4,128,128]{3,2,1,0:T(8,128)(2,1)} %w.1), custom_call_target="tpu_custom_call" | custom-call | bytes 17500000 | tf_op jit(solution)/shard_map/fetch/pallas_call | solution.py:107
  23.9 0.0 collective-permute-done.2.fw
  23.9 1.7 %collective-permute-done.3.fe = f32[8,48,128]{2,1,0:T(8,128)S(1)} collective-permute-done((f32[8,48,128]{2,1,0:T(8,128)S(1)}, f32[8,48,128]{2,1,0:T(8,128)S(1)}, u32[]{:S(2)}, u32[]{:S(2)}) %collective-permute-start.3) | collective-permute-done | bytes 196640 | tf_op jit(solution)/shard_map/ppermute | solution.py:397
  25.5 6.7 %surface.1 = (f32[4,128,128]{2,1,0:T(8,128)S(1)}, f32[1280,128]{1,0:T(8,128)S(1)}, f32[1280,128]{1,0:T(8,128)S(1)}) custom-call(s32[4,128]{1,0:T(4,128)S(1)} %fusion.4.slot, f32[4,8,128,128]{3,2,1,0:T(8,128)S(1)} %copy-done, f32[2,8,128,128]{3,2,1,0:T(8,128)S(1)} %copy-done.1, f32[8,128,128]{2,1,0:T(8,128)S(1)} %copy-done.3, s32[128,128]{1,0:T(8,128)S(1)} %copy-done.4, ...), custom_call_target="tpu_custom_call" | custom-call | bytes 24500000 | tf_op jit(solution)/shard_map/surface/pallas_call | solution.py:333
  32.3 1.6 %collective-permute-start.4 = (f32[1280,128]{1,0:T(8,128)S(1)}, f32[1280,128]{1,0:T(8,128)S(1)}, u32[]{:S(2)}, u32[]{:S(2)}) collective-permute-start(f32[1280,128]{1,0:T(8,128)S(1)} %get-tuple-element.37), channel_id=1, source_target_pairs={{0,1},{1,0},{2,3},{3,2},{4,5},{5,4},{6,7},{7,6},{8,9},{9,8},{10,11... | collective-permute-start | bytes 1966088 | tf_op jit(solution)/shard_map/ppermute | solution.py:402
  33.9 1.7 %collective-permute-done.4 = f32[1280,128]{1,0:T(8,128)S(1)} collective-permute-done((f32[1280,128]{1,0:T(8,128)S(1)}, f32[1280,128]{1,0:T(8,128)S(1)}, u32[]{:S(2)}, u32[]{:S(2)}) %collective-permute-start.4) | collective-permute-done | bytes 655392 | tf_op jit(solution)/shard_map/ppermute | solution.py:402
  35.6 0.1 add.37
  35.7 0.1 collective-permute-start.7
  35.8 1.9 %collective-permute-start.6 = (f32[320,128]{1,0:T(8,128)S(1)}, f32[320,128]{1,0:T(8,128)S(1)}, u32[]{:S(2)}, u32[]{:S(2)}) collective-permute-start(f32[320,128]{1,0:T(8,128)S(1)} %get-tuple-element.51), channel_id=1, source_target_pairs={{0,4},{1,5},{2,6},{3,7},{4,0},{5,1},{6,2},{7,3},{8,12},{9,13},{10,... | collective-permute-start | bytes 491528 | tf_op jit(solution)/shard_map/ppermute | solution.py:402
  37.7 1.6 %collective-permute-start.5 = (f32[320,128]{1,0:T(8,128)S(1)}, f32[320,128]{1,0:T(8,128)S(1)}, u32[]{:S(2)}, u32[]{:S(2)}) collective-permute-start(f32[320,128]{1,0:T(8,128)S(1)} %get-tuple-element.52), channel_id=1, source_target_pairs={{0,2},{1,3},{2,0},{3,1},{4,6},{5,7},{6,4},{7,5},{8,10},{9,11},{10,... | collective-permute-start | bytes 491528 | tf_op jit(solution)/shard_map/ppermute | solution.py:402
  39.3 9.2 %deep.2.base = f32[4,8,128,128]{3,2,1,0:T(8,128)} custom-call(f32[4,8,128,128]{3,2,1,0:T(8,128)S(1)} %copy-done, f32[2,8,128,128]{3,2,1,0:T(8,128)S(1)} %copy-done.1, f32[8,128,128]{2,1,0:T(8,128)S(1)} %copy-done.3, s32[128,128]{1,0:T(8,128)S(1)} %copy-done.4, f32[8,32,128]{2,1,0:T(8,128)S(1)} %collective-permute-done.fs, ...), custom_call_target="tpu_custom_call" | custom-call | bytes 31500000 | tf_op jit(solution)/shard_map/deep/pallas_call | solution.py:373
  48.6 2.6 %collective-permute-start.10 = (f32[80,128]{1,0:T(8,128)S(1)}, f32[80,128]{1,0:T(8,128)S(1)}, u32[]{:S(2)}, u32[]{:S(2)}) collective-permute-start(f32[80,128]{1,0:T(8,128)S(1)} %get-tuple-element.53), channel_id=1, source_target_pairs={{0,24},{1,25},{2,26},{3,27},{4,28},{5,29},{6,30},{7,31},{8,16},{9,... | collective-permute-start | bytes 122888 | tf_op jit(solution)/shard_map/ppermute | solution.py:402
  51.2 1.8 %collective-permute-start.8 = (f32[80,128]{1,0:T(8,128)S(1)}, f32[80,128]{1,0:T(8,128)S(1)}, u32[]{:S(2)}, u32[]{:S(2)}) collective-permute-start(f32[80,128]{1,0:T(8,128)S(1)} %get-tuple-element.55), channel_id=1, source_target_pairs={{0,8},{1,9},{2,10},{3,11},{4,12},{5,13},{6,14},{7,15},{8,0},{9,1},... | collective-permute-start | bytes 122888 | tf_op jit(solution)/shard_map/ppermute | solution.py:402
  53.0 7.1 %deep.3 = f32[4,8,128,128]{3,2,1,0:T(8,128)} custom-call(f32[4,8,128,128]{3,2,1,0:T(8,128)S(1)} %copy-done, f32[2,8,128,128]{3,2,1,0:T(8,128)S(1)} %copy-done.1, f32[8,128,128]{2,1,0:T(8,128)S(1)} %copy-done.3, s32[128,128]{1,0:T(8,128)S(1)} %copy-done.4, f32[8,32,128]{2,1,0:T(8,128)S(1)} %collective-permute-done.fs, ...), custom_call_target="tpu_custom_call", output_to_operand_aliasing={{}: (8, {})} | custom-call | bytes 18900000 | tf_op jit(solution)/shard_map/deep/pallas_call | solution.py:373
  60.1 0.6 %fusion.1 = f32[80,128]{1,0:T(8,128)} fusion(f32[80,128]{1,0:T(8,128)S(1)} %collective-permute-done.10, f32[80,128]{1,0:T(8,128)S(1)} %collective-permute-done.9, f32[80,128]{1,0:T(8,128)S(1)} %collective-permute-done.8, f32[320,128]{1,0:T(8,128)S(1)} %add_add_fusion), kind=kLoop, calls=%fused_computation.3 | loop fusion | flops 30720 | bytes 204800 | tf_op jit(solution)/shard_map/add | solution.py:452
  (22 shorter events, 0.1 us)
Async XLA Ops:
  0.6 9.6 %copy-start.1 = (f32[2,8,128,128]{3,2,1,0:T(8,128)S(1)}, f32[2,8,128,128]{3,2,1,0:T(8,128)}, u32[]{:S(2)}) copy-start(f32[2,8,128,128]{3,2,1,0:T(8,128)} %v.7) | copy-start | bytes 3145732
  0.6 9.6 %copy-start = (f32[4,8,128,128]{3,2,1,0:T(8,128)S(1)}, f32[4,8,128,128]{3,2,1,0:T(8,128)}, u32[]{:S(2)}) copy-start(f32[4,8,128,128]{3,2,1,0:T(8,128)} %t.7) | copy-start | bytes 6291460
  0.7 5.6 %copy-start.5 = (s32[128,1,4]{0,2,1:T(4,128)S(1)}, s32[128,1,4]{0,2,1:T(4,128)}, u32[]{:S(2)}) copy-start(s32[128,1,4]{0,2,1:T(4,128)} %param.11) | copy-start | bytes 6148
  2.6 3.7 %collective-permute-start = (f32[8,32,128]{2,1,0:T(8,128)}, f32[8,32,128]{2,1,0:T(8,128)S(1)}, u32[]{:S(2)}, u32[]{:S(2)}) collective-permute-start(f32[8,32,128]{2,1,0:T(8,128)} %get-tuple-element.26), channel_id=1, source_target_pairs={{0,1},{1,2},{2,3},{4,5},{5,6},{6,7},{8,9},{9,10},{10,11},{12,13},{... | collective-permute-start | bytes 393224 | tf_op jit(solution)/shard_map/ppermute | solution.py:389
  4.9 5.3 %collective-permute-start.1 = (f32[8,32,128]{2,1,0:T(8,128)S(1)}, f32[8,32,128]{2,1,0:T(8,128)S(1)}, u32[]{:S(2)}, u32[]{:S(2)}) collective-permute-start(f32[8,32,128]{2,1,0:T(8,128)S(1)} %get-tuple-element.27), channel_id=1, source_target_pairs={{1,0},{2,1},{3,2},{5,4},{6,5},{7,6},{9,8},{10,9},{11,10},{13,12},{... | collective-permute-start | bytes 393224 | tf_op jit(solution)/shard_map/ppermute | solution.py:390
  10.3 1.0 %copy-start.2 = (f32[8,128,128]{2,1,0:T(8,128)S(1)}, f32[8,128,128]{2,1,0:T(8,128)}, u32[]{:S(2)}) copy-start(f32[8,128,128]{2,1,0:T(8,128)} %m.7) | copy-start | bytes 1572868
  13.3 10.6 %collective-permute-start.2 = (f32[8,48,128]{2,1,0:T(8,128)S(1)}, f32[8,48,128]{2,1,0:T(8,128)S(1)}, u32[]{:S(2)}, u32[]{:S(2)}) collective-permute-start(f32[8,48,128]{2,1,0:T(8,128)S(1)} %get-tuple-element.30), channel_id=1, source_target_pairs={{0,4},{4,8},{8,12},{12,16},{16,20},{20,24},{24,28},{28,0},{1,5},{5... | collective-permute-start | bytes 589832 | tf_op jit(solution)/shard_map/ppermute | solution.py:396
  14.9 10.7 %copy-start.3 = (f32[8,128,128]{2,1,0:T(8,128)S(1)}, f32[8,128,128]{2,1,0:T(8,128)}, u32[]{:S(2)}) copy-start(f32[8,128,128]{2,1,0:T(8,128)} %m.7) | copy-start | bytes 1572868
  14.9 10.7 %copy-start.4 = (s32[128,128]{1,0:T(8,128)S(1)}, s32[128,128]{1,0:T(8,128)}, u32[]{:S(2)}) copy-start(s32[128,128]{1,0:T(8,128)} %o.5) | copy-start | bytes 196612
  14.9 10.7 %collective-permute-start.3 = (f32[8,48,128]{2,1,0:T(8,128)S(1)}, f32[8,48,128]{2,1,0:T(8,128)S(1)}, u32[]{:S(2)}, u32[]{:S(2)}) collective-permute-start(f32[8,48,128]{2,1,0:T(8,128)S(1)} %get-tuple-element.31.after), channel_id=1, source_target_pairs={{4,0},{8,4},{12,8},{16,12},{20,16},{24,20},{28,24},{0,28},{5,1},{9... | collective-permute-start | bytes 589832 | tf_op jit(solution)/shard_map/ppermute | solution.py:397
  32.3 3.3 %collective-permute-start.4 = (f32[1280,128]{1,0:T(8,128)S(1)}, f32[1280,128]{1,0:T(8,128)S(1)}, u32[]{:S(2)}, u32[]{:S(2)}) collective-permute-start(f32[1280,128]{1,0:T(8,128)S(1)} %get-tuple-element.37), channel_id=1, source_target_pairs={{0,1},{1,0},{2,3},{3,2},{4,5},{5,4},{6,7},{7,6},{8,9},{9,8},{10,11... | collective-permute-start | bytes 1966088 | tf_op jit(solution)/shard_map/ppermute | solution.py:402
  35.7 12.8 %collective-permute-start.7 = (f32[320,128]{1,0:T(8,128)S(1)}, f32[320,128]{1,0:T(8,128)S(1)}, u32[]{:S(2)}, u32[]{:S(2)}) collective-permute-start(f32[320,128]{1,0:T(8,128)S(1)} %get-tuple-element.50), channel_id=1, source_target_pairs={{0,6},{1,7},{2,4},{3,5},{4,2},{5,3},{6,0},{7,1},{8,14},{9,15},{10,... | collective-permute-start | bytes 491528 | tf_op jit(solution)/shard_map/ppermute | solution.py:402
  35.8 12.7 %collective-permute-start.6 = (f32[320,128]{1,0:T(8,128)S(1)}, f32[320,128]{1,0:T(8,128)S(1)}, u32[]{:S(2)}, u32[]{:S(2)}) collective-permute-start(f32[320,128]{1,0:T(8,128)S(1)} %get-tuple-element.51), channel_id=1, source_target_pairs={{0,4},{1,5},{2,6},{3,7},{4,0},{5,1},{6,2},{7,3},{8,12},{9,13},{10,... | collective-permute-start | bytes 491528 | tf_op jit(solution)/shard_map/ppermute | solution.py:402
  37.7 10.8 %collective-permute-start.5 = (f32[320,128]{1,0:T(8,128)S(1)}, f32[320,128]{1,0:T(8,128)S(1)}, u32[]{:S(2)}, u32[]{:S(2)}) collective-permute-start(f32[320,128]{1,0:T(8,128)S(1)} %get-tuple-element.52), channel_id=1, source_target_pairs={{0,2},{1,3},{2,0},{3,1},{4,6},{5,7},{6,4},{7,5},{8,10},{9,11},{10,... | collective-permute-start | bytes 491528 | tf_op jit(solution)/shard_map/ppermute | solution.py:402
  48.6 11.6 %collective-permute-start.10 = (f32[80,128]{1,0:T(8,128)S(1)}, f32[80,128]{1,0:T(8,128)S(1)}, u32[]{:S(2)}, u32[]{:S(2)}) collective-permute-start(f32[80,128]{1,0:T(8,128)S(1)} %get-tuple-element.53), channel_id=1, source_target_pairs={{0,24},{1,25},{2,26},{3,27},{4,28},{5,29},{6,30},{7,31},{8,16},{9,... | collective-permute-start | bytes 122888 | tf_op jit(solution)/shard_map/ppermute | solution.py:402
  51.2 8.9 %collective-permute-start.9 = (f32[80,128]{1,0:T(8,128)S(1)}, f32[80,128]{1,0:T(8,128)S(1)}, u32[]{:S(2)}, u32[]{:S(2)}) collective-permute-start(f32[80,128]{1,0:T(8,128)S(1)} %get-tuple-element.54), channel_id=1, source_target_pairs={{0,16},{1,17},{2,18},{3,19},{4,20},{5,21},{6,22},{7,23},{8,24},{9,... | collective-permute-start | bytes 122888 | tf_op jit(solution)/shard_map/ppermute | solution.py:402
  51.2 8.9 %collective-permute-start.8 = (f32[80,128]{1,0:T(8,128)S(1)}, f32[80,128]{1,0:T(8,128)S(1)}, u32[]{:S(2)}, u32[]{:S(2)}) collective-permute-start(f32[80,128]{1,0:T(8,128)S(1)} %get-tuple-element.55), channel_id=1, source_target_pairs={{0,8},{1,9},{2,10},{3,11},{4,12},{5,13},{6,14},{7,15},{8,0},{9,1},... | collective-permute-start | bytes 122888 | tf_op jit(solution)/shard_map/ppermute | solution.py:402

commit v3 on v2

v3 whole, which is shorter than its diff:
```python
import functools

import jax
import jax.numpy as jnp
from jax import lax
from jax.experimental import pallas as pl
from jax.experimental.pallas import tpu as pltpu
from jax.sharding import PartitionSpec as P

STEPS = 4
ABD = 16
NTR = 4
FIELDS = 8
OFF = 16
FIRST, SECOND = 3, 3
COUNT = 2
UNIT = 16
AXES = ("gx", "gy")


WHOLE = pl.BlockSpec(memory_space=pltpu.VMEM)
SCALARS = pl.BlockSpec(memory_space=pltpu.SMEM)


def took(us):
    return pl.CostEstimate(flops=0, bytes_accessed=int(us * 3.5e6), transcendentals=0)


def in_hbm(a):
    return pltpu.with_memory_space_constraint(a, pltpu.HBM)


def in_vmem(a):
    return pltpu.with_memory_space_constraint(a, pltpu.VMEM)


def lane_ids(rows):
    return lax.broadcasted_iota(jnp.int32, (rows, 128), 1)


def sub_ids(rows):
    return lax.broadcasted_iota(jnp.int32, (rows, 128), 0)


def parity(axis):
    return lax.axis_index(axis) & 1


def pick(odd, a, b):
    return jnp.where(odd == 0, a, b), jnp.where(odd == 0, b, a)


def lat_pack_kernel(tl, vl, ml, ol, th, vh, mh, oh, first_ref, second_ref):
    top = sub_ids(8) < 4
    for level in range(tl.shape[1]):

        def fields(t, v, m, o):
            out = [t[i, level] for i in range(NTR)] + [v[0, level], v[1, level], m[level]]
            out.append(o[...].astype(jnp.float32) if level == 0 else m[level])
            return out

        low, high = fields(tl, vl, ml, ol), fields(th, vh, mh, oh)
        for p in range(FIELDS // 2):
            here = slice(8 * p, 8 * p + 8)
            a, b = low[2 * p], low[2 * p + 1]
            south = jnp.where(top, a, pltpu.roll(b, 4, 0))
            a, b = high[2 * p], high[2 * p + 1]
            north = jnp.where(top, pltpu.roll(a, 4, 0), b)
            first_ref[level, here], second_ref[level, here] = pick(parity("gy"), north, south)


def lat_pack(tracers, velocity, mixing, ocean):
    levels, rows = tracers.shape[1:3]
    last = rows // 8 - 1

    def specs(block):
        return [
            pl.BlockSpec((NTR, levels, 8, 128), lambda l: (0, 0, block, 0)),
            pl.BlockSpec((2, levels, 8, 128), lambda l: (0, 0, block, 0)),
            pl.BlockSpec((levels, 8, 128), lambda l: (0, block, 0)),
            pl.BlockSpec((8, 128), lambda l: (block, 0)),
        ]

    arrays = [in_hbm(a) for a in (tracers, velocity, mixing, ocean)]
    strip = jax.ShapeDtypeStruct((levels, 32, 128), jnp.float32)
    return pl.pallas_call(
        lat_pack_kernel,
        grid=(1,),
        in_specs=specs(0) + specs(last),
        out_specs=[WHOLE] * 2,
        out_shape=[strip, strip],
        compiler_params=pltpu.CompilerParams(vmem_limit_bytes=4 << 20),
        cost_estimate=took(2),
        name="lat_pack",
    )(*arrays, *arrays)


def field_index(f, level, levels):
    return (FIELDS - 1) * levels if f == FIELDS - 1 else f * levels + level


def tile_copies(levels, t, v, m, o, out, mask, sems):
    sources = [t.at[i] for i in range(NTR)] + [v.at[0], v.at[1], m]
    copies = [pltpu.make_async_copy(o, mask, sems.at[FIELDS - 1])]
    for f, source in enumerate(sources):
        target = out.at[pl.ds(f * levels, levels)]
        copies.append(pltpu.make_async_copy(source.at[pl.ds(0, levels)], target, sems.at[f]))
    return copies


def tile_shape(levels, rows):
    return ((FIELDS - 1) * levels + 1, rows, 128)


def finish_tile(copies, out, mask):
    for copy in copies:
        copy.wait()
    out[out.shape[0] - 1] = mask[...].astype(jnp.float32)


def lat_halo_blocks(lat, f, level):
    first, second = lat
    p, odd = f // 2, f % 2
    here = slice(8 * p, 8 * p + 8)
    n, s = pick(parity("gy"), first[level, here], second[level, here])
    if odd:
        return s, pltpu.roll(n, 4, 0)
    return pltpu.roll(s, 4, 0), n


def one_hot(ref, rows, cols, match):
    i, j = sub_ids(128), lane_ids(128)
    for r in range(0, rows, 128):
        for c in range(0, cols, 128):
            hit = match(i, j, r // 128, c // 128)
            ref[r : r + 128, c : c + 128] = jnp.where(hit, 1.0, 0.0).astype(jnp.bfloat16)


def own_match(i, j):
    s = j & 31
    return ((s < 8) & (i == s + 120)) | ((s >= 16) & (s < 24) & (i == s - 16))


def strip_match(i, j, f):
    s = j & 31
    west = (s >= 12) & (s < 16) & (i == 4 * f + s - 12)
    east = (s >= 8) & (s < 12) & (i == 4 * f + 4 + s - 8)
    return west | east


def tables_kernel(own_q, own, strip, back):
    one_hot(own_q, NTR * 128, 128, lambda i, j, r, c: own_match(i, j) & ((j >> 5) == r))
    one_hot(own, 128, 128, lambda i, j, r, c: own_match(i, j))

    def strips(i, j, odd, c):
        if c > 0:
            f = NTR + c - 1
            if f % 2 != odd:
                return i < 0
            return strip_match(i, j, f)
        hit = i < 0
        for f in range(odd, NTR, 2):
            hit |= strip_match(i, j, f) & ((j >> 5) == f)
        return hit

    one_hot(strip, strip.shape[0], strip.shape[1], strips)
    one_hot(
        back,
        128,
        NTR * 128,
        lambda i, j, r, c: (i == 32 * c + 16 + j) & (j < 4)
        | (i == 32 * c + 4 + j - 124) & (j >= 124),
    )


TABLES = [(NTR * 128, 128), (128, 128), (256, 5 * 128), (128, NTR * 128)]


def unit_place(n):
    return UNIT * (n // 4), 32 * (n % 4)


def strip_rows(count, rows):
    return UNIT * ((count * ((rows + 16) // UNIT) + 3) // 4)


def pack_columns(first, levels, x, lat, first_ref, second_ref, count):
    units = (x.shape[1] + 16) // UNIT
    lane = lane_ids(UNIT)
    west = east = jnp.zeros((UNIT, 128), jnp.float32)
    for l in range(count):
        level = first + l
        fields = range(FIELDS if level == 0 else FIELDS - 1)
        whole = []
        for f in fields:
            s, n = lat_halo_blocks(lat, f, level)
            whole.append(jnp.concatenate([s, x[field_index(f, level, levels)], n], axis=0))
        for r in range(units):
            place, base = unit_place(l * units + r)
            for f in fields:
                at = base + 4 * f
                turned = pltpu.roll(whole[f][UNIT * r : UNIT * r + UNIT], (at - 124) % 128, 1)
                east = jnp.where((lane >= at) & (lane < at + 4), turned, east)
                to = (at + 4) % 128
                west = jnp.where((lane >= to) & (lane < to + 4), turned, west)
            if base == 96 or (l == count - 1 and r == units - 1):
                here = slice(place, place + UNIT)
                first_ref[here], second_ref[here] = pick(parity("gx"), east, west)
                west = east = jnp.zeros((UNIT, 128), jnp.float32)


def fetch_kernel(after, t, v, m, o, w, x, out, mask, sems, sem):
    copies = tile_copies(t.shape[1], t, v, m, o, x, mask, sems)
    copies.append(pltpu.make_async_copy(w.at[pl.ds(0, out.shape[0])], out, sem))
    for copy in copies:
        copy.start()
    finish_tile(copies[:-1], x, mask)
    copies[-1].wait()


def fetch(after, arrays, weights):
    levels, rows = arrays[0].shape[1:3]
    part = (rows * FIRST // 8,) + weights.shape[1:]
    return pl.pallas_call(
        fetch_kernel,
        in_specs=[pl.BlockSpec(memory_space=pl.ANY)]
        + [pl.BlockSpec(memory_space=pltpu.HBM)] * 5,
        out_specs=[WHOLE] * 2,
        out_shape=[
            pltpu.VMEM(tile_shape(levels, rows), jnp.float32),
            pltpu.VMEM(part, weights.dtype),
        ],
        scratch_shapes=[
            pltpu.VMEM(arrays[3].shape, jnp.int32),
            pltpu.SemaphoreType.DMA((FIELDS,)),
            pltpu.SemaphoreType.DMA,
        ],
        compiler_params=pltpu.CompilerParams(vmem_limit_bytes=2 << 20),
        cost_estimate=took(3),
        name="fetch",
    )(after, *(in_hbm(a) for a in (*arrays, weights)))


def lon_pack_kernel(levels, la, lb, x, first_ref, second_ref):
    pack_columns(0, levels, x, (la, lb), first_ref, second_ref, 1)


def others_pack_kernel(levels, skip, la, lb, x, w, first_ref, second_ref, *refs):
    out, own_q, own, strip, back, sem = refs
    copy = pltpu.make_async_copy(w.at[pl.ds(skip, out.shape[0])], out, sem)
    copy.start()
    pack_columns(1, levels, x, (la, lb), first_ref, second_ref, levels - 1)
    tables_kernel(own_q, own, strip, back)
    copy.wait()


def lon_pack(lat, tile, levels, weights=None):
    rows = tile.shape[1]
    count = levels - 1 if weights is not None else 1
    out = [jax.ShapeDtypeStruct((strip_rows(count, rows), 128), jnp.float32)] * 2
    if weights is None:
        kernel = functools.partial(lon_pack_kernel, levels)
    else:
        kernel = functools.partial(others_pack_kernel, levels, rows * FIRST // 8)
        out.append(pltpu.VMEM((rows * SECOND // 8,) + weights.shape[1:], weights.dtype))
        out += [pltpu.VMEM(shape, jnp.bfloat16) for shape in TABLES]
    more = [] if weights is None else [in_hbm(weights)]
    return pl.pallas_call(
        kernel,
        in_specs=[WHOLE] * 3 + [pl.BlockSpec(memory_space=pltpu.HBM)] * len(more),
        out_specs=[WHOLE] * len(out),
        out_shape=out,
        scratch_shapes=[pltpu.SemaphoreType.DMA] * len(more),
        compiler_params=pltpu.CompilerParams(vmem_limit_bytes=4 << 20),
        cost_estimate=took(0.3 if weights is None else 2),
        name="lon_pack",
    )(*lat, in_vmem(tile), *more)


def unpack_field(ext, f, level, levels, x, lat):
    rows = x.shape[1]
    s, n = lat_halo_blocks(lat, f, level)
    ext[OFF - 8 : OFF] = s
    ext[OFF : OFF + rows] = x[field_index(f, level, levels)]
    ext[OFF + rows : OFF + rows + 8] = n


def terms(x, count):
    out = []
    for i in range(count):
        out.append(x.astype(jnp.bfloat16))
        if i < count - 1:
            x = x - out[-1].astype(jnp.float32)
    return out


def moved(parts, table, count):
    n = parts[0].shape[0]
    split = [terms(p, count) for p in parts]
    lhs = jnp.concatenate(
        [jnp.concatenate([p[i] for p in split], axis=1) for i in range(count)], axis=0
    )
    out = jnp.dot(lhs, table, preferred_element_type=jnp.float32)
    total = out[:n]
    for i in range(1, count):
        total = total + out[i * n : i * n + n]
    return total


def strip_parts(lon, level, units):
    near = lane_ids(UNIT) % 8 < 4
    first, second, base = lon
    even, odd = [], []
    for r in range(units):
        row, lane = level_unit(level - base, r, units)
        here = pl.ds(row, UNIT)
        e, w = pick(parity("gx"), first[here, :], second[here, :])
        even.append(pltpu.roll(jnp.where(near, w, e), (128 - lane) & 127, 1))
        odd.append(pltpu.roll(jnp.where(near, e, w), (128 - lane) & 127, 1))
    return [jnp.concatenate(even, axis=0), jnp.concatenate(odd, axis=0)]


def level_unit(l, r, units):
    n = l * units + r
    if isinstance(n, int):
        return unit_place(n)
    return pl.multiple_of(UNIT * (n >> 2), UNIT), 32 * (n & 3)


def side_arrays(rows, level, fields, sides, columns, lon, own, strip, count):
    body = slice(OFF - 8, OFF + rows + 8)
    packed = strip_parts(lon, level, (rows + 16) // UNIT)
    first, last = 128 * columns[0], 128 * (columns[-1] + 1)
    got = moved(packed, strip[:, first:last], count)
    for i, (parts, side, table) in enumerate(zip(fields, sides, own)):
        mine = moved([p[body] for p in parts], table[...], count)
        side[body] = mine + got[:, 128 * i : 128 * i + 128]


def to_right(a):
    return pltpu.roll(a, 127, 1)


def to_left(a):
    return pltpu.roll(a, 1, 1)


def chunks(first, last, size):
    return [slice(r, r + size) for r in range(first, last, size)]


def around(rows):
    return chunks(OFF - 8, OFF + rows + 8, 24)


def moved_rows(here, by):
    return slice(here.start + by, here.stop + by)


def open_faces(rows, ocean, east, north):
    for here in around(rows):
        o = ocean[here]
        east[here] = 0.5 * (o * to_right(o))
        north[here] = 0.5 * (o * ocean[moved_rows(here, 1)])


def faces(a, b, mix, face):
    vel = a + b
    low = jnp.maximum(vel, 0.0) + mix
    return face * low, face * (low - vel)


def coefficients(rows, u, v, k, east, north, coef, above):
    for here in around(rows):
        up = moved_rows(here, 1)
        a, b = faces(v[here], v[up], k[here] + k[up], north[here])
        above[here] = a
        coef[3, here] = b
    for here in around(rows):
        below = moved_rows(here, -1)
        us, ks = u[here], k[here]
        a, b = faces(us, to_right(us), ks + to_right(ks), east[here])
        wa, wb = to_left(a), to_left(b)
        south = above[below]
        coef[0, here] = (1.0 - (a + wb)) - (above[here] + coef[3, below])
        coef[1, here] = b
        coef[2, here] = wa
        coef[4, here] = south


def stencil(c, q, here):
    mid = q[here]
    return (
        c[0] * mid
        + c[1] * to_right(mid)
        + c[2] * to_left(mid)
        + c[3] * q[moved_rows(here, 1)]
        + c[4] * q[moved_rows(here, -1)]
    )


def advance(rows, coef, side_coef, q, side):
    for step in range(STEPS):
        src, dst = step % 2, (step + 1) % 2
        last = step == STEPS - 1
        for here in chunks(OFF, OFF + rows, 32) if last else around(rows):
            c = [side_coef[i, here] for i in range(5)]
            side[dst, here] = stencil(c, side.at[src], here)
            c = [coef[i, here] for i in range(5)]
            for i in range(NTR):
                q[dst, i, here] = stencil(c, q.at[src, i], here)


def field_scratch(rows):
    ext = (rows + 32, 128)
    return [
        pltpu.VMEM((count,) + ext, jnp.float32)
        for count in (3, 3, 4, 2, 5, 5)
    ] + [
        pltpu.VMEM((2, NTR) + ext, jnp.float32),
        pltpu.VMEM((2,) + ext, jnp.float32),
    ]


def set_faces(x, levels, lat, lon, tables, scratch):
    rows = x.shape[1]
    own_q, own, strip, back = tables
    vel, side_vel, face = scratch[:3]
    ocean, side = vel.at[0], side_vel.at[0]
    unpack_field(ocean, FIELDS - 1, 0, levels, x, lat)
    side_arrays(rows, 0, [[ocean]], [side], [NTR], lon, [own], strip, 1)
    open_faces(rows, ocean, face.at[0], face.at[1])
    open_faces(rows, side, face.at[2], face.at[3])


def run_level(level, x, levels, lat, lon, tables, scratch, count):
    rows = x.shape[1]
    own_q, own, strip, back = tables
    vel, side_vel, face, above, coef, side_coef, q, side = scratch
    now = [q.at[0, i] for i in range(NTR)]
    three = [vel.at[i] for i in range(3)]
    for i, ref in enumerate(now + three):
        unpack_field(ref, i, level, levels, x, lat)
    side_arrays(
        rows,
        level,
        [now] + [[ref] for ref in three],
        [side.at[0]] + [side_vel.at[i] for i in range(3)],
        range(NTR),
        lon,
        [own_q, own, own, own],
        strip,
        count,
    )
    coefficients(rows, *three, face.at[0], face.at[1], coef, above.at[0])
    coefficients(
        rows, *(side_vel.at[i] for i in range(3)), face.at[2], face.at[3], side_coef, above.at[1]
    )
    advance(rows, coef, side_coef, q, side)
    body = slice(OFF, OFF + rows)
    ends = moved([side[0, body]], back[...], count)
    lane = lane_ids(rows)
    inner = (lane >= STEPS) & (lane < 128 - STEPS)
    return [
        jnp.where(inner, q[0, i, body], ends[:, 128 * i : 128 * i + 128]) for i in range(NTR)
    ]


def surface_kernel(order, accs, levels, slot, x, la, lb, wa, wb, *refs):
    tables, w_held, w_more, w_hbm = refs[:4], refs[4], refs[5], refs[6]
    out_q, out_send, out_keep = refs[7:10]
    scratch, surf, w_last, sem, sums = refs[10:18], refs[18], refs[19], refs[20], refs[21:]
    rows = x.shape[1]
    done_rows = w_held.shape[0] + w_more.shape[0]
    copy = pltpu.make_async_copy(w_hbm.at[pl.ds(done_rows, w_last.shape[0])], w_last, sem)
    copy.start()
    lat, lon = (la, lb), (wa, wb, 0)
    set_faces(x, levels, lat, lon, tables, scratch)
    ocean = x[field_index(FIELDS - 1, 0, levels)]
    for i, done in enumerate(run_level(0, x, levels, lat, lon, tables, scratch, 3)):
        out_q[i] = done
        surf[pl.ds(i, rows, stride=8), :] = done * ocean
    surf[pl.ds(NTR, rows, stride=8), :] = ocean
    for i in range(NTR + 1, 8):
        surf[pl.ds(i, rows, stride=8), :] = jnp.zeros((rows, 128), jnp.float32)
    for d in sums:
        d[...] = jnp.zeros_like(d)
    first = sub_ids(16) < 8
    kb = w_held.shape[1]

    def body(w, base, j, carry):
        i = j + base
        s = surf[pl.ds(pl.multiple_of(16 * i, 16), 16), :]
        lhs = jnp.concatenate(
            [jnp.where(first, s, 0.0), jnp.where(first, 0.0, s)], axis=1
        ).astype(jnp.bfloat16)
        for k in range(0, kb, 2):
            rhs = jnp.concatenate(
                [
                    jnp.concatenate([w[2 * j + r, k], w[2 * j + r, k + 1]], axis=1)
                    for r in range(2)
                ],
                axis=0,
            )
            part = jnp.dot(lhs, rhs, preferred_element_type=jnp.float32)
            for r in range(2):
                for kk in range(2):
                    d = sums[(k + kk) % accs]
                    at = pl.ds(
                        pl.multiple_of(8 * slot[k + kk, 2 * i + r], 8), 8
                    )
                    d[at, :] += part[8 * r : 8 * r + 8, 128 * kk : 128 * kk + 128]
        return carry

    start = 0
    for w in (w_held, w_more, w_last):
        if w is w_last:
            copy.wait()
        pairs = w.shape[0] // 2
        lax.fori_loop(0, pairs, functools.partial(body, w, start), 0, unroll=8)
        start += pairs
    chunk = ABD * (NTR + 1)
    half = len(order) // 2
    for place, owner in enumerate(order):
        ref, base = (out_keep, place) if place < half else (out_send, place - half)
        for f in range(NTR + 1):
            total = sums[0][pl.ds(owner * ABD * 8 + f, ABD, stride=8), :]
            for d in sums[1:]:
                total = total + d[pl.ds(owner * ABD * 8 + f, ABD, stride=8), :]
            at = base * chunk + f * ABD
            ref[at : at + ABD, :] = total


def surface(order, slot, tile, levels, lat, lon, tables, held, weights):
    rows = tile.shape[1]
    owners = len(order)
    accs = 2 if owners <= 32 else 1
    half = owners // 2 * ABD * (NTR + 1)
    last = (rows - sum(w.shape[0] for w in held),) + weights.shape[1:]
    return pl.pallas_call(
        functools.partial(surface_kernel, order, accs, levels),
        in_specs=[SCALARS] + [WHOLE] * 11 + [pl.BlockSpec(memory_space=pltpu.HBM)],
        out_specs=[WHOLE] * 3,
        scratch_shapes=field_scratch(rows)
        + [pltpu.VMEM((rows * 8, 128), jnp.float32)]
        + [pltpu.VMEM(last, weights.dtype), pltpu.SemaphoreType.DMA]
        + [pltpu.VMEM((owners * ABD * 8, 128), jnp.float32)] * accs,
        out_shape=[
            jax.ShapeDtypeStruct((NTR, rows, 128), jnp.float32),
            jax.ShapeDtypeStruct((half, 128), jnp.float32),
            jax.ShapeDtypeStruct((half, 128), jnp.float32),
        ],
        compiler_params=pltpu.CompilerParams(vmem_limit_bytes=24 << 20),
        cost_estimate=took(7),
        name="surface",
    )(slot, in_vmem(tile), *lat, *lon, *tables, *(in_vmem(w) for w in held), in_hbm(weights))


def deep_kernel(first, levels, x, la, lb, oa, ob, wa, wb, *refs):
    tables, base, out, scratch = refs[:4], refs[4], refs[5], refs[6:]
    lat = (la, lb)
    level = pl.program_id(0) + first

    @pl.when(pl.program_id(0) == 0)
    def _():
        set_faces(x, levels, lat, (oa, ob, 0), tables, scratch)

    if first == 0:
        @pl.when(level == 0)
        def _():
            out[:, 0] = base[...]

    @pl.when(level > 0)
    def _():
        lon = (wa, wb, 1)
        for i, done in enumerate(run_level(level, x, levels, lat, lon, tables, scratch, COUNT)):
            out[i, 0] = done


def deep(tile, levels, lat, lon0, lon, tables, base, first, count):
    rows = tile.shape[1]
    return pl.pallas_call(
        functools.partial(deep_kernel, first, levels),
        grid=(count,),
        in_specs=[WHOLE] * 11 + [pl.BlockSpec(memory_space=pl.ANY) if first else WHOLE],
        out_specs=pl.BlockSpec((NTR, 1, rows, 128), lambda l: (0, l + first, 0, 0)),
        out_shape=jax.ShapeDtypeStruct((NTR, levels, rows, 128), jnp.float32),
        scratch_shapes=field_scratch(rows),
        input_output_aliases={11: 0} if first else {},
        compiler_params=pltpu.CompilerParams(vmem_limit_bytes=16 << 20),
        cost_estimate=took(1.3 * count),
        name="deep",
    )(in_vmem(tile), *lat, *lon0, *lon, *tables, base)


def swap(first, second, axis, ring):
    n = lax.axis_size(axis)
    even = [(i, i + 1) for i in range(0, n - 1, 2)]
    odd = [(i, (i + 1) % n) for i in range(1, n if ring else n - 1, 2)]
    second = lax.ppermute(second, axis, odd + [(j, i) for i, j in odd])
    first = lax.ppermute(first, axis, even + [(j, i) for i, j in even])
    return first, second


def partner(a, mask, n):
    return lax.ppermute(a, AXES, [(i, i ^ mask) for i in range(n)])


def rounds_of(owners):
    bits = owners.bit_length() - 1
    out, at = [(0, 1)], 1
    while at < bits:
        width = min(2, bits - at)
        out.append((at, width))
        at += width
    return out


def order_of(owners):
    def key(owner):
        return tuple((owner >> at) & ((1 << width) - 1) for at, width in rounds_of(owners))
    return sorted(range(owners), key=key)


def per_device(tracers, velocity, mixing, land_mask, remap_weights, remap_dest):
    owners = lax.axis_size("gx") * lax.axis_size("gy")
    levels = tracers.shape[1]
    me = lax.axis_index("gx") * lax.axis_size("gy") + lax.axis_index("gy")
    dest = remap_dest[:, 0].T
    slot = jnp.bitwise_xor(dest // ABD, me) * ABD + dest % ABD

    arrays = (tracers, velocity, mixing, land_mask)
    strips = lat_pack(*arrays)
    lat = swap(*strips, "gy", False)
    slot, first = lax.optimization_barrier((slot, strips[0]))
    tile, held = fetch(slot, arrays, remap_weights)
    lat, tile, held = lax.optimization_barrier((lat, tile, held))
    first, second = lon_pack(lat, tile, levels)
    lon0 = swap(first, second, "gx", True)
    lat, first = lax.optimization_barrier((lat, first))
    first, second, more, *tables = lon_pack(lat, tile, levels, remap_weights)
    lon0, first, more, tables = lax.optimization_barrier((lon0, first, more, tables))
    lon = swap(first, second, "gx", True)

    order = order_of(owners)
    done, send, keep = surface(
        order, slot, tile, levels, lat, lon0, tables, (held, more), remap_weights
    )
    lon, send = lax.optimization_barrier((lon, send))
    total = keep + partner(send, 1, owners)
    lon, total = lax.optimization_barrier((lon, total))
    values = done
    rounds = rounds_of(owners)[1:]
    cut = [0] + [levels * 3 * (i + 1) // (3 * len(rounds) - 2) for i in range(len(rounds) - 1)]
    cut.append(levels)
    for i, (at, width) in enumerate(rounds):
        parts = total.reshape((1 << width, -1, 128))
        got = [partner(parts[j], j << at, owners) for j in range(1, 1 << width)]
        values = deep(
            tile, levels, lat, lon0, lon, tables, values, cut[i], cut[i + 1] - cut[i]
        )
        got, values = lax.optimization_barrier((got, values))
        total = parts[0]
        for g in got:
            total = total + g
    atmo = total.reshape(NTR + 1, ABD, 128).transpose(1, 0, 2)
    return values, atmo


def solution(mesh):
    placed = (
        P(None, None, "gy", "gx"),
        P(None, None, "gy", "gx"),
        P(None, "gy", "gx"),
        P("gy", "gx"),
        P("gy", None, "gx", None),
        P("gy", "gx", None),
    )
    return jax.shard_map(
        per_device,
        mesh=mesh,
        in_specs=placed,
        out_specs=(P(None, None, "gy", "gx"), P(("gx", "gy"), None, None)),
        check_vma=False,
    )
```

time: 61 us -> 51.3 us (0.84)
  Pallas kernels: 32.7 us -> 27.1 us
  waiting for transfers between devices: 7.39 us -> 5.04 us
  local copies, waits for them, and re-layouts: 1.11 us -> 0.05 us
  starting transfers between devices: 18.1 us -> 17.4 us
    pallas_call x5 -> x6, Pallas kernels: 30.8 us -> 26 us  [the longest x2 11.7 us: deep(): pl.pallas_call(functools.partial(deep_kernel, first, levels), grid=(count...]
    ppermute x4 -> x6, waiting for transfers between devices: 5.65 us -> 1.98 us  [the longest x3 1.52 us: swap(): first = lax.ppermute(first, axis, even + [(j, i) for i, j in even])]
    ppermute x7, waiting for transfers between devices: 1.74 us -> 3.06 us  [partner(): return lax.ppermute(a, AXES, [(i, i ^ mask) for i in range(n)])]
    unnamed x12 -> x2, local copies, waits for them, and re-layouts: 1.06 us -> 0.01 us
    pallas_call x1, Pallas kernels: 1.9 us -> 1.13 us  [lat_pack(): pl.pallas_call(lat_pack_kernel, grid=(1,), in_specs=specs(0) + specs(last...]
    ppermute x7, starting transfers between devices: 9.64 us -> 8.87 us  [partner(): return lax.ppermute(a, AXES, [(i, i ^ mask) for i in range(n)])]
    ppermute x4 -> x6, starting transfers between devices: 8.42 us -> 8.57 us  [the longest x3 5.44 us: swap(): second = lax.ppermute(second, axis, odd + [(j, i) for i, j in odd])]
  transfers between devices with their start and end apart: 11 -> 13, of which waited for: 3 -> 4; matrix products, arithmetic and copies ran while one was open for 0% -> 0% of each run, Pallas kernels for 36% -> 50%
where the time goes in v3:
time: 51.3 us; the launch traced here: 51.1 us
  Pallas kernels  27.1 us (53%)
  starting transfers between devices  17.4 us (34%)
  waiting for transfers between devices  5.04 us (10%)
  between operations  0.77 us (2%)
  other arithmetic  0.76 us (1%)
    pallas_call x2, Pallas kernels, deep(): pl.pallas_call(functools.partial(deep_kernel, first, levels), grid=(count...  11.7 us
    ppermute x7, starting transfers between devices, partner(): return lax.ppermute(a, AXES, [(i, i ^ mask) for i in range(n)])  8.87 us
    pallas_call x1, Pallas kernels, surface(): pl.pallas_call(functools.partial(surface_kernel, order, accs, levels), in...  6.16 us
    ppermute x3, starting transfers between devices, swap(): second = lax.ppermute(second, axis, odd + [(j, i) for i, j in odd])  5.44 us
    pallas_call x2, Pallas kernels, lon_pack(): pl.pallas_call(kernel, in_specs=[WHOLE] * 3 + [pl.BlockSpec(memory_space=...  4.05 us
    pallas_call x1, Pallas kernels, fetch(): pl.pallas_call(fetch_kernel, in_specs=[pl.BlockSpec(memory_space=pl.ANY)]...  4.03 us
    ppermute x3, starting transfers between devices, swap(): first = lax.ppermute(first, axis, even + [(j, i) for i, j in even])  3.13 us
    ppermute x7, waiting for transfers between devices, partner(): return lax.ppermute(a, AXES, [(i, i ^ mask) for i in range(n)])  3.06 us
  transfers between devices with their start and end apart: 13, of which 4 were waited for; matrix products, arithmetic and copies ran while one was open for 0% of the time, Pallas kernels for 50%

profile of v3, /device:TPU:0, one launch (start us, length us, event | category | flops | bytes accessed | tf_op | source)
XLA Modules:
  0.0 51.1 jit_solution(10313052644372046333)
XLA Ops:
  0.6 1.1 %lat_pack.1 = (f32[8,32,128]{2,1,0:T(8,128)S(1)}, f32[8,32,128]{2,1,0:T(8,128)S(1)}) custom-call(f32[4,8,128,128]{3,2,1,0:T(8,128)} %t.1, f32[2,8,128,128]{3,2,1,0:T(8,128)} %v.1, f32[8,128,128]{2,1,0:T(8,128)} %m.1, s32[128,128]{1,0:T(8,128)} %o.1, f32[4,8,128,128]{3,2,1,0:T(8,128)} %t.1, f32[2,8,128,128]{3,2,1,0:T(8,128)} %v.1, f32[8,128,128]{2,1,0:T(8,128)} %m.1, ...), custom_call_target="tpu_custom_call" | custom-call | bytes 7000000 | tf_op jit(solution)/shard_map/lat_pack/pallas_call | solution.py:86
  1.8 0.5 %collective-permute-start = (f32[8,32,128]{2,1,0:T(8,128)S(1)}, f32[8,32,128]{2,1,0:T(8,128)S(1)}, u32[]{:S(2)}, u32[]{:S(2)}) collective-permute-start(f32[8,32,128]{2,1,0:T(8,128)S(1)} %get-tuple-element.47), channel_id=1, source_target_pairs={{0,1},{2,3},{1,0},{3,2},{4,5},{6,7},{5,4},{7,6},{8,9},{10,11},{9,8... | collective-permute-start | bytes 393224 | tf_op jit(solution)/shard_map/ppermute | solution.py:601
  2.3 0.7 %collective-permute-start.1 = (f32[8,32,128]{2,1,0:T(8,128)S(1)}, f32[8,32,128]{2,1,0:T(8,128)S(1)}, u32[]{:S(2)}, u32[]{:S(2)}) collective-permute-start(f32[8,32,128]{2,1,0:T(8,128)S(1)} %get-tuple-element.48), channel_id=1, source_target_pairs={{1,2},{2,1},{5,6},{6,5},{9,10},{10,9},{13,14},{14,13},{17,18},{18,... | collective-permute-start | bytes 393224 | tf_op jit(solution)/shard_map/ppermute | solution.py:600
  3.0 4.0 %fetch.1 = (f32[57,128,128]{2,1,0:T(8,128)S(1)}, bf16[48,4,128,128]{3,2,1,0:T(8,128)(2,1)S(1)}) custom-call(s32[4,128]{1,0:T(4,128)S(1)} %fusion.4.after.slot, f32[4,8,128,128]{3,2,1,0:T(8,128)} %t.1, f32[2,8,128,128]{3,2,1,0:T(8,128)} %v.1, f32[8,128,128]{2,1,0:T(8,128)} %m.1, s32[128,128]{1,0:T(8,128)} %o.1, bf16[128,4,128,128]{3,2,1,0:T(8,128)(2,1)} %refs_6_.1), custom_call_target="tpu_custom_call" | custom-call | bytes 10500000 | tf_op jit(solution)/shard_map/fetch/pallas_call | solution.py:224
  7.0 0.2 lon_pack.2
  7.3 2.6 %collective-permute-start.2 = (f32[48,128]{1,0:T(8,128)S(1)}, f32[48,128]{1,0:T(8,128)S(1)}, u32[]{:S(2)}, u32[]{:S(2)}) collective-permute-start(f32[48,128]{1,0:T(8,128)S(1)} %get-tuple-element.55), channel_id=1, source_target_pairs={{0,4},{8,12},{16,20},{24,28},{4,0},{12,8},{20,16},{28,24},{1,5},{9... | collective-permute-start | bytes 73736 | tf_op jit(solution)/shard_map/ppermute | solution.py:601
  9.9 3.5 %collective-permute-start.3 = (f32[48,128]{1,0:T(8,128)S(1)}, f32[48,128]{1,0:T(8,128)S(1)}, u32[]{:S(2)}, u32[]{:S(2)}) collective-permute-start(f32[48,128]{1,0:T(8,128)S(1)} %get-tuple-element.56), channel_id=1, source_target_pairs={{4,8},{12,16},{20,24},{28,0},{8,4},{16,12},{24,20},{0,28},{5,9},{1... | collective-permute-start | bytes 73736 | tf_op jit(solution)/shard_map/ppermute | solution.py:600
  13.4 3.8 %lon_pack.3 = (f32[256,128]{1,0:T(8,128)S(1)}, f32[256,128]{1,0:T(8,128)S(1)}, bf16[48,4,128,128]{3,2,1,0:T(8,128)(2,1)S(1)}, bf16[512,128]{1,0:T(8,128)(2,1)S(1...) custom-call(f32[8,32,128]{2,1,0:T(8,128)S(1)} %collective-permute-done.la, ...), custom_call_target="tpu_custom_call" | custom-call | bytes 7000000 | tf_op jit(solution)/shard_map/lon_pack/pallas_call | solution.py:268
  17.3 1.2 %collective-permute-start.5 = (f32[256,128]{1,0:T(8,128)S(1)}, f32[256,128]{1,0:T(8,128)S(1)}, u32[]{:S(2)}, u32[]{:S(2)}) collective-permute-start(f32[256,128]{1,0:T(8,128)S(1)} %get-tuple-element.66), channel_id=1, source_target_pairs={{4,8},{12,16},{20,24},{28,0},{8,4},{16,12},{24,20},{0,28},{5,9},{1... | collective-permute-start | bytes 393224 | tf_op jit(solution)/shard_map/ppermute | solution.py:600
  18.5 6.2 %surface.1 = (f32[4,128,128]{2,1,0:T(8,128)S(1)}, f32[1280,128]{1,0:T(8,128)S(1)}, f32[1280,128]{1,0:T(8,128)S(1)}) custom-call(s32[4,128]{1,0:T(4,128)S(1)} %fusion.4.after.slot, f32[57,128,128]{2,1,0:T(8,128)S(1)} %get-tuple-element.54.x, f32[8,32,128]{2,1,0:T(8,128)S(1)} %collective-permute-done.la, f32[8,32,128]{2,1,0:T(8,128)S(1)} %collective-permute-done.1.lb, ...), custom_call_target="tpu_custom_call" | custom-call | bytes 24500000 | tf_op jit(solution)/shard_map/surface/pallas_call | solution.py:540
  24.7 0.5 collective-permute-done.5.wb
  25.1 1.5 %collective-permute-done.4.wa = f32[256,128]{1,0:T(8,128)S(1)} collective-permute-done((f32[256,128]{1,0:T(8,128)S(1)}, f32[256,128]{1,0:T(8,128)S(1)}, u32[]{:S(2)}, u32[]{:S(2)}) %collective-permute-start.4) | collective-permute-done | bytes 131104 | tf_op jit(solution)/shard_map/ppermute | solution.py:601
  26.7 0.9 %collective-permute-start.6 = (f32[1280,128]{1,0:T(8,128)S(1)}, f32[1280,128]{1,0:T(8,128)S(1)}, u32[]{:S(2)}, u32[]{:S(2)}) collective-permute-start(f32[1280,128]{1,0:T(8,128)S(1)} %get-tuple-element.79), channel_id=1, source_target_pairs={{0,1},{1,0},{2,3},{3,2},{4,5},{5,4},{6,7},{7,6},{8,9},{9,8},{10,11... | collective-permute-start | bytes 1966088 | tf_op jit(solution)/shard_map/ppermute | solution.py:606
  27.5 1.7 %collective-permute-done.6 = f32[1280,128]{1,0:T(8,128)S(1)} collective-permute-done((f32[1280,128]{1,0:T(8,128)S(1)}, f32[1280,128]{1,0:T(8,128)S(1)}, u32[]{:S(2)}, u32[]{:S(2)}) %collective-permute-start.6) | collective-permute-done | bytes 655392 | tf_op jit(solution)/shard_map/ppermute | solution.py:606
  29.2 0.1 add.37
  29.4 1.3 %collective-permute-start.7 = (f32[320,128]{1,0:T(8,128)S(1)}, f32[320,128]{1,0:T(8,128)S(1)}, u32[]{:S(2)}, u32[]{:S(2)}) collective-permute-start(f32[320,128]{1,0:T(8,128)S(1)} %get-tuple-element.94), channel_id=1, source_target_pairs={{0,2},{1,3},{2,0},{3,1},{4,6},{5,7},{6,4},{7,5},{8,10},{9,11},{10,... | collective-permute-start | bytes 491528 | tf_op jit(solution)/shard_map/ppermute | solution.py:606
  30.6 1.8 %collective-permute-start.8 = (f32[320,128]{1,0:T(8,128)S(1)}, f32[320,128]{1,0:T(8,128)S(1)}, u32[]{:S(2)}, u32[]{:S(2)}) collective-permute-start(f32[320,128]{1,0:T(8,128)S(1)} %get-tuple-element.93), channel_id=1, source_target_pairs={{0,4},{1,5},{2,6},{3,7},{4,0},{5,1},{6,2},{7,3},{8,12},{9,13},{10,... | collective-permute-start | bytes 491528 | tf_op jit(solution)/shard_map/ppermute | solution.py:606
  32.4 0.5 collective-permute-start.9
  32.9 8.0 %deep.2.refs_4_ = f32[4,8,128,128]{3,2,1,0:T(8,128)} custom-call(f32[57,128,128]{2,1,0:T(8,128)S(1)} %get-tuple-element.54.x, f32[8,32,128]{2,1,0:T(8,128)S(1)} %collective-permute-done.la, f32[8,32,128]{2,1,0:T(8,128)S(1)} %collective-permute-done.1.lb, f32[48,128]{1,0:T(8,128)S(1)} %collective-permute-done.2.wa.oa, ...), custom_call_target="tpu_custom_call" | custom-call | bytes 27300000 | tf_op jit(solution)/shard_map/deep/pallas_call | solution.py:582
  41.0 3.7 %collective-permute-start.11 = (f32[80,128]{1,0:T(8,128)S(1)}, f32[80,128]{1,0:T(8,128)S(1)}, u32[]{:S(2)}, u32[]{:S(2)}) collective-permute-start(f32[80,128]{1,0:T(8,128)S(1)} %get-tuple-element.96), channel_id=1, source_target_pairs={{0,16},{1,17},{2,18},{3,19},{4,20},{5,21},{6,22},{7,23},{8,24},{9,... | collective-permute-start | bytes 122888 | tf_op jit(solution)/shard_map/ppermute | solution.py:606
  44.7 0.7 %collective-permute-start.12 = (f32[80,128]{1,0:T(8,128)S(1)}, f32[80,128]{1,0:T(8,128)S(1)}, u32[]{:S(2)}, u32[]{:S(2)}) collective-permute-start(f32[80,128]{1,0:T(8,128)S(1)} %get-tuple-element.95), channel_id=1, source_target_pairs={{0,24},{1,25},{2,26},{3,27},{4,28},{5,29},{6,30},{7,31},{8,16},{9,... | collective-permute-start | bytes 122888 | tf_op jit(solution)/shard_map/ppermute | solution.py:606
  45.4 3.8 %deep.3 = f32[4,8,128,128]{3,2,1,0:T(8,128)} custom-call(f32[57,128,128]{2,1,0:T(8,128)S(1)} %get-tuple-element.54.x, f32[8,32,128]{2,1,0:T(8,128)S(1)} %collective-permute-done.la, f32[8,32,128]{2,1,0:T(8,128)S(1)} %collective-permute-done.1.lb, f32[48,128]{1,0:T(8,128)S(1)} %collective-permute-done.2.wa.oa, ...), custom_call_target="tpu_custom_call", output_to_operand_aliasing={{}: (11, {})} | custom-call | bytes 9100000 | tf_op jit(solution)/shard_map/deep/pallas_call | solution.py:582
  49.2 1.3 %collective-permute-done.12 = f32[80,128]{1,0:T(8,128)S(1)} collective-permute-done((f32[80,128]{1,0:T(8,128)S(1)}, f32[80,128]{1,0:T(8,128)S(1)}, u32[]{:S(2)}, u32[]{:S(2)}) %collective-permute-start.12) | collective-permute-done | bytes 40992 | tf_op jit(solution)/shard_map/ppermute | solution.py:606
  50.5 0.6 %fusion.1 = f32[80,128]{1,0:T(8,128)} fusion(f32[80,128]{1,0:T(8,128)S(1)} %collective-permute-done.12, f32[80,128]{1,0:T(8,128)S(1)} %collective-permute-done.11, f32[80,128]{1,0:T(8,128)S(1)} %collective-permute-done.10, f32[320,128]{1,0:T(8,128)S(1)} %add_add_fusion), kind=kLoop, calls=%fused_computation.3 | loop fusion | flops 30720 | bytes 204800 | tf_op jit(solution)/shard_map/add | solution.py:665
  (17 shorter events, 0.2 us)
Async XLA Ops:
  0.6 2.3 %copy-start = (s32[128,1,4]{0,2,1:T(4,128)S(1)}, s32[128,1,4]{0,2,1:T(4,128)}, u32[]{:S(2)}) copy-start(s32[128,1,4]{0,2,1:T(4,128)} %param.11) | copy-start | bytes 6148
  1.8 5.3 %collective-permute-start = (f32[8,32,128]{2,1,0:T(8,128)S(1)}, f32[8,32,128]{2,1,0:T(8,128)S(1)}, u32[]{:S(2)}, u32[]{:S(2)}) collective-permute-start(f32[8,32,128]{2,1,0:T(8,128)S(1)} %get-tuple-element.47), channel_id=1, source_target_pairs={{0,1},{2,3},{1,0},{3,2},{4,5},{6,7},{5,4},{7,6},{8,9},{10,11},{9,8... | collective-permute-start | bytes 393224 | tf_op jit(solution)/shard_map/ppermute | solution.py:601
  2.3 4.8 %collective-permute-start.1 = (f32[8,32,128]{2,1,0:T(8,128)S(1)}, f32[8,32,128]{2,1,0:T(8,128)S(1)}, u32[]{:S(2)}, u32[]{:S(2)}) collective-permute-start(f32[8,32,128]{2,1,0:T(8,128)S(1)} %get-tuple-element.48), channel_id=1, source_target_pairs={{1,2},{2,1},{5,6},{6,5},{9,10},{10,9},{13,14},{14,13},{17,18},{18,... | collective-permute-start | bytes 393224 | tf_op jit(solution)/shard_map/ppermute | solution.py:600
  7.3 11.2 %collective-permute-start.2 = (f32[48,128]{1,0:T(8,128)S(1)}, f32[48,128]{1,0:T(8,128)S(1)}, u32[]{:S(2)}, u32[]{:S(2)}) collective-permute-start(f32[48,128]{1,0:T(8,128)S(1)} %get-tuple-element.55), channel_id=1, source_target_pairs={{0,4},{8,12},{16,20},{24,28},{4,0},{12,8},{20,16},{28,24},{1,5},{9... | collective-permute-start | bytes 73736 | tf_op jit(solution)/shard_map/ppermute | solution.py:601
  9.9 8.6 %collective-permute-start.3 = (f32[48,128]{1,0:T(8,128)S(1)}, f32[48,128]{1,0:T(8,128)S(1)}, u32[]{:S(2)}, u32[]{:S(2)}) collective-permute-start(f32[48,128]{1,0:T(8,128)S(1)} %get-tuple-element.56), channel_id=1, source_target_pairs={{4,8},{12,16},{20,24},{28,0},{8,4},{16,12},{24,20},{0,28},{5,9},{1... | collective-permute-start | bytes 73736 | tf_op jit(solution)/shard_map/ppermute | solution.py:600
  17.3 7.9 %collective-permute-start.5 = (f32[256,128]{1,0:T(8,128)S(1)}, f32[256,128]{1,0:T(8,128)S(1)}, u32[]{:S(2)}, u32[]{:S(2)}) collective-permute-start(f32[256,128]{1,0:T(8,128)S(1)} %get-tuple-element.66), channel_id=1, source_target_pairs={{4,8},{12,16},{20,24},{28,0},{8,4},{16,12},{24,20},{0,28},{5,9},{1... | collective-permute-start | bytes 393224 | tf_op jit(solution)/shard_map/ppermute | solution.py:600
  18.5 8.1 %collective-permute-start.4 = (f32[256,128]{1,0:T(8,128)S(1)}, f32[256,128]{1,0:T(8,128)S(1)}, u32[]{:S(2)}, u32[]{:S(2)}) collective-permute-start(f32[256,128]{1,0:T(8,128)S(1)} %get-tuple-element.65), channel_id=1, source_target_pairs={{0,4},{8,12},{16,20},{24,28},{4,0},{12,8},{20,16},{28,24},{1,5},{9... | collective-permute-start | bytes 393224 | tf_op jit(solution)/shard_map/ppermute | solution.py:601
  26.7 2.6 %collective-permute-start.6 = (f32[1280,128]{1,0:T(8,128)S(1)}, f32[1280,128]{1,0:T(8,128)S(1)}, u32[]{:S(2)}, u32[]{:S(2)}) collective-permute-start(f32[1280,128]{1,0:T(8,128)S(1)} %get-tuple-element.79), channel_id=1, source_target_pairs={{0,1},{1,0},{2,3},{3,2},{4,5},{5,4},{6,7},{7,6},{8,9},{9,8},{10,11... | collective-permute-start | bytes 1966088 | tf_op jit(solution)/shard_map/ppermute | solution.py:606
  29.4 11.5 %collective-permute-start.7 = (f32[320,128]{1,0:T(8,128)S(1)}, f32[320,128]{1,0:T(8,128)S(1)}, u32[]{:S(2)}, u32[]{:S(2)}) collective-permute-start(f32[320,128]{1,0:T(8,128)S(1)} %get-tuple-element.94), channel_id=1, source_target_pairs={{0,2},{1,3},{2,0},{3,1},{4,6},{5,7},{6,4},{7,5},{8,10},{9,11},{10,... | collective-permute-start | bytes 491528 | tf_op jit(solution)/shard_map/ppermute | solution.py:606
  30.6 10.3 %collective-permute-start.8 = (f32[320,128]{1,0:T(8,128)S(1)}, f32[320,128]{1,0:T(8,128)S(1)}, u32[]{:S(2)}, u32[]{:S(2)}) collective-permute-start(f32[320,128]{1,0:T(8,128)S(1)} %get-tuple-element.93), channel_id=1, source_target_pairs={{0,4},{1,5},{2,6},{3,7},{4,0},{5,1},{6,2},{7,3},{8,12},{9,13},{10,... | collective-permute-start | bytes 491528 | tf_op jit(solution)/shard_map/ppermute | solution.py:606
  32.4 8.5 %collective-permute-start.9 = (f32[320,128]{1,0:T(8,128)S(1)}, f32[320,128]{1,0:T(8,128)S(1)}, u32[]{:S(2)}, u32[]{:S(2)}) collective-permute-start(f32[320,128]{1,0:T(8,128)S(1)} %get-tuple-element.92), channel_id=1, source_target_pairs={{0,6},{1,7},{2,4},{3,5},{4,2},{5,3},{6,0},{7,1},{8,14},{9,15},{10,... | collective-permute-start | bytes 491528 | tf_op jit(solution)/shard_map/ppermute | solution.py:606
  41.0 8.2 %collective-permute-start.10 = (f32[80,128]{1,0:T(8,128)S(1)}, f32[80,128]{1,0:T(8,128)S(1)}, u32[]{:S(2)}, u32[]{:S(2)}) collective-permute-start(f32[80,128]{1,0:T(8,128)S(1)} %get-tuple-element.97), channel_id=1, source_target_pairs={{0,8},{1,9},{2,10},{3,11},{4,12},{5,13},{6,14},{7,15},{8,0},{9,1},... | collective-permute-start | bytes 122888 | tf_op jit(solution)/shard_map/ppermute | solution.py:606
  41.0 8.2 %collective-permute-start.11 = (f32[80,128]{1,0:T(8,128)S(1)}, f32[80,128]{1,0:T(8,128)S(1)}, u32[]{:S(2)}, u32[]{:S(2)}) collective-permute-start(f32[80,128]{1,0:T(8,128)S(1)} %get-tuple-element.96), channel_id=1, source_target_pairs={{0,16},{1,17},{2,18},{3,19},{4,20},{5,21},{6,22},{7,23},{8,24},{9,... | collective-permute-start | bytes 122888 | tf_op jit(solution)/shard_map/ppermute | solution.py:606
  44.7 5.8 %collective-permute-start.12 = (f32[80,128]{1,0:T(8,128)S(1)}, f32[80,128]{1,0:T(8,128)S(1)}, u32[]{:S(2)}, u32[]{:S(2)}) collective-permute-start(f32[80,128]{1,0:T(8,128)S(1)} %get-tuple-element.95), channel_id=1, source_target_pairs={{0,24},{1,25},{2,26},{3,27},{4,28},{5,29},{6,30},{7,31},{8,16},{9,... | collective-permute-start | bytes 122888 | tf_op jit(solution)/shard_map/ppermute | solution.py:606

commit v4 on v3

--- a/solution.py
+++ b/solution.py
@@ -542,9 +542,9 @@
         in_specs=[SCALARS] + [WHOLE] * 11 + [pl.BlockSpec(memory_space=pltpu.HBM)],
         out_specs=[WHOLE] * 3,
         scratch_shapes=field_scratch(rows)
-        + [pltpu.VMEM((rows * 8, 128), jnp.float32)]
+        + [pltpu.VMEM((rows * 8 + 8, 128), jnp.float32)]
         + [pltpu.VMEM(last, weights.dtype), pltpu.SemaphoreType.DMA]
-        + [pltpu.VMEM((owners * ABD * 8, 128), jnp.float32)] * accs,
+        + [pltpu.VMEM((owners * ABD * 8 + 8, 128), jnp.float32)] * accs,
         out_shape=[
             jax.ShapeDtypeStruct((NTR, rows, 128), jnp.float32),
             jax.ShapeDtypeStruct((half, 128), jnp.float32),
@@ -616,9 +616,14 @@
     return out
 
 
+def cuts(levels, rounds):
+    between = [2 + (levels - 4) * i // (rounds - 2) for i in range(rounds - 1)]
+    return [0] + between + [levels]
+
+
 def order_of(owners):
     def key(owner):
-        return tuple((owner >> at) & ((1 << width) - 1) for at, width in rounds_of(owners))
+        return tuple((-(owner >> at)) & ((1 << width) - 1) for at, width in rounds_of(owners))
     return sorted(range(owners), key=key)
 
 
@@ -647,22 +652,20 @@
         order, slot, tile, levels, lat, lon0, tables, (held, more), remap_weights
     )
     lon, send = lax.optimization_barrier((lon, send))
-    total = keep + partner(send, 1, owners)
-    lon, total = lax.optimization_barrier((lon, total))
+    rounds = rounds_of(owners)
+    cut = cuts(levels, len(rounds))
+    parts = [keep, send]
     values = done
-    rounds = rounds_of(owners)[1:]
-    cut = [0] + [levels * 3 * (i + 1) // (3 * len(rounds) - 2) for i in range(len(rounds) - 1)]
-    cut.append(levels)
     for i, (at, width) in enumerate(rounds):
-        parts = total.reshape((1 << width, -1, 128))
-        got = [partner(parts[j], j << at, owners) for j in range(1, 1 << width)]
-        values = deep(
-            tile, levels, lat, lon0, lon, tables, values, cut[i], cut[i + 1] - cut[i]
-        )
+        got = [partner(parts[j], (-j % (1 << width)) << at, owners) for j in range(1, 1 << width)]
+        values = deep(tile, levels, lat, lon0, lon, tables, values, cut[i], cut[i + 1] - cut[i])
         got, values = lax.optimization_barrier((got, values))
         total = parts[0]
         for g in got:
             total = total + g
+        if i < len(rounds) - 1:
+            lon, total = lax.optimization_barrier((lon, total))
+            parts = total.reshape((1 << rounds[i + 1][1], -1, 128))
     atmo = total.reshape(NTR + 1, ABD, 128).transpose(1, 0, 2)
     return values, atmo
 

time: 51.3 us -> 49.8 us (0.971)
  waiting for transfers between devices: 5.04 us -> 2.47 us
  Pallas kernels: 27.1 us -> 28.1 us
    ppermute x7, waiting for transfers between devices: 3.06 us -> 0.5 us  [partner(): return lax.ppermute(a, AXES, [(i, i ^ mask) for i in range(n)])]
    pallas_call x2 -> x3, Pallas kernels: 11.7 us -> 12.7 us  [deep(): pl.pallas_call(functools.partial(deep_kernel, first, levels), grid=(count...]
  transfers between devices with their start and end apart: 13 -> 13, of which waited for: 4 -> 3; matrix products, arithmetic and copies ran while one was open for 0% -> 0% of each run, Pallas kernels for 50% -> 54%
where the time goes in v4:
time: 49.8 us; the launch traced here: 49.6 us
  Pallas kernels  28.1 us (56%)
  starting transfers between devices  17.4 us (35%)
  waiting for transfers between devices  2.47 us (5%)
  other arithmetic  0.76 us (2%)
  between operations  0.76 us (2%)
    pallas_call x3, Pallas kernels, deep(): pl.pallas_call(functools.partial(deep_kernel, first, levels), grid=(count...  12.7 us
    ppermute x7, starting transfers between devices, partner(): return lax.ppermute(a, AXES, [(i, i ^ mask) for i in range(n)])  8.86 us
    pallas_call x1, Pallas kernels, surface(): pl.pallas_call(functools.partial(surface_kernel, order, accs, levels), in...  6.17 us
    ppermute x3, starting transfers between devices, swap(): second = lax.ppermute(second, axis, odd + [(j, i) for i, j in odd])  5.44 us
    pallas_call x2, Pallas kernels, lon_pack(): pl.pallas_call(kernel, in_specs=[WHOLE] * 3 + [pl.BlockSpec(memory_space=...  4.05 us
    pallas_call x1, Pallas kernels, fetch(): pl.pallas_call(fetch_kernel, in_specs=[pl.BlockSpec(memory_space=pl.ANY)]...  4.03 us
    ppermute x3, starting transfers between devices, swap(): first = lax.ppermute(first, axis, even + [(j, i) for i, j in even])  3.13 us
    ppermute x3, waiting for transfers between devices, swap(): first = lax.ppermute(first, axis, even + [(j, i) for i, j in even])  1.52 us
  transfers between devices with their start and end apart: 13, of which 3 were waited for; matrix products, arithmetic and copies ran while one was open for 0% of the time, Pallas kernels for 54%

profile of v4, /device:TPU:0, one launch (start us, length us, event | category | flops | bytes accessed | tf_op | source)
XLA Modules:
  0.0 49.6 jit_solution(938186029509421792)
XLA Ops:
  0.6 1.1 %lat_pack.1 = (f32[8,32,128]{2,1,0:T(8,128)S(1)}, f32[8,32,128]{2,1,0:T(8,128)S(1)}) custom-call(f32[4,8,128,128]{3,2,1,0:T(8,128)} %t.1, f32[2,8,128,128]{3,2,1,0:T(8,128)} %v.1, f32[8,128,128]{2,1,0:T(8,128)} %m.1, s32[128,128]{1,0:T(8,128)} %o.1, f32[4,8,128,128]{3,2,1,0:T(8,128)} %t.1, f32[2,8,128,128]{3,2,1,0:T(8,128)} %v.1, f32[8,128,128]{2,1,0:T(8,128)} %m.1, ...), custom_call_target="tpu_custom_call" | custom-call | bytes 7000000 | tf_op jit(solution)/shard_map/lat_pack/pallas_call | solution.py:86
  1.8 0.5 %collective-permute-start = (f32[8,32,128]{2,1,0:T(8,128)S(1)}, f32[8,32,128]{2,1,0:T(8,128)S(1)}, u32[]{:S(2)}, u32[]{:S(2)}) collective-permute-start(f32[8,32,128]{2,1,0:T(8,128)S(1)} %get-tuple-element.52), channel_id=1, source_target_pairs={{0,1},{2,3},{1,0},{3,2},{4,5},{6,7},{5,4},{7,6},{8,9},{10,11},{9,8... | collective-permute-start | bytes 393224 | tf_op jit(solution)/shard_map/ppermute | solution.py:601
  2.3 0.7 %collective-permute-start.1 = (f32[8,32,128]{2,1,0:T(8,128)S(1)}, f32[8,32,128]{2,1,0:T(8,128)S(1)}, u32[]{:S(2)}, u32[]{:S(2)}) collective-permute-start(f32[8,32,128]{2,1,0:T(8,128)S(1)} %get-tuple-element.53), channel_id=1, source_target_pairs={{1,2},{2,1},{5,6},{6,5},{9,10},{10,9},{13,14},{14,13},{17,18},{18,... | collective-permute-start | bytes 393224 | tf_op jit(solution)/shard_map/ppermute | solution.py:600
  3.0 4.0 %fetch.1 = (f32[57,128,128]{2,1,0:T(8,128)S(1)}, bf16[48,4,128,128]{3,2,1,0:T(8,128)(2,1)S(1)}) custom-call(s32[4,128]{1,0:T(4,128)S(1)} %fusion.2.after.slot, f32[4,8,128,128]{3,2,1,0:T(8,128)} %t.1, f32[2,8,128,128]{3,2,1,0:T(8,128)} %v.1, f32[8,128,128]{2,1,0:T(8,128)} %m.1, s32[128,128]{1,0:T(8,128)} %o.1, bf16[128,4,128,128]{3,2,1,0:T(8,128)(2,1)} %refs_6_.1), custom_call_target="tpu_custom_call" | custom-call | bytes 10500000 | tf_op jit(solution)/shard_map/fetch/pallas_call | solution.py:224
  7.0 0.2 lon_pack.2
  7.3 2.6 %collective-permute-start.2 = (f32[48,128]{1,0:T(8,128)S(1)}, f32[48,128]{1,0:T(8,128)S(1)}, u32[]{:S(2)}, u32[]{:S(2)}) collective-permute-start(f32[48,128]{1,0:T(8,128)S(1)} %get-tuple-element.60), channel_id=1, source_target_pairs={{0,4},{8,12},{16,20},{24,28},{4,0},{12,8},{20,16},{28,24},{1,5},{9... | collective-permute-start | bytes 73736 | tf_op jit(solution)/shard_map/ppermute | solution.py:601
  9.9 3.5 %collective-permute-start.3 = (f32[48,128]{1,0:T(8,128)S(1)}, f32[48,128]{1,0:T(8,128)S(1)}, u32[]{:S(2)}, u32[]{:S(2)}) collective-permute-start(f32[48,128]{1,0:T(8,128)S(1)} %get-tuple-element.61), channel_id=1, source_target_pairs={{4,8},{12,16},{20,24},{28,0},{8,4},{16,12},{24,20},{0,28},{5,9},{1... | collective-permute-start | bytes 73736 | tf_op jit(solution)/shard_map/ppermute | solution.py:600
  13.4 3.8 %lon_pack.3 = (f32[256,128]{1,0:T(8,128)S(1)}, f32[256,128]{1,0:T(8,128)S(1)}, bf16[48,4,128,128]{3,2,1,0:T(8,128)(2,1)S(1)}, bf16[512,128]{1,0:T(8,128)(2,1)S(1...) custom-call(f32[8,32,128]{2,1,0:T(8,128)S(1)} %collective-permute-done.la, ...), custom_call_target="tpu_custom_call" | custom-call | bytes 7000000 | tf_op jit(solution)/shard_map/lon_pack/pallas_call | solution.py:268
  17.3 1.2 %collective-permute-start.5 = (f32[256,128]{1,0:T(8,128)S(1)}, f32[256,128]{1,0:T(8,128)S(1)}, u32[]{:S(2)}, u32[]{:S(2)}) collective-permute-start(f32[256,128]{1,0:T(8,128)S(1)} %get-tuple-element.71), channel_id=1, source_target_pairs={{4,8},{12,16},{20,24},{28,0},{8,4},{16,12},{24,20},{0,28},{5,9},{1... | collective-permute-start | bytes 393224 | tf_op jit(solution)/shard_map/ppermute | solution.py:600
  18.5 6.2 %surface.1 = (f32[4,128,128]{2,1,0:T(8,128)S(1)}, f32[1280,128]{1,0:T(8,128)S(1)}, f32[1280,128]{1,0:T(8,128)S(1)}) custom-call(s32[4,128]{1,0:T(4,128)S(1)} %fusion.2.after.slot, f32[57,128,128]{2,1,0:T(8,128)S(1)} %get-tuple-element.59.x, f32[8,32,128]{2,1,0:T(8,128)S(1)} %collective-permute-done.la, f32[8,32,128]{2,1,0:T(8,128)S(1)} %collective-permute-done.1.lb, ...), custom_call_target="tpu_custom_call" | custom-call | bytes 24500000 | tf_op jit(solution)/shard_map/surface/pallas_call | solution.py:540
  24.7 0.4 collective-permute-done.5.wb
  25.1 1.5 %collective-permute-done.4.wa = f32[256,128]{1,0:T(8,128)S(1)} collective-permute-done((f32[256,128]{1,0:T(8,128)S(1)}, f32[256,128]{1,0:T(8,128)S(1)}, u32[]{:S(2)}, u32[]{:S(2)}) %collective-permute-start.4) | collective-permute-done | bytes 131104 | tf_op jit(solution)/shard_map/ppermute | solution.py:601
  26.7 0.9 %collective-permute-start.6 = (f32[1280,128]{1,0:T(8,128)S(1)}, f32[1280,128]{1,0:T(8,128)S(1)}, u32[]{:S(2)}, u32[]{:S(2)}) collective-permute-start(f32[1280,128]{1,0:T(8,128)S(1)} %get-tuple-element.84), channel_id=1, source_target_pairs={{0,1},{1,0},{2,3},{3,2},{4,5},{5,4},{6,7},{7,6},{8,9},{9,8},{10,11... | collective-permute-start | bytes 1966088 | tf_op jit(solution)/shard_map/ppermute | solution.py:606
  27.5 2.4 %deep.3.refs_4_ = f32[4,8,128,128]{3,2,1,0:T(8,128)} custom-call(f32[57,128,128]{2,1,0:T(8,128)S(1)} %get-tuple-element.59.x, f32[8,32,128]{2,1,0:T(8,128)S(1)} %collective-permute-done.la, f32[8,32,128]{2,1,0:T(8,128)S(1)} %collective-permute-done.1.lb, f32[48,128]{1,0:T(8,128)S(1)} %collective-permute-done.2.wa.oa, ...), custom_call_target="tpu_custom_call" | custom-call | bytes 9100000 | tf_op jit(solution)/shard_map/deep/pallas_call | solution.py:582
  29.9 0.1 add.37
  30.1 2.2 %collective-permute-start.7 = (f32[320,128]{1,0:T(8,128)S(1)}, f32[320,128]{1,0:T(8,128)S(1)}, u32[]{:S(2)}, u32[]{:S(2)}) collective-permute-start(f32[320,128]{1,0:T(8,128)S(1)} %get-tuple-element.104), channel_id=1, source_target_pairs={{0,6},{1,7},{2,4},{3,5},{4,2},{5,3},{6,0},{7,1},{8,14},{9,15},{10,... | collective-permute-start | bytes 491528 | tf_op jit(solution)/shard_map/ppermute | solution.py:606
  32.2 0.2 collective-permute-start.8
  32.5 1.2 %collective-permute-start.9 = (f32[320,128]{1,0:T(8,128)S(1)}, f32[320,128]{1,0:T(8,128)S(1)}, u32[]{:S(2)}, u32[]{:S(2)}) collective-permute-start(f32[320,128]{1,0:T(8,128)S(1)} %get-tuple-element.102), channel_id=1, source_target_pairs={{0,2},{1,3},{2,0},{3,1},{4,6},{5,7},{6,4},{7,5},{8,10},{9,11},{10,... | collective-permute-start | bytes 491528 | tf_op jit(solution)/shard_map/ppermute | solution.py:606
  33.6 6.5 %deep.4.refs_4_ = f32[4,8,128,128]{3,2,1,0:T(8,128)} custom-call(f32[57,128,128]{2,1,0:T(8,128)S(1)} %get-tuple-element.59.x, f32[8,32,128]{2,1,0:T(8,128)S(1)} %collective-permute-done.la, f32[8,32,128]{2,1,0:T(8,128)S(1)} %collective-permute-done.1.lb, f32[48,128]{1,0:T(8,128)S(1)} %collective-permute-done.2.wa.oa, ...), custom_call_target="tpu_custom_call", output_to_operand_aliasing={{}: (11, {})} | custom-call | bytes 18200000 | tf_op jit(solution)/shard_map/deep/pallas_call | solution.py:582
  40.2 0.5 collective-permute-done.8
  40.7 3.2 %collective-permute-start.10 = (f32[80,128]{1,0:T(8,128)S(1)}, f32[80,128]{1,0:T(8,128)S(1)}, u32[]{:S(2)}, u32[]{:S(2)}) collective-permute-start(f32[80,128]{1,0:T(8,128)S(1)} %get-tuple-element.107), channel_id=1, source_target_pairs={{0,24},{1,25},{2,26},{3,27},{4,28},{5,29},{6,30},{7,31},{8,16},{9,... | collective-permute-start | bytes 122888 | tf_op jit(solution)/shard_map/ppermute | solution.py:606
  43.9 1.3 %collective-permute-start.12 = (f32[80,128]{1,0:T(8,128)S(1)}, f32[80,128]{1,0:T(8,128)S(1)}, u32[]{:S(2)}, u32[]{:S(2)}) collective-permute-start(f32[80,128]{1,0:T(8,128)S(1)} %get-tuple-element.105), channel_id=1, source_target_pairs={{0,8},{1,9},{2,10},{3,11},{4,12},{5,13},{6,14},{7,15},{8,0},{9,1},... | collective-permute-start | bytes 122888 | tf_op jit(solution)/shard_map/ppermute | solution.py:606
  45.2 3.8 %deep.5 = f32[4,8,128,128]{3,2,1,0:T(8,128)} custom-call(f32[57,128,128]{2,1,0:T(8,128)S(1)} %get-tuple-element.59.x, f32[8,32,128]{2,1,0:T(8,128)S(1)} %collective-permute-done.la, f32[8,32,128]{2,1,0:T(8,128)S(1)} %collective-permute-done.1.lb, f32[48,128]{1,0:T(8,128)S(1)} %collective-permute-done.2.wa.oa, ...), custom_call_target="tpu_custom_call", output_to_operand_aliasing={{}: (11, {})} | custom-call | bytes 9100000 | tf_op jit(solution)/shard_map/deep/pallas_call | solution.py:582
  48.9 0.6 %add_add_fusion.1 = f32[80,128]{1,0:T(8,128)} fusion(f32[80,128]{1,0:T(8,128)S(1)} %collective-permute-done.12, f32[80,128]{1,0:T(8,128)S(1)} %collective-permute-done.11, f32[80,128]{1,0:T(8,128)S(1)} %collective-permute-done.10, f32[320,128]{1,0:T(8,128)S(1)} %add_add_fusion), kind=kLoop, calls=%fused_computation.1 | loop fusion | flops 30720 | bytes 204800 | tf_op jit(solution)/shard_map/add | solution.py:665
  (18 shorter events, 0.1 us)
Async XLA Ops:
  0.6 2.3 %copy-start = (s32[128,1,4]{0,2,1:T(4,128)S(1)}, s32[128,1,4]{0,2,1:T(4,128)}, u32[]{:S(2)}) copy-start(s32[128,1,4]{0,2,1:T(4,128)} %param.11) | copy-start | bytes 6148
  1.8 5.3 %collective-permute-start = (f32[8,32,128]{2,1,0:T(8,128)S(1)}, f32[8,32,128]{2,1,0:T(8,128)S(1)}, u32[]{:S(2)}, u32[]{:S(2)}) collective-permute-start(f32[8,32,128]{2,1,0:T(8,128)S(1)} %get-tuple-element.52), channel_id=1, source_target_pairs={{0,1},{2,3},{1,0},{3,2},{4,5},{6,7},{5,4},{7,6},{8,9},{10,11},{9,8... | collective-permute-start | bytes 393224 | tf_op jit(solution)/shard_map/ppermute | solution.py:601
  2.3 4.8 %collective-permute-start.1 = (f32[8,32,128]{2,1,0:T(8,128)S(1)}, f32[8,32,128]{2,1,0:T(8,128)S(1)}, u32[]{:S(2)}, u32[]{:S(2)}) collective-permute-start(f32[8,32,128]{2,1,0:T(8,128)S(1)} %get-tuple-element.53), channel_id=1, source_target_pairs={{1,2},{2,1},{5,6},{6,5},{9,10},{10,9},{13,14},{14,13},{17,18},{18,... | collective-permute-start | bytes 393224 | tf_op jit(solution)/shard_map/ppermute | solution.py:600
  7.3 11.2 %collective-permute-start.2 = (f32[48,128]{1,0:T(8,128)S(1)}, f32[48,128]{1,0:T(8,128)S(1)}, u32[]{:S(2)}, u32[]{:S(2)}) collective-permute-start(f32[48,128]{1,0:T(8,128)S(1)} %get-tuple-element.60), channel_id=1, source_target_pairs={{0,4},{8,12},{16,20},{24,28},{4,0},{12,8},{20,16},{28,24},{1,5},{9... | collective-permute-start | bytes 73736 | tf_op jit(solution)/shard_map/ppermute | solution.py:601
  9.9 8.6 %collective-permute-start.3 = (f32[48,128]{1,0:T(8,128)S(1)}, f32[48,128]{1,0:T(8,128)S(1)}, u32[]{:S(2)}, u32[]{:S(2)}) collective-permute-start(f32[48,128]{1,0:T(8,128)S(1)} %get-tuple-element.61), channel_id=1, source_target_pairs={{4,8},{12,16},{20,24},{28,0},{8,4},{16,12},{24,20},{0,28},{5,9},{1... | collective-permute-start | bytes 73736 | tf_op jit(solution)/shard_map/ppermute | solution.py:600
  17.3 7.9 %collective-permute-start.5 = (f32[256,128]{1,0:T(8,128)S(1)}, f32[256,128]{1,0:T(8,128)S(1)}, u32[]{:S(2)}, u32[]{:S(2)}) collective-permute-start(f32[256,128]{1,0:T(8,128)S(1)} %get-tuple-element.71), channel_id=1, source_target_pairs={{4,8},{12,16},{20,24},{28,0},{8,4},{16,12},{24,20},{0,28},{5,9},{1... | collective-permute-start | bytes 393224 | tf_op jit(solution)/shard_map/ppermute | solution.py:600
  18.5 8.1 %collective-permute-start.4 = (f32[256,128]{1,0:T(8,128)S(1)}, f32[256,128]{1,0:T(8,128)S(1)}, u32[]{:S(2)}, u32[]{:S(2)}) collective-permute-start(f32[256,128]{1,0:T(8,128)S(1)} %get-tuple-element.70), channel_id=1, source_target_pairs={{0,4},{8,12},{16,20},{24,28},{4,0},{12,8},{20,16},{28,24},{1,5},{9... | collective-permute-start | bytes 393224 | tf_op jit(solution)/shard_map/ppermute | solution.py:601
  26.7 3.3 %collective-permute-start.6 = (f32[1280,128]{1,0:T(8,128)S(1)}, f32[1280,128]{1,0:T(8,128)S(1)}, u32[]{:S(2)}, u32[]{:S(2)}) collective-permute-start(f32[1280,128]{1,0:T(8,128)S(1)} %get-tuple-element.84), channel_id=1, source_target_pairs={{0,1},{1,0},{2,3},{3,2},{4,5},{5,4},{6,7},{7,6},{8,9},{9,8},{10,11... | collective-permute-start | bytes 1966088 | tf_op jit(solution)/shard_map/ppermute | solution.py:606
  30.1 10.1 %collective-permute-start.7 = (f32[320,128]{1,0:T(8,128)S(1)}, f32[320,128]{1,0:T(8,128)S(1)}, u32[]{:S(2)}, u32[]{:S(2)}) collective-permute-start(f32[320,128]{1,0:T(8,128)S(1)} %get-tuple-element.104), channel_id=1, source_target_pairs={{0,6},{1,7},{2,4},{3,5},{4,2},{5,3},{6,0},{7,1},{8,14},{9,15},{10,... | collective-permute-start | bytes 491528 | tf_op jit(solution)/shard_map/ppermute | solution.py:606
  32.2 8.4 %collective-permute-start.8 = (f32[320,128]{1,0:T(8,128)S(1)}, f32[320,128]{1,0:T(8,128)S(1)}, u32[]{:S(2)}, u32[]{:S(2)}) collective-permute-start(f32[320,128]{1,0:T(8,128)S(1)} %get-tuple-element.103), channel_id=1, source_target_pairs={{0,4},{1,5},{2,6},{3,7},{4,0},{5,1},{6,2},{7,3},{8,12},{9,13},{10,... | collective-permute-start | bytes 491528 | tf_op jit(solution)/shard_map/ppermute | solution.py:606
  32.5 8.2 %collective-permute-start.9 = (f32[320,128]{1,0:T(8,128)S(1)}, f32[320,128]{1,0:T(8,128)S(1)}, u32[]{:S(2)}, u32[]{:S(2)}) collective-permute-start(f32[320,128]{1,0:T(8,128)S(1)} %get-tuple-element.102), channel_id=1, source_target_pairs={{0,2},{1,3},{2,0},{3,1},{4,6},{5,7},{6,4},{7,5},{8,10},{9,11},{10,... | collective-permute-start | bytes 491528 | tf_op jit(solution)/shard_map/ppermute | solution.py:606
  40.7 8.2 %collective-permute-start.10 = (f32[80,128]{1,0:T(8,128)S(1)}, f32[80,128]{1,0:T(8,128)S(1)}, u32[]{:S(2)}, u32[]{:S(2)}) collective-permute-start(f32[80,128]{1,0:T(8,128)S(1)} %get-tuple-element.107), channel_id=1, source_target_pairs={{0,24},{1,25},{2,26},{3,27},{4,28},{5,29},{6,30},{7,31},{8,16},{9,... | collective-permute-start | bytes 122888 | tf_op jit(solution)/shard_map/ppermute | solution.py:606
  43.9 5.0 %collective-permute-start.11 = (f32[80,128]{1,0:T(8,128)S(1)}, f32[80,128]{1,0:T(8,128)S(1)}, u32[]{:S(2)}, u32[]{:S(2)}) collective-permute-start(f32[80,128]{1,0:T(8,128)S(1)} %get-tuple-element.106), channel_id=1, source_target_pairs={{0,16},{1,17},{2,18},{3,19},{4,20},{5,21},{6,22},{7,23},{8,24},{9,... | collective-permute-start | bytes 122888 | tf_op jit(solution)/shard_map/ppermute | solution.py:606
  43.9 5.0 %collective-permute-start.12 = (f32[80,128]{1,0:T(8,128)S(1)}, f32[80,128]{1,0:T(8,128)S(1)}, u32[]{:S(2)}, u32[]{:S(2)}) collective-permute-start(f32[80,128]{1,0:T(8,128)S(1)} %get-tuple-element.105), channel_id=1, source_target_pairs={{0,8},{1,9},{2,10},{3,11},{4,12},{5,13},{6,14},{7,15},{8,0},{9,1},... | collective-permute-start | bytes 122888 | tf_op jit(solution)/shard_map/ppermute | solution.py:606

commit v5 on v4

--- a/solution.py
+++ b/solution.py
@@ -477,7 +477,7 @@
     lat, lon = (la, lb), (wa, wb, 0)
     set_faces(x, levels, lat, lon, tables, scratch)
     ocean = x[field_index(FIELDS - 1, 0, levels)]
-    for i, done in enumerate(run_level(0, x, levels, lat, lon, tables, scratch, 3)):
+    for i, done in enumerate(run_level(0, x, levels, lat, lon, tables, scratch, 2)):
         out_q[i] = done
         surf[pl.ds(i, rows, stride=8), :] = done * ocean
     surf[pl.ds(NTR, rows, stride=8), :] = ocean

time: 49.8 us -> 49.8 us (level)
  no operation moved by 1% of the time
where the time goes in v5:
time: 49.8 us; the launch traced here: 49.6 us
  Pallas kernels  28 us (56%)
  starting transfers between devices  17.4 us (35%)
  waiting for transfers between devices  2.57 us (5%)
  other arithmetic  0.76 us (2%)
  between operations  0.76 us (2%)
    pallas_call x3, Pallas kernels, deep(): pl.pallas_call(functools.partial(deep_kernel, first, levels), grid=(count...  12.7 us
    ppermute x7, starting transfers between devices, partner(): return lax.ppermute(a, AXES, [(i, i ^ mask) for i in range(n)])  8.86 us
    pallas_call x1, Pallas kernels, surface(): pl.pallas_call(functools.partial(surface_kernel, order, accs, levels), in...  6.07 us
    ppermute x3, starting transfers between devices, swap(): second = lax.ppermute(second, axis, odd + [(j, i) for i, j in odd])  5.44 us
    pallas_call x2, Pallas kernels, lon_pack(): pl.pallas_call(kernel, in_specs=[WHOLE] * 3 + [pl.BlockSpec(memory_space=...  4.05 us
    pallas_call x1, Pallas kernels, fetch(): pl.pallas_call(fetch_kernel, in_specs=[pl.BlockSpec(memory_space=pl.ANY)]...  4.03 us
    ppermute x3, starting transfers between devices, swap(): first = lax.ppermute(first, axis, even + [(j, i) for i, j in even])  3.13 us
    ppermute x3, waiting for transfers between devices, swap(): first = lax.ppermute(first, axis, even + [(j, i) for i, j in even])  1.52 us
  transfers between devices with their start and end apart: 13, of which 3 were waited for; matrix products, arithmetic and copies ran while one was open for 0% of the time, Pallas kernels for 54%

profile of v5, /device:TPU:0, one launch (start us, length us, event | category | flops | bytes accessed | tf_op | source)
XLA Modules:
  0.0 49.6 jit_solution(17561781218242757711)
XLA Ops:
  0.6 1.1 %lat_pack.1 = (f32[8,32,128]{2,1,0:T(8,128)S(1)}, f32[8,32,128]{2,1,0:T(8,128)S(1)}) custom-call(f32[4,8,128,128]{3,2,1,0:T(8,128)} %t.1, f32[2,8,128,128]{3,2,1,0:T(8,128)} %v.1, f32[8,128,128]{2,1,0:T(8,128)} %m.1, s32[128,128]{1,0:T(8,128)} %o.1, f32[4,8,128,128]{3,2,1,0:T(8,128)} %t.1, f32[2,8,128,128]{3,2,1,0:T(8,128)} %v.1, f32[8,128,128]{2,1,0:T(8,128)} %m.1, ...), custom_call_target="tpu_custom_call" | custom-call | bytes 7000000 | tf_op jit(solution)/shard_map/lat_pack/pallas_call | solution.py:86
  1.8 0.5 %collective-permute-start = (f32[8,32,128]{2,1,0:T(8,128)S(1)}, f32[8,32,128]{2,1,0:T(8,128)S(1)}, u32[]{:S(2)}, u32[]{:S(2)}) collective-permute-start(f32[8,32,128]{2,1,0:T(8,128)S(1)} %get-tuple-element.52), channel_id=1, source_target_pairs={{0,1},{2,3},{1,0},{3,2},{4,5},{6,7},{5,4},{7,6},{8,9},{10,11},{9,8... | collective-permute-start | bytes 393224 | tf_op jit(solution)/shard_map/ppermute | solution.py:601
  2.3 0.7 %collective-permute-start.1 = (f32[8,32,128]{2,1,0:T(8,128)S(1)}, f32[8,32,128]{2,1,0:T(8,128)S(1)}, u32[]{:S(2)}, u32[]{:S(2)}) collective-permute-start(f32[8,32,128]{2,1,0:T(8,128)S(1)} %get-tuple-element.53), channel_id=1, source_target_pairs={{1,2},{2,1},{5,6},{6,5},{9,10},{10,9},{13,14},{14,13},{17,18},{18,... | collective-permute-start | bytes 393224 | tf_op jit(solution)/shard_map/ppermute | solution.py:600
  3.0 4.0 %fetch.1 = (f32[57,128,128]{2,1,0:T(8,128)S(1)}, bf16[48,4,128,128]{3,2,1,0:T(8,128)(2,1)S(1)}) custom-call(s32[4,128]{1,0:T(4,128)S(1)} %fusion.2.after.slot, f32[4,8,128,128]{3,2,1,0:T(8,128)} %t.1, f32[2,8,128,128]{3,2,1,0:T(8,128)} %v.1, f32[8,128,128]{2,1,0:T(8,128)} %m.1, s32[128,128]{1,0:T(8,128)} %o.1, bf16[128,4,128,128]{3,2,1,0:T(8,128)(2,1)} %refs_6_.1), custom_call_target="tpu_custom_call" | custom-call | bytes 10500000 | tf_op jit(solution)/shard_map/fetch/pallas_call | solution.py:224
  7.0 0.2 lon_pack.2
  7.3 2.6 %collective-permute-start.2 = (f32[48,128]{1,0:T(8,128)S(1)}, f32[48,128]{1,0:T(8,128)S(1)}, u32[]{:S(2)}, u32[]{:S(2)}) collective-permute-start(f32[48,128]{1,0:T(8,128)S(1)} %get-tuple-element.60), channel_id=1, source_target_pairs={{0,4},{8,12},{16,20},{24,28},{4,0},{12,8},{20,16},{28,24},{1,5},{9... | collective-permute-start | bytes 73736 | tf_op jit(solution)/shard_map/ppermute | solution.py:601
  9.9 3.5 %collective-permute-start.3 = (f32[48,128]{1,0:T(8,128)S(1)}, f32[48,128]{1,0:T(8,128)S(1)}, u32[]{:S(2)}, u32[]{:S(2)}) collective-permute-start(f32[48,128]{1,0:T(8,128)S(1)} %get-tuple-element.61), channel_id=1, source_target_pairs={{4,8},{12,16},{20,24},{28,0},{8,4},{16,12},{24,20},{0,28},{5,9},{1... | collective-permute-start | bytes 73736 | tf_op jit(solution)/shard_map/ppermute | solution.py:600
  13.4 3.8 %lon_pack.3 = (f32[256,128]{1,0:T(8,128)S(1)}, f32[256,128]{1,0:T(8,128)S(1)}, bf16[48,4,128,128]{3,2,1,0:T(8,128)(2,1)S(1)}, bf16[512,128]{1,0:T(8,128)(2,1)S(1...) custom-call(f32[8,32,128]{2,1,0:T(8,128)S(1)} %collective-permute-done.la, ...), custom_call_target="tpu_custom_call" | custom-call | bytes 7000000 | tf_op jit(solution)/shard_map/lon_pack/pallas_call | solution.py:268
  17.3 1.2 %collective-permute-start.5 = (f32[256,128]{1,0:T(8,128)S(1)}, f32[256,128]{1,0:T(8,128)S(1)}, u32[]{:S(2)}, u32[]{:S(2)}) collective-permute-start(f32[256,128]{1,0:T(8,128)S(1)} %get-tuple-element.71), channel_id=1, source_target_pairs={{4,8},{12,16},{20,24},{28,0},{8,4},{16,12},{24,20},{0,28},{5,9},{1... | collective-permute-start | bytes 393224 | tf_op jit(solution)/shard_map/ppermute | solution.py:600
  18.5 6.1 %surface.1 = (f32[4,128,128]{2,1,0:T(8,128)S(1)}, f32[1280,128]{1,0:T(8,128)S(1)}, f32[1280,128]{1,0:T(8,128)S(1)}) custom-call(s32[4,128]{1,0:T(4,128)S(1)} %fusion.2.after.slot, f32[57,128,128]{2,1,0:T(8,128)S(1)} %get-tuple-element.59.x, f32[8,32,128]{2,1,0:T(8,128)S(1)} %collective-permute-done.la, f32[8,32,128]{2,1,0:T(8,128)S(1)} %collective-permute-done.1.lb, ...), custom_call_target="tpu_custom_call" | custom-call | bytes 24500000 | tf_op jit(solution)/shard_map/surface/pallas_call | solution.py:540
  24.6 0.5 %collective-permute-done.5.wb = f32[256,128]{1,0:T(8,128)S(1)} collective-permute-done((f32[256,128]{1,0:T(8,128)S(1)}, f32[256,128]{1,0:T(8,128)S(1)}, u32[]{:S(2)}, u32[]{:S(2)}) %collective-permute-start.5) | collective-permute-done | bytes 131104 | tf_op jit(solution)/shard_map/ppermute | solution.py:600
  25.1 1.5 %collective-permute-done.4.wa = f32[256,128]{1,0:T(8,128)S(1)} collective-permute-done((f32[256,128]{1,0:T(8,128)S(1)}, f32[256,128]{1,0:T(8,128)S(1)}, u32[]{:S(2)}, u32[]{:S(2)}) %collective-permute-start.4) | collective-permute-done | bytes 131104 | tf_op jit(solution)/shard_map/ppermute | solution.py:601
  26.7 0.9 %collective-permute-start.6 = (f32[1280,128]{1,0:T(8,128)S(1)}, f32[1280,128]{1,0:T(8,128)S(1)}, u32[]{:S(2)}, u32[]{:S(2)}) collective-permute-start(f32[1280,128]{1,0:T(8,128)S(1)} %get-tuple-element.84), channel_id=1, source_target_pairs={{0,1},{1,0},{2,3},{3,2},{4,5},{5,4},{6,7},{7,6},{8,9},{9,8},{10,11... | collective-permute-start | bytes 1966088 | tf_op jit(solution)/shard_map/ppermute | solution.py:606
  27.5 2.4 %deep.3.refs_4_ = f32[4,8,128,128]{3,2,1,0:T(8,128)} custom-call(f32[57,128,128]{2,1,0:T(8,128)S(1)} %get-tuple-element.59.x, f32[8,32,128]{2,1,0:T(8,128)S(1)} %collective-permute-done.la, f32[8,32,128]{2,1,0:T(8,128)S(1)} %collective-permute-done.1.lb, f32[48,128]{1,0:T(8,128)S(1)} %collective-permute-done.2.wa.oa, ...), custom_call_target="tpu_custom_call" | custom-call | bytes 9100000 | tf_op jit(solution)/shard_map/deep/pallas_call | solution.py:582
  29.9 0.1 add.37
  30.1 2.1 %collective-permute-start.7 = (f32[320,128]{1,0:T(8,128)S(1)}, f32[320,128]{1,0:T(8,128)S(1)}, u32[]{:S(2)}, u32[]{:S(2)}) collective-permute-start(f32[320,128]{1,0:T(8,128)S(1)} %get-tuple-element.104), channel_id=1, source_target_pairs={{0,6},{1,7},{2,4},{3,5},{4,2},{5,3},{6,0},{7,1},{8,14},{9,15},{10,... | collective-permute-start | bytes 491528 | tf_op jit(solution)/shard_map/ppermute | solution.py:606
  32.2 0.3 collective-permute-start.8
  32.5 1.2 %collective-permute-start.9 = (f32[320,128]{1,0:T(8,128)S(1)}, f32[320,128]{1,0:T(8,128)S(1)}, u32[]{:S(2)}, u32[]{:S(2)}) collective-permute-start(f32[320,128]{1,0:T(8,128)S(1)} %get-tuple-element.102), channel_id=1, source_target_pairs={{0,2},{1,3},{2,0},{3,1},{4,6},{5,7},{6,4},{7,5},{8,10},{9,11},{10,... | collective-permute-start | bytes 491528 | tf_op jit(solution)/shard_map/ppermute | solution.py:606
  33.6 6.5 %deep.4.refs_4_ = f32[4,8,128,128]{3,2,1,0:T(8,128)} custom-call(f32[57,128,128]{2,1,0:T(8,128)S(1)} %get-tuple-element.59.x, f32[8,32,128]{2,1,0:T(8,128)S(1)} %collective-permute-done.la, f32[8,32,128]{2,1,0:T(8,128)S(1)} %collective-permute-done.1.lb, f32[48,128]{1,0:T(8,128)S(1)} %collective-permute-done.2.wa.oa, ...), custom_call_target="tpu_custom_call", output_to_operand_aliasing={{}: (11, {})} | custom-call | bytes 18200000 | tf_op jit(solution)/shard_map/deep/pallas_call | solution.py:582
  40.2 0.5 collective-permute-done.8
  40.7 3.1 %collective-permute-start.10 = (f32[80,128]{1,0:T(8,128)S(1)}, f32[80,128]{1,0:T(8,128)S(1)}, u32[]{:S(2)}, u32[]{:S(2)}) collective-permute-start(f32[80,128]{1,0:T(8,128)S(1)} %get-tuple-element.107), channel_id=1, source_target_pairs={{0,24},{1,25},{2,26},{3,27},{4,28},{5,29},{6,30},{7,31},{8,16},{9,... | collective-permute-start | bytes 122888 | tf_op jit(solution)/shard_map/ppermute | solution.py:606
  43.8 1.3 %collective-permute-start.12 = (f32[80,128]{1,0:T(8,128)S(1)}, f32[80,128]{1,0:T(8,128)S(1)}, u32[]{:S(2)}, u32[]{:S(2)}) collective-permute-start(f32[80,128]{1,0:T(8,128)S(1)} %get-tuple-element.105), channel_id=1, source_target_pairs={{0,8},{1,9},{2,10},{3,11},{4,12},{5,13},{6,14},{7,15},{8,0},{9,1},... | collective-permute-start | bytes 122888 | tf_op jit(solution)/shard_map/ppermute | solution.py:606
  45.2 3.8 %deep.5 = f32[4,8,128,128]{3,2,1,0:T(8,128)} custom-call(f32[57,128,128]{2,1,0:T(8,128)S(1)} %get-tuple-element.59.x, f32[8,32,128]{2,1,0:T(8,128)S(1)} %collective-permute-done.la, f32[8,32,128]{2,1,0:T(8,128)S(1)} %collective-permute-done.1.lb, f32[48,128]{1,0:T(8,128)S(1)} %collective-permute-done.2.wa.oa, ...), custom_call_target="tpu_custom_call", output_to_operand_aliasing={{}: (11, {})} | custom-call | bytes 9100000 | tf_op jit(solution)/shard_map/deep/pallas_call | solution.py:582
  48.9 0.6 %add_add_fusion.1 = f32[80,128]{1,0:T(8,128)} fusion(f32[80,128]{1,0:T(8,128)S(1)} %collective-permute-done.12, f32[80,128]{1,0:T(8,128)S(1)} %collective-permute-done.11, f32[80,128]{1,0:T(8,128)S(1)} %collective-permute-done.10, f32[320,128]{1,0:T(8,128)S(1)} %add_add_fusion), kind=kLoop, calls=%fused_computation.1 | loop fusion | flops 30720 | bytes 204800 | tf_op jit(solution)/shard_map/add | solution.py:665
  (18 shorter events, 0.1 us)
Async XLA Ops:
  0.6 2.3 %copy-start = (s32[128,1,4]{0,2,1:T(4,128)S(1)}, s32[128,1,4]{0,2,1:T(4,128)}, u32[]{:S(2)}) copy-start(s32[128,1,4]{0,2,1:T(4,128)} %param.11) | copy-start | bytes 6148
  1.8 5.3 %collective-permute-start = (f32[8,32,128]{2,1,0:T(8,128)S(1)}, f32[8,32,128]{2,1,0:T(8,128)S(1)}, u32[]{:S(2)}, u32[]{:S(2)}) collective-permute-start(f32[8,32,128]{2,1,0:T(8,128)S(1)} %get-tuple-element.52), channel_id=1, source_target_pairs={{0,1},{2,3},{1,0},{3,2},{4,5},{6,7},{5,4},{7,6},{8,9},{10,11},{9,8... | collective-permute-start | bytes 393224 | tf_op jit(solution)/shard_map/ppermute | solution.py:601
  2.3 4.8 %collective-permute-start.1 = (f32[8,32,128]{2,1,0:T(8,128)S(1)}, f32[8,32,128]{2,1,0:T(8,128)S(1)}, u32[]{:S(2)}, u32[]{:S(2)}) collective-permute-start(f32[8,32,128]{2,1,0:T(8,128)S(1)} %get-tuple-element.53), channel_id=1, source_target_pairs={{1,2},{2,1},{5,6},{6,5},{9,10},{10,9},{13,14},{14,13},{17,18},{18,... | collective-permute-start | bytes 393224 | tf_op jit(solution)/shard_map/ppermute | solution.py:600
  7.3 11.2 %collective-permute-start.2 = (f32[48,128]{1,0:T(8,128)S(1)}, f32[48,128]{1,0:T(8,128)S(1)}, u32[]{:S(2)}, u32[]{:S(2)}) collective-permute-start(f32[48,128]{1,0:T(8,128)S(1)} %get-tuple-element.60), channel_id=1, source_target_pairs={{0,4},{8,12},{16,20},{24,28},{4,0},{12,8},{20,16},{28,24},{1,5},{9... | collective-permute-start | bytes 73736 | tf_op jit(solution)/shard_map/ppermute | solution.py:601
  9.9 8.6 %collective-permute-start.3 = (f32[48,128]{1,0:T(8,128)S(1)}, f32[48,128]{1,0:T(8,128)S(1)}, u32[]{:S(2)}, u32[]{:S(2)}) collective-permute-start(f32[48,128]{1,0:T(8,128)S(1)} %get-tuple-element.61), channel_id=1, source_target_pairs={{4,8},{12,16},{20,24},{28,0},{8,4},{16,12},{24,20},{0,28},{5,9},{1... | collective-permute-start | bytes 73736 | tf_op jit(solution)/shard_map/ppermute | solution.py:600
  17.3 7.9 %collective-permute-start.5 = (f32[256,128]{1,0:T(8,128)S(1)}, f32[256,128]{1,0:T(8,128)S(1)}, u32[]{:S(2)}, u32[]{:S(2)}) collective-permute-start(f32[256,128]{1,0:T(8,128)S(1)} %get-tuple-element.71), channel_id=1, source_target_pairs={{4,8},{12,16},{20,24},{28,0},{8,4},{16,12},{24,20},{0,28},{5,9},{1... | collective-permute-start | bytes 393224 | tf_op jit(solution)/shard_map/ppermute | solution.py:600
  18.5 8.1 %collective-permute-start.4 = (f32[256,128]{1,0:T(8,128)S(1)}, f32[256,128]{1,0:T(8,128)S(1)}, u32[]{:S(2)}, u32[]{:S(2)}) collective-permute-start(f32[256,128]{1,0:T(8,128)S(1)} %get-tuple-element.70), channel_id=1, source_target_pairs={{0,4},{8,12},{16,20},{24,28},{4,0},{12,8},{20,16},{28,24},{1,5},{9... | collective-permute-start | bytes 393224 | tf_op jit(solution)/shard_map/ppermute | solution.py:601
  26.7 3.3 %collective-permute-start.6 = (f32[1280,128]{1,0:T(8,128)S(1)}, f32[1280,128]{1,0:T(8,128)S(1)}, u32[]{:S(2)}, u32[]{:S(2)}) collective-permute-start(f32[1280,128]{1,0:T(8,128)S(1)} %get-tuple-element.84), channel_id=1, source_target_pairs={{0,1},{1,0},{2,3},{3,2},{4,5},{5,4},{6,7},{7,6},{8,9},{9,8},{10,11... | collective-permute-start | bytes 1966088 | tf_op jit(solution)/shard_map/ppermute | solution.py:606
  30.1 10.1 %collective-permute-start.7 = (f32[320,128]{1,0:T(8,128)S(1)}, f32[320,128]{1,0:T(8,128)S(1)}, u32[]{:S(2)}, u32[]{:S(2)}) collective-permute-start(f32[320,128]{1,0:T(8,128)S(1)} %get-tuple-element.104), channel_id=1, source_target_pairs={{0,6},{1,7},{2,4},{3,5},{4,2},{5,3},{6,0},{7,1},{8,14},{9,15},{10,... | collective-permute-start | bytes 491528 | tf_op jit(solution)/shard_map/ppermute | solution.py:606
  32.2 8.5 %collective-permute-start.8 = (f32[320,128]{1,0:T(8,128)S(1)}, f32[320,128]{1,0:T(8,128)S(1)}, u32[]{:S(2)}, u32[]{:S(2)}) collective-permute-start(f32[320,128]{1,0:T(8,128)S(1)} %get-tuple-element.103), channel_id=1, source_target_pairs={{0,4},{1,5},{2,6},{3,7},{4,0},{5,1},{6,2},{7,3},{8,12},{9,13},{10,... | collective-permute-start | bytes 491528 | tf_op jit(solution)/shard_map/ppermute | solution.py:606
  32.5 8.2 %collective-permute-start.9 = (f32[320,128]{1,0:T(8,128)S(1)}, f32[320,128]{1,0:T(8,128)S(1)}, u32[]{:S(2)}, u32[]{:S(2)}) collective-permute-start(f32[320,128]{1,0:T(8,128)S(1)} %get-tuple-element.102), channel_id=1, source_target_pairs={{0,2},{1,3},{2,0},{3,1},{4,6},{5,7},{6,4},{7,5},{8,10},{9,11},{10,... | collective-permute-start | bytes 491528 | tf_op jit(solution)/shard_map/ppermute | solution.py:606
  40.7 8.2 %collective-permute-start.10 = (f32[80,128]{1,0:T(8,128)S(1)}, f32[80,128]{1,0:T(8,128)S(1)}, u32[]{:S(2)}, u32[]{:S(2)}) collective-permute-start(f32[80,128]{1,0:T(8,128)S(1)} %get-tuple-element.107), channel_id=1, source_target_pairs={{0,24},{1,25},{2,26},{3,27},{4,28},{5,29},{6,30},{7,31},{8,16},{9,... | collective-permute-start | bytes 122888 | tf_op jit(solution)/shard_map/ppermute | solution.py:606
  43.8 5.1 %collective-permute-start.11 = (f32[80,128]{1,0:T(8,128)S(1)}, f32[80,128]{1,0:T(8,128)S(1)}, u32[]{:S(2)}, u32[]{:S(2)}) collective-permute-start(f32[80,128]{1,0:T(8,128)S(1)} %get-tuple-element.106), channel_id=1, source_target_pairs={{0,16},{1,17},{2,18},{3,19},{4,20},{5,21},{6,22},{7,23},{8,24},{9,... | collective-permute-start | bytes 122888 | tf_op jit(solution)/shard_map/ppermute | solution.py:606
  43.8 5.1 %collective-permute-start.12 = (f32[80,128]{1,0:T(8,128)S(1)}, f32[80,128]{1,0:T(8,128)S(1)}, u32[]{:S(2)}, u32[]{:S(2)}) collective-permute-start(f32[80,128]{1,0:T(8,128)S(1)} %get-tuple-element.105), channel_id=1, source_target_pairs={{0,8},{1,9},{2,10},{3,11},{4,12},{5,13},{6,14},{7,15},{8,0},{9,1},... | collective-permute-start | bytes 122888 | tf_op jit(solution)/shard_map/ppermute | solution.py:606

commit v6 on v4

--- a/solution.py
+++ b/solution.py
@@ -12,7 +12,7 @@
 NTR = 4
 FIELDS = 8
 OFF = 16
-FIRST, SECOND = 3, 3
+FIRST, SECOND = 4, 2
 COUNT = 2
 UNIT = 16
 AXES = ("gx", "gy")
@@ -517,7 +517,7 @@
         if w is w_last:
             copy.wait()
         pairs = w.shape[0] // 2
-        lax.fori_loop(0, pairs, functools.partial(body, w, start), 0, unroll=8)
+        lax.fori_loop(0, pairs, functools.partial(body, w, start), 0, unroll=16)
         start += pairs
     chunk = ABD * (NTR + 1)
     half = len(order) // 2

time: 49.8 us -> 49.8 us (level)
  Pallas kernels: 28.1 us -> 27.6 us
    pallas_call x2, Pallas kernels: 4.05 us -> 3.45 us  [lon_pack(): pl.pallas_call(kernel, in_specs=[WHOLE] * 3 + [pl.BlockSpec(memory_space=...]
    pallas_call x1, Pallas kernels: 4.03 us -> 4.63 us  [fetch(): pl.pallas_call(fetch_kernel, in_specs=[pl.BlockSpec(memory_space=pl.ANY)]...]
  transfers between devices with their start and end apart: 13 -> 13, of which waited for: 3 -> 3; matrix products, arithmetic and copies ran while one was open for 0% -> 0% of each run, Pallas kernels for 54% -> 53%
where the time goes in v6:
time: 49.8 us; the launch traced here: 49.6 us
  Pallas kernels  27.6 us (55%)
  starting transfers between devices  17.4 us (35%)
  waiting for transfers between devices  2.95 us (6%)
  other arithmetic  0.76 us (2%)
  between operations  0.76 us (2%)
    pallas_call x3, Pallas kernels, deep(): pl.pallas_call(functools.partial(deep_kernel, first, levels), grid=(count...  12.7 us
    ppermute x7, starting transfers between devices, partner(): return lax.ppermute(a, AXES, [(i, i ^ mask) for i in range(n)])  8.86 us
    pallas_call x1, Pallas kernels, surface(): pl.pallas_call(functools.partial(surface_kernel, order, accs, levels), in...  5.69 us
    ppermute x3, starting transfers between devices, swap(): second = lax.ppermute(second, axis, odd + [(j, i) for i, j in odd])  5.44 us
    pallas_call x1, Pallas kernels, fetch(): pl.pallas_call(fetch_kernel, in_specs=[pl.BlockSpec(memory_space=pl.ANY)]...  4.63 us
    pallas_call x2, Pallas kernels, lon_pack(): pl.pallas_call(kernel, in_specs=[WHOLE] * 3 + [pl.BlockSpec(memory_space=...  3.45 us
    ppermute x3, starting transfers between devices, swap(): first = lax.ppermute(first, axis, even + [(j, i) for i, j in even])  3.13 us
    ppermute x3, waiting for transfers between devices, swap(): first = lax.ppermute(first, axis, even + [(j, i) for i, j in even])  1.52 us
  transfers between devices with their start and end apart: 13, of which 3 were waited for; matrix products, arithmetic and copies ran while one was open for 0% of the time, Pallas kernels for 53%

profile of v6, /device:TPU:0, one launch (start us, length us, event | category | flops | bytes accessed | tf_op | source)
XLA Modules:
  0.0 49.6 jit_solution(6650181391766254642)
XLA Ops:
  0.6 1.1 %lat_pack.1 = (f32[8,32,128]{2,1,0:T(8,128)S(1)}, f32[8,32,128]{2,1,0:T(8,128)S(1)}) custom-call(f32[4,8,128,128]{3,2,1,0:T(8,128)} %t.1, f32[2,8,128,128]{3,2,1,0:T(8,128)} %v.1, f32[8,128,128]{2,1,0:T(8,128)} %m.1, s32[128,128]{1,0:T(8,128)} %o.1, f32[4,8,128,128]{3,2,1,0:T(8,128)} %t.1, f32[2,8,128,128]{3,2,1,0:T(8,128)} %v.1, f32[8,128,128]{2,1,0:T(8,128)} %m.1, ...), custom_call_target="tpu_custom_call" | custom-call | bytes 7000000 | tf_op jit(solution)/shard_map/lat_pack/pallas_call | solution.py:86
  1.8 0.5 %collective-permute-start = (f32[8,32,128]{2,1,0:T(8,128)S(1)}, f32[8,32,128]{2,1,0:T(8,128)S(1)}, u32[]{:S(2)}, u32[]{:S(2)}) collective-permute-start(f32[8,32,128]{2,1,0:T(8,128)S(1)} %get-tuple-element.52), channel_id=1, source_target_pairs={{0,1},{2,3},{1,0},{3,2},{4,5},{6,7},{5,4},{7,6},{8,9},{10,11},{9,8... | collective-permute-start | bytes 393224 | tf_op jit(solution)/shard_map/ppermute | solution.py:601
  2.3 0.7 %collective-permute-start.1 = (f32[8,32,128]{2,1,0:T(8,128)S(1)}, f32[8,32,128]{2,1,0:T(8,128)S(1)}, u32[]{:S(2)}, u32[]{:S(2)}) collective-permute-start(f32[8,32,128]{2,1,0:T(8,128)S(1)} %get-tuple-element.53), channel_id=1, source_target_pairs={{1,2},{2,1},{5,6},{6,5},{9,10},{10,9},{13,14},{14,13},{17,18},{18,... | collective-permute-start | bytes 393224 | tf_op jit(solution)/shard_map/ppermute | solution.py:600
  3.0 4.6 %fetch.1 = (f32[57,128,128]{2,1,0:T(8,128)S(1)}, bf16[64,4,128,128]{3,2,1,0:T(8,128)(2,1)S(1)}) custom-call(s32[4,128]{1,0:T(4,128)S(1)} %fusion.2.after.slot, f32[4,8,128,128]{3,2,1,0:T(8,128)} %t.1, f32[2,8,128,128]{3,2,1,0:T(8,128)} %v.1, f32[8,128,128]{2,1,0:T(8,128)} %m.1, s32[128,128]{1,0:T(8,128)} %o.1, bf16[128,4,128,128]{3,2,1,0:T(8,128)(2,1)} %refs_6_.1), custom_call_target="tpu_custom_call" | custom-call | bytes 10500000 | tf_op jit(solution)/shard_map/fetch/pallas_call | solution.py:224
  7.6 0.2 lon_pack.2
  7.9 2.6 %collective-permute-start.2 = (f32[48,128]{1,0:T(8,128)S(1)}, f32[48,128]{1,0:T(8,128)S(1)}, u32[]{:S(2)}, u32[]{:S(2)}) collective-permute-start(f32[48,128]{1,0:T(8,128)S(1)} %get-tuple-element.60), channel_id=1, source_target_pairs={{0,4},{8,12},{16,20},{24,28},{4,0},{12,8},{20,16},{28,24},{1,5},{9... | collective-permute-start | bytes 73736 | tf_op jit(solution)/shard_map/ppermute | solution.py:601
  10.5 3.5 %collective-permute-start.3 = (f32[48,128]{1,0:T(8,128)S(1)}, f32[48,128]{1,0:T(8,128)S(1)}, u32[]{:S(2)}, u32[]{:S(2)}) collective-permute-start(f32[48,128]{1,0:T(8,128)S(1)} %get-tuple-element.61), channel_id=1, source_target_pairs={{4,8},{12,16},{20,24},{28,0},{8,4},{16,12},{24,20},{0,28},{5,9},{1... | collective-permute-start | bytes 73736 | tf_op jit(solution)/shard_map/ppermute | solution.py:600
  14.0 3.2 %lon_pack.3 = (f32[256,128]{1,0:T(8,128)S(1)}, f32[256,128]{1,0:T(8,128)S(1)}, bf16[32,4,128,128]{3,2,1,0:T(8,128)(2,1)S(1)}, bf16[512,128]{1,0:T(8,128)(2,1)S(1...) custom-call(f32[8,32,128]{2,1,0:T(8,128)S(1)} %collective-permute-done.la, ...), custom_call_target="tpu_custom_call" | custom-call | bytes 7000000 | tf_op jit(solution)/shard_map/lon_pack/pallas_call | solution.py:268
  17.3 1.2 %collective-permute-start.5 = (f32[256,128]{1,0:T(8,128)S(1)}, f32[256,128]{1,0:T(8,128)S(1)}, u32[]{:S(2)}, u32[]{:S(2)}) collective-permute-start(f32[256,128]{1,0:T(8,128)S(1)} %get-tuple-element.71), channel_id=1, source_target_pairs={{4,8},{12,16},{20,24},{28,0},{8,4},{16,12},{24,20},{0,28},{5,9},{1... | collective-permute-start | bytes 393224 | tf_op jit(solution)/shard_map/ppermute | solution.py:600
  18.5 5.7 %surface.1 = (f32[4,128,128]{2,1,0:T(8,128)S(1)}, f32[1280,128]{1,0:T(8,128)S(1)}, f32[1280,128]{1,0:T(8,128)S(1)}) custom-call(s32[4,128]{1,0:T(4,128)S(1)} %fusion.2.after.slot, f32[57,128,128]{2,1,0:T(8,128)S(1)} %get-tuple-element.59.x, f32[8,32,128]{2,1,0:T(8,128)S(1)} %collective-permute-done.la, f32[8,32,128]{2,1,0:T(8,128)S(1)} %collective-permute-done.1.lb, ...), custom_call_target="tpu_custom_call" | custom-call | bytes 24500000 | tf_op jit(solution)/shard_map/surface/pallas_call | solution.py:540
  24.2 0.9 %collective-permute-done.5.wb = f32[256,128]{1,0:T(8,128)S(1)} collective-permute-done((f32[256,128]{1,0:T(8,128)S(1)}, f32[256,128]{1,0:T(8,128)S(1)}, u32[]{:S(2)}, u32[]{:S(2)}) %collective-permute-start.5) | collective-permute-done | bytes 131104 | tf_op jit(solution)/shard_map/ppermute | solution.py:600
  25.1 1.5 %collective-permute-done.4.wa = f32[256,128]{1,0:T(8,128)S(1)} collective-permute-done((f32[256,128]{1,0:T(8,128)S(1)}, f32[256,128]{1,0:T(8,128)S(1)}, u32[]{:S(2)}, u32[]{:S(2)}) %collective-permute-start.4) | collective-permute-done | bytes 131104 | tf_op jit(solution)/shard_map/ppermute | solution.py:601
  26.7 0.9 %collective-permute-start.6 = (f32[1280,128]{1,0:T(8,128)S(1)}, f32[1280,128]{1,0:T(8,128)S(1)}, u32[]{:S(2)}, u32[]{:S(2)}) collective-permute-start(f32[1280,128]{1,0:T(8,128)S(1)} %get-tuple-element.84), channel_id=1, source_target_pairs={{0,1},{1,0},{2,3},{3,2},{4,5},{5,4},{6,7},{7,6},{8,9},{9,8},{10,11... | collective-permute-start | bytes 1966088 | tf_op jit(solution)/shard_map/ppermute | solution.py:606
  27.5 2.4 %deep.3.refs_4_ = f32[4,8,128,128]{3,2,1,0:T(8,128)} custom-call(f32[57,128,128]{2,1,0:T(8,128)S(1)} %get-tuple-element.59.x, f32[8,32,128]{2,1,0:T(8,128)S(1)} %collective-permute-done.la, f32[8,32,128]{2,1,0:T(8,128)S(1)} %collective-permute-done.1.lb, f32[48,128]{1,0:T(8,128)S(1)} %collective-permute-done.2.wa.oa, ...), custom_call_target="tpu_custom_call" | custom-call | bytes 9100000 | tf_op jit(solution)/shard_map/deep/pallas_call | solution.py:582
  29.9 0.1 add.37
  30.1 1.7 %collective-permute-start.7 = (f32[320,128]{1,0:T(8,128)S(1)}, f32[320,128]{1,0:T(8,128)S(1)}, u32[]{:S(2)}, u32[]{:S(2)}) collective-permute-start(f32[320,128]{1,0:T(8,128)S(1)} %get-tuple-element.104), channel_id=1, source_target_pairs={{0,6},{1,7},{2,4},{3,5},{4,2},{5,3},{6,0},{7,1},{8,14},{9,15},{10,... | collective-permute-start | bytes 491528 | tf_op jit(solution)/shard_map/ppermute | solution.py:606
  31.8 0.7 %collective-permute-start.8 = (f32[320,128]{1,0:T(8,128)S(1)}, f32[320,128]{1,0:T(8,128)S(1)}, u32[]{:S(2)}, u32[]{:S(2)}) collective-permute-start(f32[320,128]{1,0:T(8,128)S(1)} %get-tuple-element.103), channel_id=1, source_target_pairs={{0,4},{1,5},{2,6},{3,7},{4,0},{5,1},{6,2},{7,3},{8,12},{9,13},{10,... | collective-permute-start | bytes 491528 | tf_op jit(solution)/shard_map/ppermute | solution.py:606
  32.5 1.2 %collective-permute-start.9 = (f32[320,128]{1,0:T(8,128)S(1)}, f32[320,128]{1,0:T(8,128)S(1)}, u32[]{:S(2)}, u32[]{:S(2)}) collective-permute-start(f32[320,128]{1,0:T(8,128)S(1)} %get-tuple-element.102), channel_id=1, source_target_pairs={{0,2},{1,3},{2,0},{3,1},{4,6},{5,7},{6,4},{7,5},{8,10},{9,11},{10,... | collective-permute-start | bytes 491528 | tf_op jit(solution)/shard_map/ppermute | solution.py:606
  33.6 6.5 %deep.4.refs_4_ = f32[4,8,128,128]{3,2,1,0:T(8,128)} custom-call(f32[57,128,128]{2,1,0:T(8,128)S(1)} %get-tuple-element.59.x, f32[8,32,128]{2,1,0:T(8,128)S(1)} %collective-permute-done.la, f32[8,32,128]{2,1,0:T(8,128)S(1)} %collective-permute-done.1.lb, f32[48,128]{1,0:T(8,128)S(1)} %collective-permute-done.2.wa.oa, ...), custom_call_target="tpu_custom_call", output_to_operand_aliasing={{}: (11, {})} | custom-call | bytes 18200000 | tf_op jit(solution)/shard_map/deep/pallas_call | solution.py:582
  40.2 0.5 collective-permute-done.8
  40.7 2.7 %collective-permute-start.10 = (f32[80,128]{1,0:T(8,128)S(1)}, f32[80,128]{1,0:T(8,128)S(1)}, u32[]{:S(2)}, u32[]{:S(2)}) collective-permute-start(f32[80,128]{1,0:T(8,128)S(1)} %get-tuple-element.107), channel_id=1, source_target_pairs={{0,24},{1,25},{2,26},{3,27},{4,28},{5,29},{6,30},{7,31},{8,16},{9,... | collective-permute-start | bytes 122888 | tf_op jit(solution)/shard_map/ppermute | solution.py:606
  43.4 1.7 %collective-permute-start.12 = (f32[80,128]{1,0:T(8,128)S(1)}, f32[80,128]{1,0:T(8,128)S(1)}, u32[]{:S(2)}, u32[]{:S(2)}) collective-permute-start(f32[80,128]{1,0:T(8,128)S(1)} %get-tuple-element.105), channel_id=1, source_target_pairs={{0,8},{1,9},{2,10},{3,11},{4,12},{5,13},{6,14},{7,15},{8,0},{9,1},... | collective-permute-start | bytes 122888 | tf_op jit(solution)/shard_map/ppermute | solution.py:606
  45.2 3.8 %deep.5 = f32[4,8,128,128]{3,2,1,0:T(8,128)} custom-call(f32[57,128,128]{2,1,0:T(8,128)S(1)} %get-tuple-element.59.x, f32[8,32,128]{2,1,0:T(8,128)S(1)} %collective-permute-done.la, f32[8,32,128]{2,1,0:T(8,128)S(1)} %collective-permute-done.1.lb, f32[48,128]{1,0:T(8,128)S(1)} %collective-permute-done.2.wa.oa, ...), custom_call_target="tpu_custom_call", output_to_operand_aliasing={{}: (11, {})} | custom-call | bytes 9100000 | tf_op jit(solution)/shard_map/deep/pallas_call | solution.py:582
  48.9 0.6 %add_add_fusion.1 = f32[80,128]{1,0:T(8,128)} fusion(f32[80,128]{1,0:T(8,128)S(1)} %collective-permute-done.12, f32[80,128]{1,0:T(8,128)S(1)} %collective-permute-done.11, f32[80,128]{1,0:T(8,128)S(1)} %collective-permute-done.10, f32[320,128]{1,0:T(8,128)S(1)} %add_add_fusion), kind=kLoop, calls=%fused_computation.1 | loop fusion | flops 30720 | bytes 204800 | tf_op jit(solution)/shard_map/add | solution.py:665
  (18 shorter events, 0.1 us)
Async XLA Ops:
  0.6 2.3 %copy-start = (s32[128,1,4]{0,2,1:T(4,128)S(1)}, s32[128,1,4]{0,2,1:T(4,128)}, u32[]{:S(2)}) copy-start(s32[128,1,4]{0,2,1:T(4,128)} %param.11) | copy-start | bytes 6148
  1.8 5.9 %collective-permute-start = (f32[8,32,128]{2,1,0:T(8,128)S(1)}, f32[8,32,128]{2,1,0:T(8,128)S(1)}, u32[]{:S(2)}, u32[]{:S(2)}) collective-permute-start(f32[8,32,128]{2,1,0:T(8,128)S(1)} %get-tuple-element.52), channel_id=1, source_target_pairs={{0,1},{2,3},{1,0},{3,2},{4,5},{6,7},{5,4},{7,6},{8,9},{10,11},{9,8... | collective-permute-start | bytes 393224 | tf_op jit(solution)/shard_map/ppermute | solution.py:601
  2.3 5.3 %collective-permute-start.1 = (f32[8,32,128]{2,1,0:T(8,128)S(1)}, f32[8,32,128]{2,1,0:T(8,128)S(1)}, u32[]{:S(2)}, u32[]{:S(2)}) collective-permute-start(f32[8,32,128]{2,1,0:T(8,128)S(1)} %get-tuple-element.53), channel_id=1, source_target_pairs={{1,2},{2,1},{5,6},{6,5},{9,10},{10,9},{13,14},{14,13},{17,18},{18,... | collective-permute-start | bytes 393224 | tf_op jit(solution)/shard_map/ppermute | solution.py:600
  7.9 10.6 %collective-permute-start.2 = (f32[48,128]{1,0:T(8,128)S(1)}, f32[48,128]{1,0:T(8,128)S(1)}, u32[]{:S(2)}, u32[]{:S(2)}) collective-permute-start(f32[48,128]{1,0:T(8,128)S(1)} %get-tuple-element.60), channel_id=1, source_target_pairs={{0,4},{8,12},{16,20},{24,28},{4,0},{12,8},{20,16},{28,24},{1,5},{9... | collective-permute-start | bytes 73736 | tf_op jit(solution)/shard_map/ppermute | solution.py:601
  10.5 8.0 %collective-permute-start.3 = (f32[48,128]{1,0:T(8,128)S(1)}, f32[48,128]{1,0:T(8,128)S(1)}, u32[]{:S(2)}, u32[]{:S(2)}) collective-permute-start(f32[48,128]{1,0:T(8,128)S(1)} %get-tuple-element.61), channel_id=1, source_target_pairs={{4,8},{12,16},{20,24},{28,0},{8,4},{16,12},{24,20},{0,28},{5,9},{1... | collective-permute-start | bytes 73736 | tf_op jit(solution)/shard_map/ppermute | solution.py:600
  17.3 7.9 %collective-permute-start.5 = (f32[256,128]{1,0:T(8,128)S(1)}, f32[256,128]{1,0:T(8,128)S(1)}, u32[]{:S(2)}, u32[]{:S(2)}) collective-permute-start(f32[256,128]{1,0:T(8,128)S(1)} %get-tuple-element.71), channel_id=1, source_target_pairs={{4,8},{12,16},{20,24},{28,0},{8,4},{16,12},{24,20},{0,28},{5,9},{1... | collective-permute-start | bytes 393224 | tf_op jit(solution)/shard_map/ppermute | solution.py:600
  18.5 8.1 %collective-permute-start.4 = (f32[256,128]{1,0:T(8,128)S(1)}, f32[256,128]{1,0:T(8,128)S(1)}, u32[]{:S(2)}, u32[]{:S(2)}) collective-permute-start(f32[256,128]{1,0:T(8,128)S(1)} %get-tuple-element.70), channel_id=1, source_target_pairs={{0,4},{8,12},{16,20},{24,28},{4,0},{12,8},{20,16},{28,24},{1,5},{9... | collective-permute-start | bytes 393224 | tf_op jit(solution)/shard_map/ppermute | solution.py:601
  26.7 3.3 %collective-permute-start.6 = (f32[1280,128]{1,0:T(8,128)S(1)}, f32[1280,128]{1,0:T(8,128)S(1)}, u32[]{:S(2)}, u32[]{:S(2)}) collective-permute-start(f32[1280,128]{1,0:T(8,128)S(1)} %get-tuple-element.84), channel_id=1, source_target_pairs={{0,1},{1,0},{2,3},{3,2},{4,5},{5,4},{6,7},{7,6},{8,9},{9,8},{10,11... | collective-permute-start | bytes 1966088 | tf_op jit(solution)/shard_map/ppermute | solution.py:606
  30.1 10.1 %collective-permute-start.7 = (f32[320,128]{1,0:T(8,128)S(1)}, f32[320,128]{1,0:T(8,128)S(1)}, u32[]{:S(2)}, u32[]{:S(2)}) collective-permute-start(f32[320,128]{1,0:T(8,128)S(1)} %get-tuple-element.104), channel_id=1, source_target_pairs={{0,6},{1,7},{2,4},{3,5},{4,2},{5,3},{6,0},{7,1},{8,14},{9,15},{10,... | collective-permute-start | bytes 491528 | tf_op jit(solution)/shard_map/ppermute | solution.py:606
  31.8 8.9 %collective-permute-start.8 = (f32[320,128]{1,0:T(8,128)S(1)}, f32[320,128]{1,0:T(8,128)S(1)}, u32[]{:S(2)}, u32[]{:S(2)}) collective-permute-start(f32[320,128]{1,0:T(8,128)S(1)} %get-tuple-element.103), channel_id=1, source_target_pairs={{0,4},{1,5},{2,6},{3,7},{4,0},{5,1},{6,2},{7,3},{8,12},{9,13},{10,... | collective-permute-start | bytes 491528 | tf_op jit(solution)/shard_map/ppermute | solution.py:606
  32.5 8.2 %collective-permute-start.9 = (f32[320,128]{1,0:T(8,128)S(1)}, f32[320,128]{1,0:T(8,128)S(1)}, u32[]{:S(2)}, u32[]{:S(2)}) collective-permute-start(f32[320,128]{1,0:T(8,128)S(1)} %get-tuple-element.102), channel_id=1, source_target_pairs={{0,2},{1,3},{2,0},{3,1},{4,6},{5,7},{6,4},{7,5},{8,10},{9,11},{10,... | collective-permute-start | bytes 491528 | tf_op jit(solution)/shard_map/ppermute | solution.py:606
  40.7 8.2 %collective-permute-start.10 = (f32[80,128]{1,0:T(8,128)S(1)}, f32[80,128]{1,0:T(8,128)S(1)}, u32[]{:S(2)}, u32[]{:S(2)}) collective-permute-start(f32[80,128]{1,0:T(8,128)S(1)} %get-tuple-element.107), channel_id=1, source_target_pairs={{0,24},{1,25},{2,26},{3,27},{4,28},{5,29},{6,30},{7,31},{8,16},{9,... | collective-permute-start | bytes 122888 | tf_op jit(solution)/shard_map/ppermute | solution.py:606
  43.4 5.5 %collective-permute-start.11 = (f32[80,128]{1,0:T(8,128)S(1)}, f32[80,128]{1,0:T(8,128)S(1)}, u32[]{:S(2)}, u32[]{:S(2)}) collective-permute-start(f32[80,128]{1,0:T(8,128)S(1)} %get-tuple-element.106), channel_id=1, source_target_pairs={{0,16},{1,17},{2,18},{3,19},{4,20},{5,21},{6,22},{7,23},{8,24},{9,... | collective-permute-start | bytes 122888 | tf_op jit(solution)/shard_map/ppermute | solution.py:606
  43.4 5.5 %collective-permute-start.12 = (f32[80,128]{1,0:T(8,128)S(1)}, f32[80,128]{1,0:T(8,128)S(1)}, u32[]{:S(2)}, u32[]{:S(2)}) collective-permute-start(f32[80,128]{1,0:T(8,128)S(1)} %get-tuple-element.105), channel_id=1, source_target_pairs={{0,8},{1,9},{2,10},{3,11},{4,12},{5,13},{6,14},{7,15},{8,0},{9,1},... | collective-permute-start | bytes 122888 | tf_op jit(solution)/shard_map/ppermute | solution.py:606
